TPU v7x, 512 devices: a whole 4x4x16 slice. The times are simulated.
512 devices in a mesh: seq: 64 (over z, x), tp: 8 (over y, core).
Axes of the slice: x: 4, y: 4, z: 16, core: 2. Of those that a mesh axis runs over, the one named last changes fastest.
Arguments:
- queries: bfloat16 [32768, 4096], P('seq', 'tp'), may hold values from -6 to 6
- keys: bfloat16 [32768, 4096], P('seq', 'tp'), may hold values from -6 to 6
- values: bfloat16 [32768, 4096], P('seq', 'tp'), may hold values from -6 to 6
- norm_gain: float32 [4096], P('tp'), may hold values from 0.1 to 1.9
- out_weight: bfloat16 [4096, 4096], P('tp', 'seq'), may hold values from -0.25 to 0.25
Outputs:
- mixed: bfloat16 [32768, 4096], P('seq', 'tp')
All inputs are finite; a program needn't handle non-finite values.
Results may differ from a plain program's by a relative error of at most 0.017.
Values may be sent and summed in bfloat16 or wider, within the bound.
No kernel may reach another device: no remote copies, remote signals or barrier semaphores. Data moves between devices by JAX's collectives and lax.ppermute only.
A program may use at most 64 MiB of HBM per device.

v0:
```python
import jax
import jax.numpy as jnp
from jax import lax
from jax.sharding import PartitionSpec as P

HEAD = 128
BLOCK = 512


def entering(part, axis, combine, identity):
    place = lax.axis_index(axis)
    gathered = lax.all_gather(part, axis)
    state = jnp.zeros_like(part) + jnp.asarray(identity, part.dtype)

    def one(step, state):
        return combine(state, lax.dynamic_index_in_dim(gathered, step, 0, False))

    return lax.fori_loop(0, place, one, state)


def add_states(earlier, later):
    return earlier + later


def shards(queries, keys, values, norm_gain, out_weight):
    rows, width = queries.shape
    heads = width // HEAD
    count = rows // BLOCK
    query_b = queries.reshape(count, BLOCK, heads, HEAD)
    key_b = keys.reshape(count, BLOCK, heads, HEAD)
    value_b = values.reshape(count, BLOCK, heads, HEAD)
    block_states = jnp.einsum("bthd,bthe->bhde", key_b, value_b, preferred_element_type=jnp.float32)
    own_total = jnp.sum(block_states, axis=0)
    prefix = entering(own_total, "seq", add_states, jnp.zeros_like(own_total))
    within = jnp.cumsum(block_states, axis=0) - block_states
    states = prefix[None] + within
    carried = jnp.einsum(
        "bthd,bhde->bthe", query_b.astype(jnp.float32), states, precision=lax.Precision.HIGHEST
    )
    scores = jnp.einsum("bthd,bshd->bhts", query_b, key_b, preferred_element_type=jnp.float32)
    causal = jnp.arange(BLOCK)[:, None] >= jnp.arange(BLOCK)[None, :]
    weights = jnp.where(causal[None, None], scores, 0.0).astype(jnp.bfloat16)
    local = jnp.einsum("bhts,bshe->bthe", weights, value_b, preferred_element_type=jnp.float32)
    attended = carried + local
    meansq = jnp.mean(attended * attended, axis=-1, keepdims=True)
    normed = attended * lax.rsqrt(meansq + 1e-06) * norm_gain.reshape(heads, HEAD)
    hidden = normed.reshape(rows, width).astype(jnp.bfloat16)
    partials = jnp.dot(
        hidden,
        lax.all_gather(out_weight, "seq", axis=1, tiled=True),
        preferred_element_type=jnp.float32,
    )
    summed = lax.psum_scatter(partials.astype(jnp.bfloat16), "tp", scatter_dimension=1, tiled=True)
    return summed


def solution(mesh):
    return jax.shard_map(
        shards,
        mesh=mesh,
        in_specs=(P("seq", "tp"), P("seq", "tp"), P("seq", "tp"), P("tp"), P("tp", "seq")),
        out_specs=P("seq", "tp"),
        check_vma=False,
    )
```

profile of v0, /device:TPU:24, one launch (start us, length us, event | category | flops | bytes accessed | tf_op | source)
XLA Modules:
  0.0 403.8 jit_solution(13292133541478626910)
XLA Ops:
  6.5 0.0 copy-start
  6.5 0.0 all-gather.6.cloned.1.call-start
  6.5 1.3 copy.17
  7.9 1.3 copy.18
  9.1 1.0 fusion.16
  10.1 0.0 copy-start.1
  10.1 0.0 all-gather.6.cloned.1.call-update
  10.1 0.0 all-gather.4.cloned.1.call-start
  10.2 0.7 all-gather.4.cloned.1.call-update
  10.9 0.0 reduce-scatter.2.cloned.1.call-start
  10.9 0.1 iota_compare_fusion
  11.0 197.1 %all-gather.6.cloned.1.call-done = f32[256,128,128]{2,1,0:T(8,128)} async-done(((f32[4,128,128]{2,1,0:T(8,128)}), f32[256,128,128]{2,1,0:T(8,128)}) %all-gather.6.cloned.1.call-update) | async-done | bytes 16777232 | tf_op jit(solution)/shard_map/all_gather | solution.py:12
  208.2 0.0 copy-start.2
  208.2 0.0 copy-done
  208.2 0.0 copy-done.1
  208.2 1.6 fusion.6
  209.8 2.6 multiply_reduce_fusion
  212.4 0.0 copy-done.2
  212.4 0.2 multiply_convert_fusion
  212.6 141.5 %all-gather.4.cloned.1.call-done = bf16[512,4096]{0,1:T(8,128)(2,1)} async-done(((bf16[512,64]{0,1:T(8,128)(2,1)}), bf16[512,4096]{0,1:T(8,128)(2,1)}) %all-gather.4.cloned.1.call-update) | async-done | bytes 4194320 | tf_op jit(solution)/shard_map/all_gather | solution.py:50
  354.1 6.5 %convolution_convert_fusion = bf16[512,4096]{1,0:T(8,128)(2,1)} fusion(bf16[512,512]{0,1:T(8,128)(2,1)S(1)} %bitcast.45, bf16[512,4096]{0,1:T(8,128)(2,1)} %all-gather.4.cloned.1.call-done), kind=kOutput, calls=%fused_computation.1 | convolution fusion | flops 2149580800 | bytes 8912896 | tf_op jit(solution)/shard_map/dot_general | solution.py:48
  360.6 0.0 reduce-scatter.2.cloned.1.call-update
  360.6 36.7 %reduce-scatter.2.cloned.1.call-done = bf16[512,512]{1,0:T(8,128)(2,1)} async-done(((bf16[512,4096]{1,0:T(8,128)(2,1)}), bf16[512,512]{1,0:T(8,128)(2,1)}) %reduce-scatter.2.cloned.1.call-update) | async-done | bytes 524304 | tf_op jit(solution)/shard_map/reduce_scatter | solution.py:53
  (3 shorter events, 0.0 us)
Async XLA Ops:
  6.5 201.7 %copy-start = (bf16[512,512]{1,0:T(8,128)(2,1)S(1)}, bf16[512,512]{1,0:T(8,128)(2,1)}, u32[]{:S(2)}) copy-start(bf16[512,512]{1,0:T(8,128)(2,1)} %param.7) | copy-start | bytes 1572868
  6.5 201.6 %all-gather.6.cloned.1.call-start = ((), (), s32[]{:S(2)}) async-start(), calls=%async_computation.3 | async-start | bytes 17039360 | tf_op jit(solution)/shard_map/all_gather | solution.py:12
  10.1 198.1 %copy-start.1 = (f32[4,128,128]{2,1,0:T(8,128)S(1)}, f32[4,128,128]{2,1,0:T(8,128)}, u32[]{:S(2)}) copy-start(f32[4,128,128]{2,1,0:T(8,128)} %fusion.16) | copy-start | bytes 786436
  10.1 343.9 %all-gather.4.cloned.1.call-start = ((), (), s32[]{:S(2)}) async-start(), calls=%async_computation.1 | async-start | bytes 4259840 | tf_op jit(solution)/shard_map/all_gather | solution.py:50
  10.9 386.4 %reduce-scatter.2.cloned.1.call-start = ((), (), s32[]{:S(2)}) async-start(), calls=%async_computation.2 | async-start | bytes 4718592 | tf_op jit(solution)/shard_map/reduce_scatter | solution.py:53
  208.2 4.2 %copy-start.2 = (f32[512]{0:T(512)S(1)}, f32[512]{0:T(512)}, u32[]{:S(2)}) copy-start(f32[512]{0:T(512)} %param.10) | copy-start | bytes 6148
Sparse Core Ops, SparseCore 0:
  10.3 197.7 all-gather.5
  211.1 142.9 all-gather.3
  360.8 36.5 reduce-scatter.1
where the time goes:
time: 410 us; the launch traced here: 404 us
  waiting for transfers between devices  376 us (92%)
  between operations  13.2 us (3%)
  matrix products  11.7 us (3%)
    all_gather x1, waiting for transfers between devices, entering(): gathered = lax.all_gather(part, axis)  197 us
    all_gather x1, waiting for transfers between devices, shards(): lax.all_gather(out_weight, 'seq', axis=1, tiled=True)  142 us
    reduce_scatter x1, waiting for transfers between devices, shards(): lax.psum_scatter(partials.astype(jnp.bfloat16), 'tp', scatter_dimension=1...  36.7 us
  transfers between devices with their start and end apart: 3, of which 3 were waited for; matrix products, arithmetic and copies ran while one was open for 1% of the time, Pallas kernels for 0%

commit v1 on v0

v1 whole, which is shorter than its diff:
```python
import functools

import jax
import jax.numpy as jnp
from jax import lax
from jax.experimental import pallas as pl
from jax.experimental.pallas import tpu as pltpu
from jax.sharding import Mesh, PartitionSpec as P

HEAD = 128
TILE = 256
NT = (((1,), (1,)), ((), ()))
TN = (((0,), (0,)), ((), ()))


def params():
    return pltpu.CompilerParams(vmem_limit_bytes=40 * 1024 * 1024)


def vmem(count):
    return [pl.BlockSpec(memory_space=pltpu.VMEM)] * count


def block_state_kernel(k_ref, v_ref, s_ref):
    heads = k_ref.shape[1] // HEAD
    for h in range(heads):
        cols = slice(h * HEAD, (h + 1) * HEAD)
        s_ref[cols, :] = lax.dot_general(k_ref[:, cols], v_ref[:, cols], TN, preferred_element_type=jnp.float32)


def block_state(keys, values):
    width = keys.shape[1]
    return pl.pallas_call(
        block_state_kernel,
        out_shape=jax.ShapeDtypeStruct((width, HEAD), jnp.float32),
        in_specs=vmem(2),
        out_specs=pl.BlockSpec(memory_space=pltpu.VMEM),
        compiler_params=params(),
    )(keys, values)


def prefix_kernel(blocks, s_ref, p_ref):
    rows = s_ref.shape[0] // blocks
    total = jnp.zeros((rows, HEAD), jnp.float32)
    for b in range(blocks):
        at = slice(b * rows, (b + 1) * rows)
        p_ref[at, :] = total
        total = total + s_ref[at, :]


def prefix(pieces, blocks):
    return pl.pallas_call(
        functools.partial(prefix_kernel, blocks),
        out_shape=jax.ShapeDtypeStruct(pieces.shape, jnp.float32),
        in_specs=vmem(1),
        out_specs=pl.BlockSpec(memory_space=pltpu.VMEM),
        compiler_params=params(),
    )(pieces)


def attend_kernel(q_ref, k_ref, v_ref, s_ref, g_ref, o_ref):
    rows, width = q_ref.shape
    for h in range(width // HEAD):
        cols = slice(h * HEAD, (h + 1) * HEAD)
        state = s_ref[cols, :]
        high = state.astype(jnp.bfloat16)
        low = (state - high.astype(jnp.float32)).astype(jnp.bfloat16)
        both = jnp.concatenate([high, low], axis=0)
        gain = g_ref[:, cols]
        for first in range(0, rows, TILE):
            own = slice(first, first + TILE)
            seen = first + TILE
            query = q_ref[own, cols]
            carried = jnp.dot(jnp.concatenate([query, query], axis=1), both, preferred_element_type=jnp.float32)
            scores = lax.dot_general(query, k_ref[:seen, cols], NT, preferred_element_type=jnp.float32)
            row = lax.broadcasted_iota(jnp.int32, scores.shape, 0) + first
            col = lax.broadcasted_iota(jnp.int32, scores.shape, 1)
            weights = jnp.where(row >= col, scores, 0.0).astype(jnp.bfloat16)
            local = jnp.dot(weights, v_ref[:seen, cols], preferred_element_type=jnp.float32)
            attended = carried + local
            meansq = jnp.mean(attended * attended, axis=-1, keepdims=True)
            o_ref[own, cols] = (attended * lax.rsqrt(meansq + 1e-06) * gain).astype(jnp.bfloat16)


def attend(queries, keys, values, states, gain):
    return pl.pallas_call(
        attend_kernel,
        out_shape=jax.ShapeDtypeStruct(queries.shape, jnp.bfloat16),
        in_specs=vmem(5),
        out_specs=pl.BlockSpec(memory_space=pltpu.VMEM),
        compiler_params=params(),
    )(queries, keys, values, states, gain)


def shards(queries, keys, values, norm_gain, out_weight):
    blocks = lax.axis_size("z") * lax.axis_size("x")
    near = lax.all_gather(out_weight.T, "x", axis=0, tiled=True)
    near, keys, values = lax.optimization_barrier((near, keys, values))
    weight = lax.all_gather(near, "z", axis=0, tiled=True)
    state = block_state(keys, values)
    pieces = lax.all_to_all(state, ("z", "x"), 0, 0, tiled=True)
    states = lax.all_to_all(prefix(pieces, blocks), ("z", "x"), 0, 0, tiled=True)
    hidden = attend(queries, keys, values, states, norm_gain[None, :])
    partials = lax.dot_general(hidden, weight, NT, preferred_element_type=jnp.float32)
    return lax.psum_scatter(partials.astype(jnp.bfloat16), ("y", "c"), scatter_dimension=1, tiled=True)


def solution(mesh):
    axes = ("z", "x", "y", "c")
    grid = Mesh(mesh.devices.reshape(mesh.devices.shape[0] // 4, 4, 4, 2), axes)
    seq, tp = axes[:2], axes[2:]
    return jax.shard_map(
        shards,
        mesh=grid,
        in_specs=(P(seq, tp), P(seq, tp), P(seq, tp), P(tp), P(tp, seq)),
        out_specs=P(seq, tp),
        check_vma=False,
    )
```

time: 410 us -> 175 us (0.43)
  the two profiles are of different devices: /device:TPU:24 before, /device:TPU:2 now
where the time goes in v1:
time: 175 us
  blocking collectives  81.2 us (46%)
  waiting for transfers between devices  66.7 us (38%)
  between operations  13.4 us (8%)
  matrix products  6.54 us (4%)
  local copies, waits for them, and re-layouts  4.85 us (3%)
  Pallas kernels  2.19 us (1%)
    reduce_scatter x1, waiting for transfers between devices, shards(): lax.psum_scatter(partials.astype(jnp.bfloat16), ('y', 'c'), scatter_dimen...  42.3 us
    all_to_all x1, blocking collectives, shards(): pieces = lax.all_to_all(state, ('z', 'x'), 0, 0, tiled=True)  35.5 us
    all_to_all x1, blocking collectives, shards(): lax.all_to_all(prefix(pieces, blocks), ('z', 'x'), 0, 0, tiled=True)  28.2 us
    all_gather x1, waiting for transfers between devices, shards(): weight = lax.all_gather(near, 'z', axis=0, tiled=True)  24.3 us
    all_gather x1, blocking collectives, shards(): near = lax.all_gather(out_weight.T, 'x', axis=0, tiled=True)  17.5 us
    dot_general x1, matrix products, shards(): lax.dot_general(hidden, weight, NT, preferred_element_type=jnp.float32)  6.54 us
    unnamed x10, local copies, waits for them, and re-layouts  4.85 us
  transfers between devices with their start and end apart: 2, of which 2 were waited for; matrix products, arithmetic and copies ran while one was open for 0% of the time, Pallas kernels for 1%

profile of v1, /device:TPU:2, one launch (start us, length us, event | category | flops | bytes accessed | tf_op | source)
XLA Modules:
  0.0 174.9 jit_solution(2358142792617885693)
XLA Ops:
  6.5 0.0 all-gather.2.cloned.1.call-start
  6.5 17.5 %all_gather.6 = bf16[256,512]{1,0:T(8,128)(2,1)} all-gather(bf16[64,512]{1,0:T(8,128)(2,1)} %bitcast.13), channel_id=1, replica_groups=mesh['z'=16,'x'=4,'y'=4,'c'=2] {'x'}, dimensions={0}, use_global_device_ids=true | all-gather | bytes 327680 | tf_op jit(solution)/shard_map/all_gather | solution.py:97
  24.1 0.0 all-gather.2.cloned.1.call-update
  24.1 0.0 reduce-scatter.2.cloned.1.call-start
  24.1 0.0 copy-start
  24.1 1.0 copy-done
  25.2 0.0 copy-start.2
  25.2 1.0 copy-done.2
  26.2 0.3 shard_map.55
  26.6 35.5 %all_to_all.22 = f32[64,8,128]{2,1,0:T(8,128)S(1)} all-to-all(f32[64,8,128]{2,1,0:T(8,128)S(1)} %bitcast.8), channel_id=1, replica_groups=mesh['z'=16,'x'=4,'y'=4,'c'=2] {'z','x'}, dimensions={0} | all-to-all | bytes 524288 | tf_op jit(solution)/shard_map/all_to_all | solution.py:101
  62.1 0.1 shard_map.56
  62.1 28.2 %all_to_all.23 = f32[64,8,128]{2,1,0:T(8,128)S(1)} all-to-all(f32[64,8,128]{2,1,0:T(8,128)S(1)} %bitcast.10), channel_id=1, replica_groups=mesh['z'=16,'x'=4,'y'=4,'c'=2] {'z','x'}, dimensions={0} | all-to-all | bytes 524288 | tf_op jit(solution)/shard_map/all_to_all | solution.py:102
  90.4 0.0 copy-start.1
  90.4 1.0 copy-done.1
  91.4 0.0 copy-start.3
  91.4 1.0 copy-done.3
  92.5 0.0 copy-start.4
  92.5 0.7 copy-done.4
  93.1 1.8 %shard_map.57 = bf16[512,512]{1,0:T(8,128)(2,1)S(1)} custom-call(bf16[512,512]{1,0:T(8,128)(2,1)S(1)} %copy-done.3, bf16[512,512]{1,0:T(8,128)(2,1)S(1)} %copy-done.1, bf16[512,512]{1,0:T(8,128)(2,1)S(1)} %copy-done.2, f32[512,128]{1,0:T(8,128)S(1)} %bitcast.11, f32[1,512]{1,0:T(1,128)S(1)} %bitcast.12), custom_call_target="tpu_custom_call" | custom-call | tf_op jit(solution)/shard_map/pallas_call | solution.py:86
  94.9 24.3 %all-gather.2.cloned.1.call-done = bf16[4096,512]{1,0:T(8,128)(2,1)} async-done(((bf16[256,512]{1,0:T(8,128)(2,1)}), bf16[4096,512]{1,0:T(8,128)(2,1)}) %all-gather.2.cloned.1.call-update) | async-done | bytes 4194320 | tf_op jit(solution)/shard_map/all_gather | solution.py:99
  119.3 6.5 %convolution_convert_fusion = bf16[512,4096]{1,0:T(8,128)(2,1)} fusion(bf16[512,512]{1,0:T(8,128)(2,1)S(1)} %shard_map.57, bf16[4096,512]{1,0:T(8,128)(2,1)} %all-gather.2.cloned.1.call-done), kind=kOutput, calls=%fused_computation | convolution fusion | flops 2149580800 | bytes 8912896 | tf_op jit(solution)/shard_map/dot_general | solution.py:104
  125.8 0.0 reduce-scatter.2.cloned.1.call-update
  125.8 42.3 %reduce-scatter.2.cloned.1.call-done = bf16[512,512]{1,0:T(8,128)(2,1)} async-done(((bf16[512,4096]{1,0:T(8,128)(2,1)}), bf16[512,512]{1,0:T(8,128)(2,1)}) %reduce-scatter.2.cloned.1.call-update) | async-done | bytes 524304 | tf_op jit(solution)/shard_map/reduce_scatter | solution.py:105
Async XLA Ops:
  6.5 112.7 %all-gather.2.cloned.1.call-start = ((), (), s32[]{:S(2)}) async-start(), calls=%async_computation.3 | async-start | bytes 4456448 | tf_op jit(solution)/shard_map/all_gather | solution.py:99
  24.1 144.0 %reduce-scatter.2.cloned.1.call-start = ((), (), s32[]{:S(2)}) async-start(), calls=%async_computation.4 | async-start | bytes 4718592 | tf_op jit(solution)/shard_map/reduce_scatter | solution.py:105
  24.1 1.0 copy-start
  25.2 1.0 copy-start.2
  90.4 1.0 copy-start.1
  91.4 1.1 copy-start.3
  92.5 0.7 copy-start.4
Sparse Core Ops, SparseCore 0:
  24.2 95.0 all-gather.1
  126.0 42.1 reduce-scatter.1

commit v2 on v1

v2 whole, which is shorter than its diff:
```python
import functools

import jax
import jax.numpy as jnp
from jax import lax
from jax.experimental import pallas as pl
from jax.experimental.pallas import tpu as pltpu
from jax.sharding import Mesh, PartitionSpec as P

HEAD = 128
TILE = 256
GROUP = ("zl", "x")
NT = (((1,), (1,)), ((), ()))
TN = (((0,), (0,)), ((), ()))


def params(mib):
    return pltpu.CompilerParams(vmem_limit_bytes=mib * 1024 * 1024)


def in_vmem():
    return pl.BlockSpec(memory_space=pltpu.VMEM)


def by_head(rows):
    return pl.BlockSpec((rows, HEAD), lambda h: (0, h))


def block_state_kernel(k_ref, v_ref, s_ref):
    s_ref[...] = lax.dot_general(k_ref[...], v_ref[...], TN, preferred_element_type=jnp.float32)


def block_state(keys, values):
    rows, width = keys.shape
    return pl.pallas_call(
        block_state_kernel,
        grid=(width // HEAD,),
        out_shape=jax.ShapeDtypeStruct((width, HEAD), jnp.float32),
        in_specs=[by_head(rows)] * 2,
        out_specs=pl.BlockSpec((HEAD, HEAD), lambda h: (h, 0)),
        compiler_params=params(63),
    )(keys, values)


def total_kernel(s_ref, t_ref):
    rows = t_ref.shape[0]
    total = s_ref[:rows, :]
    for b in range(1, s_ref.shape[0] // rows):
        total = total + s_ref[b * rows:(b + 1) * rows, :]
    t_ref[...] = total


def group_total(pieces, blocks):
    return pl.pallas_call(
        total_kernel,
        out_shape=jax.ShapeDtypeStruct((pieces.shape[0] // blocks, HEAD), jnp.float32),
        in_specs=[in_vmem()],
        out_specs=in_vmem(),
        compiler_params=params(32),
    )(pieces)


def prefix_kernel(group_ref, s_ref, t_ref, p_ref, *, groups):
    rows = t_ref.shape[0] // groups
    total = jnp.zeros((rows, HEAD), jnp.float32)
    for g in range(groups - 1):
        total = total + jnp.where(g < group_ref[0], t_ref[g * rows:(g + 1) * rows, :], 0.0)
    for b in range(s_ref.shape[0] // rows):
        at = slice(b * rows, (b + 1) * rows)
        p_ref[at, :] = total
        total = total + s_ref[at, :]


def prefix(pieces, totals, group, groups):
    return pl.pallas_call(
        functools.partial(prefix_kernel, groups=groups),
        out_shape=jax.ShapeDtypeStruct(pieces.shape, jnp.float32),
        in_specs=[pl.BlockSpec(memory_space=pltpu.SMEM), in_vmem(), in_vmem()],
        out_specs=in_vmem(),
        compiler_params=params(32),
    )(group, pieces, totals)


def attend_kernel(q_ref, k_ref, v_ref, s_ref, g_ref, o_ref):
    rows = q_ref.shape[0]
    state = s_ref[...]
    high = state.astype(jnp.bfloat16)
    low = (state - high.astype(jnp.float32)).astype(jnp.bfloat16)
    both = jnp.concatenate([high, low], axis=0)
    for first in range(0, rows, TILE):
        own = slice(first, first + TILE)
        seen = first + TILE
        query = q_ref[own, :]
        carried = jnp.dot(jnp.concatenate([query, query], axis=1), both, preferred_element_type=jnp.float32)
        scores = lax.dot_general(query, k_ref[:seen, :], NT, preferred_element_type=jnp.float32)
        row = lax.broadcasted_iota(jnp.int32, scores.shape, 0) + first
        col = lax.broadcasted_iota(jnp.int32, scores.shape, 1)
        weights = jnp.where(row >= col, scores, 0.0).astype(jnp.bfloat16)
        local = jnp.dot(weights, v_ref[:seen, :], preferred_element_type=jnp.float32)
        attended = carried + local
        meansq = jnp.mean(attended * attended, axis=-1, keepdims=True)
        o_ref[own, :] = (attended * lax.rsqrt(meansq + 1e-06) * g_ref[...]).astype(jnp.bfloat16)


def attend(queries, keys, values, states, gain):
    rows, width = queries.shape
    return pl.pallas_call(
        attend_kernel,
        grid=(width // HEAD,),
        out_shape=jax.ShapeDtypeStruct(queries.shape, jnp.bfloat16),
        in_specs=[by_head(rows)] * 3 + [pl.BlockSpec((HEAD, HEAD), lambda h: (h, 0)), by_head(1)],
        out_specs=by_head(rows),
        compiler_params=params(63),
    )(queries, keys, values, states, gain)


def project_kernel(order_ref, *refs):
    *hidden_refs, w_ref, o_ref, total = refs
    step = pl.program_id(0)
    for at, h_ref in enumerate(hidden_refs):
        @pl.when(step == at)
        def _():
            part = lax.dot_general(h_ref[...], w_ref[0], NT, preferred_element_type=jnp.float32)
            total[...] = part if at == 0 else total[...] + part

    @pl.when(step == len(hidden_refs) - 1)
    def _():
        o_ref[...] = total[...].astype(o_ref.dtype)


def project(order, hidden, weight):
    groups, columns, depth = weight.shape
    rows = hidden[0].shape[0]
    return pl.pallas_call(
        project_kernel,
        grid_spec=pltpu.PrefetchScalarGridSpec(
            num_scalar_prefetch=1,
            grid=(groups,),
            in_specs=[in_vmem()] * groups
            + [pl.BlockSpec((1, columns, depth), lambda g, order: (order[g], 0, 0))],
            out_specs=pl.BlockSpec((rows, columns), lambda g, order: (0, 0)),
            scratch_shapes=[pltpu.VMEM((rows, columns), jnp.float32)],
        ),
        out_shape=jax.ShapeDtypeStruct((rows, columns), jnp.bfloat16),
        compiler_params=params(47),
    )(order, *hidden, weight)


def shift(array, axis, by):
    size = lax.axis_size(axis)
    return lax.ppermute(array, axis, [(i, (i + by) % size) for i in range(size)])


def to_columns(shard):
    pairs = []
    for z in range(16):
        for t in range(8):
            pairs.append((z * 8 + t, (t * 2 + z % 2) * 8 + z // 2))
    return lax.ppermute(shard, ("zh", "zl", "y", "c"), pairs)


def shards(queries, keys, values, norm_gain, out_weight):
    groups = lax.axis_size("zh")
    blocks = lax.axis_size("zl") * lax.axis_size("x")
    tp = lax.axis_size("y") * lax.axis_size("c")
    near = lax.all_gather(to_columns(out_weight.T), "x", axis=0, tiled=True)
    near, keys, values = lax.optimization_barrier((near, keys, values))
    weight = lax.all_gather(near, ("zh", "zl"), axis=0, tiled=True).reshape(tp, -1, out_weight.shape[0])

    state = block_state(keys, values)
    pieces = lax.all_to_all(state, GROUP, 0, 0, tiled=True)
    totals = lax.all_gather(group_total(pieces, blocks), "zh", axis=0, tiled=True)
    group = lax.axis_index("zh").astype(jnp.int32)[None]
    states = lax.all_to_all(prefix(pieces, totals, group, groups), GROUP, 0, 0, tiled=True)
    hidden = attend(queries, keys, values, states, norm_gain[None, :])

    steps = (0, 1, -1, 2)
    held = [hidden] + [shift(hidden, "y", by) for by in steps[1:]]
    held = held + [shift(h, "c", 1) for h in held]
    row, core = lax.axis_index("y"), lax.axis_index("c")
    place = (row - jnp.array(steps, jnp.int32)) % lax.axis_size("y") * 2
    order = jnp.concatenate([place + core, place + 1 - core]).astype(jnp.int32)
    return project(order, held, weight)


def solution(mesh):
    axes = ("zh", "zl", "x", "y", "c")
    grid = Mesh(mesh.devices.reshape(4, 4, 4, 4, 2), axes)
    seq, tp = axes[:3], axes[3:]
    return jax.shard_map(
        shards,
        mesh=grid,
        in_specs=(P(seq, tp), P(seq, tp), P(seq, tp), P(tp), P(tp, seq)),
        out_specs=P(seq, tp),
        check_vma=False,
    )
```

time: 175 us -> 152 us (0.87)
  the two profiles are of different devices: /device:TPU:2 before, /device:TPU:9 now
where the time goes in v2:
time: 152 us; the launch traced here: 151 us
  blocking collectives  52.3 us (34%)
  starting transfers between devices  50.4 us (33%)
  Pallas kernels  16.9 us (11%)
  waiting for transfers between devices  14.7 us (10%)
  between operations  13.5 us (9%)
  local copies, waits for them, and re-layouts  2.88 us (2%)
    ppermute x7, starting transfers between devices, shift(): lax.ppermute(array, axis, [(i, (i + by) % size) for i in range(size)])  32.4 us
    all_gather x1, blocking collectives, shards(): lax.all_gather(group_total(pieces, blocks), 'zh', axis=0, tiled=True)  25.3 us
    all_to_all x1, blocking collectives, shards(): lax.all_to_all(prefix(pieces, totals, group, groups), GROUP, 0, 0, tiled=...  16.6 us
    ppermute x1, starting transfers between devices, to_columns(): return lax.ppermute(shard, ('zh', 'zl', 'y', 'c'), pairs)  12.1 us
    all_gather x1, blocking collectives, shards(): near = lax.all_gather(to_columns(out_weight.T), 'x', axis=0, tiled=True)  10.4 us
    all_to_all x1, waiting for transfers between devices, shards(): pieces = lax.all_to_all(state, GROUP, 0, 0, tiled=True)  8.83 us
    pallas_call x1, Pallas kernels, project(): pl.pallas_call(project_kernel, grid_spec=pltpu.PrefetchScalarGridSpec(num...  8.13 us
    all_to_all x1, starting transfers between devices, shards(): pieces = lax.all_to_all(state, GROUP, 0, 0, tiled=True)  5.82 us
  transfers between devices with their start and end apart: 10, of which 4 were waited for; matrix products, arithmetic and copies ran while one was open for 0% of the time, Pallas kernels for 6%

profile of v2, /device:TPU:9, one launch (start us, length us, event | category | flops | bytes accessed | tf_op | source)
XLA Modules:
  0.0 150.7 jit_solution(11257690090427919433)
XLA Ops:
  6.5 0.0 copy-start.3
  6.5 0.0 all-gather.2.cloned.1.call-start
  6.5 12.1 %collective-permute-start = (bf16[64,512]{1,0:T(8,128)(2,1)}, bf16[64,512]{1,0:T(8,128)(2,1)S(1)}, u32[]{:S(2)}, u32[]{:S(2)}) collective-permute-start(bf16[64,512]{1,0:T(8,128)(2,1)} %bitcast.15), channel_id=1, source_target_pairs={{0,0},{1,64},{2,128},{3,192},{4,256},{5,320},{6,384},{7,448},{32,3... | collective-permute-start | bytes 196616 | tf_op jit(solution)/shard_map/ppermute | solution.py:159
  18.6 3.6 %collective-permute-done = bf16[64,512]{1,0:T(8,128)(2,1)S(1)} collective-permute-done((bf16[64,512]{1,0:T(8,128)(2,1)}, bf16[64,512]{1,0:T(8,128)(2,1)S(1)}, u32[]{:S(2)}, u32[]{:S(2)}) %collective-permute-start) | collective-permute-done | bytes 65568 | tf_op jit(solution)/shard_map/ppermute | solution.py:159
  22.2 10.4 %all_gather.9 = bf16[256,512]{1,0:T(8,128)(2,1)} all-gather(bf16[64,512]{1,0:T(8,128)(2,1)S(1)} %collective-permute-done), channel_id=1, replica_groups=mesh['zh'=4,'zl'=4,'x'=4,'y'=4,'c'=2] {'x'}, dimensions={0}, use_global_device_ids=true | all-gather | bytes 327680 | tf_op jit(solution)/shard_map/all_gather | solution.py:166
  32.7 0.0 all-gather.2.cloned.1.call-update
  32.7 3.7 %shard_map.64 = f32[512,128]{1,0:T(8,128)} custom-call(bf16[512,512]{1,0:T(8,128)(2,1)} %k_ref.1, bf16[512,512]{1,0:T(8,128)(2,1)} %v_ref.1), custom_call_target="tpu_custom_call" | custom-call | tf_op jit(solution)/shard_map/pallas_call | solution.py:35
  36.4 5.8 %all-to-all-start = ((f32[16,32,128]{2,1,0:T(8,128)}), f32[16,32,128]{2,1,0:T(8,128)S(1)}, u32[]{:S(2)}, u32[]{:S(2)}) async-start(f32[16,32,128]{2,1,0:T(8,128)} %bitcast.12), calls=%async_computation | async-start | bytes 524288 | tf_op jit(solution)/shard_map/all_to_all | solution.py:171
  42.2 8.8 %all-to-all-done = f32[16,32,128]{2,1,0:T(8,128)S(1)} async-done(((f32[16,32,128]{2,1,0:T(8,128)}), f32[16,32,128]{2,1,0:T(8,128)S(1)}, u32[]{:S(2)}, u32[]{:S(2)}) %all-to-all-start) | async-done | bytes 262176 | tf_op jit(solution)/shard_map/all_to_all | solution.py:171
  51.1 25.3 %all_gather.10.t_ref = f32[128,128]{1,0:T(8,128)S(1)} all-gather(f32[32,128]{1,0:T(8,128)S(1)} %shard_map.65), channel_id=1, replica_groups=mesh['zh'=4,'zl'=4,'x'=4,'y'=4,'c'=2] {'zh'}, dimensions={0}, use_global_device_ids=true | all-gather | bytes 81920 | tf_op jit(solution)/shard_map/all_gather | solution.py:172
  76.4 16.6 %all_to_all.22 = f32[16,32,128]{2,1,0:T(8,128)} all-to-all(f32[16,32,128]{2,1,0:T(8,128)S(1)} %bitcast.10), channel_id=1, replica_groups=mesh['zh'=4,'zl'=4,'x'=4,'y'=4,'c'=2] {'zl','x'}, dimensions={0} | all-to-all | bytes 524288 | tf_op jit(solution)/shard_map/all_to_all | solution.py:174
  93.0 5.0 %shard_map.67.refs_0_ = bf16[512,512]{1,0:T(8,128)(2,1)} custom-call(bf16[512,512]{1,0:T(8,128)(2,1)} %q_ref.1, bf16[512,512]{1,0:T(8,128)(2,1)} %k_ref.1, bf16[512,512]{1,0:T(8,128)(2,1)} %v_ref.1, f32[512,128]{1,0:T(8,128)} %bitcast.13, f32[1,512]{1,0:T(1,128)} %bitcast.14), custom_call_target="tpu_custom_call" | custom-call | tf_op jit(solution)/shard_map/pallas_call | solution.py:107
  98.0 1.9 %collective-permute-start.3 = (bf16[512,512]{1,0:T(8,128)(2,1)}, bf16[512,512]{1,0:T(8,128)(2,1)S(1)}, u32[]{:S(2)}, u32[]{:S(2)}) collective-permute-start(bf16[512,512]{1,0:T(8,128)(2,1)} %shard_map.67.refs_0_), channel_id=1, source_target_pairs={{0,4},{2,6},{4,0},{6,2},{1,5},{3,7},{5,1},{7,3},{8,12},{10,14},{12... | collective-permute-start | bytes 1572872 | tf_op jit(solution)/shard_map/ppermute | solution.py:151
  99.9 1.9 %collective-permute-start.2 = (bf16[512,512]{1,0:T(8,128)(2,1)}, bf16[512,512]{1,0:T(8,128)(2,1)S(1)}, u32[]{:S(2)}, u32[]{:S(2)}) collective-permute-start(bf16[512,512]{1,0:T(8,128)(2,1)} %shard_map.67.refs_0_), channel_id=1, source_target_pairs={{0,6},{2,0},{4,2},{6,4},{1,7},{3,1},{5,3},{7,5},{8,14},{10,8},{12,... | collective-permute-start | bytes 1572872 | tf_op jit(solution)/shard_map/ppermute | solution.py:151
  101.8 3.4 %collective-permute-start.1 = (bf16[512,512]{1,0:T(8,128)(2,1)}, bf16[512,512]{1,0:T(8,128)(2,1)S(1)}, u32[]{:S(2)}, u32[]{:S(2)}) collective-permute-start(bf16[512,512]{1,0:T(8,128)(2,1)} %shard_map.67.refs_0_), channel_id=1, source_target_pairs={{0,2},{2,4},{4,6},{6,0},{1,3},{3,5},{5,7},{7,1},{8,10},{10,12},{12... | collective-permute-start | bytes 1572872 | tf_op jit(solution)/shard_map/ppermute | solution.py:151
  105.2 10.8 %collective-permute-start.4 = (bf16[512,512]{1,0:T(8,128)(2,1)}, bf16[512,512]{1,0:T(8,128)(2,1)S(1)}, u32[]{:S(2)}, u32[]{:S(2)}) collective-permute-start(bf16[512,512]{1,0:T(8,128)(2,1)} %shard_map.67.refs_0_), channel_id=1, source_target_pairs={{0,1},{1,0},{2,3},{3,2},{4,5},{5,4},{6,7},{7,6},{8,9},{9,8},{10,11... | collective-permute-start | bytes 1572872 | tf_op jit(solution)/shard_map/ppermute | solution.py:151
  116.0 0.0 collective-permute-done.3.refs_3_
  116.0 7.6 %collective-permute-start.7 = (bf16[512,512]{1,0:T(8,128)(2,1)S(1)}, bf16[512,512]{1,0:T(8,128)(2,1)S(1)}, u32[]{:S(2)}, u32[]{:S(2)}) collective-permute-start(bf16[512,512]{1,0:T(8,128)(2,1)S(1)} %collective-permute-done.3.refs_3_), channel_id=1, source_target_pairs={{0,1},{1,0},{2,3},{3,2},{4,5},{5,4},{6,7},{7,6},{8,9},{9,8},{10,11... | collective-permute-start | bytes 1572872 | tf_op jit(solution)/shard_map/ppermute | solution.py:151
  123.6 0.5 collective-permute-done.2.refs_2_
  124.1 5.0 %collective-permute-start.6 = (bf16[512,512]{1,0:T(8,128)(2,1)S(1)}, bf16[512,512]{1,0:T(8,128)(2,1)S(1)}, u32[]{:S(2)}, u32[]{:S(2)}) collective-permute-start(bf16[512,512]{1,0:T(8,128)(2,1)S(1)} %collective-permute-done.2.refs_2_), channel_id=1, source_target_pairs={{0,1},{1,0},{2,3},{3,2},{4,5},{5,4},{6,7},{7,6},{8,9},{9,8},{10,11... | collective-permute-start | bytes 1572872 | tf_op jit(solution)/shard_map/ppermute | solution.py:151
  129.1 0.0 collective-permute-done.1.refs_1_
  129.1 1.9 %collective-permute-start.5 = (bf16[512,512]{1,0:T(8,128)(2,1)S(1)}, bf16[512,512]{1,0:T(8,128)(2,1)S(1)}, u32[]{:S(2)}, u32[]{:S(2)}) collective-permute-start(bf16[512,512]{1,0:T(8,128)(2,1)S(1)} %collective-permute-done.1.refs_1_), channel_id=1, source_target_pairs={{0,1},{1,0},{2,3},{3,2},{4,5},{5,4},{6,7},{7,6},{8,9},{9,8},{10,11... | collective-permute-start | bytes 1572872 | tf_op jit(solution)/shard_map/ppermute | solution.py:151
  131.0 0.0 copy-done.3
  131.0 0.1 pad_add_fusion.order_ref
  131.1 0.0 collective-permute-done.4.refs_4_
  131.1 0.0 collective-permute-done.7.refs_7_
  131.1 0.0 collective-permute-done.6.refs_6_
  131.1 1.7 %collective-permute-done.5.refs_5_ = bf16[512,512]{1,0:T(8,128)(2,1)S(1)} collective-permute-done((bf16[512,512]{1,0:T(8,128)(2,1)S(1)}, bf16[512,512]{1,0:T(8,128)(2,1)S(1)}, u32[]{:S(2)}, u32[]{:S(2)}) %collective-permute-start.5) | collective-permute-done | bytes 524320 | tf_op jit(solution)/shard_map/ppermute | solution.py:151
  132.9 0.8 copy-done.1
  133.7 1.0 copy-done
  134.7 1.0 copy-done.2
  135.8 8.1 %shard_map.68 = bf16[512,512]{1,0:T(8,128)(2,1)} custom-call(s32[8]{0:T(128)S(1)} %pad_add_fusion.order_ref, bf16[512,512]{1,0:T(8,128)(2,1)S(1)} %copy-done, bf16[512,512]{1,0:T(8,128)(2,1)S(1)} %collective-permute-done.1.refs_1_, bf16[512,512]{1,0:T(8,128)(2,1)S(1)} %collective-permute-done.2.refs_2_, bf16[512,512]{1,0:T(8,128)(2,1)S(1)} %collective-permute-done.3.refs_3_, ...), custom_call_target="tpu_custom_call" | custom-call | tf_op jit(solution)/shard_map/pallas_call | solution.py:134
  (8 shorter events, 0.1 us)
Async XLA Ops:
  6.5 124.5 %copy-start.3 = (s32[4]{0:T(128)S(1)}, s32[4]{0:T(128)}, u32[]{:S(2)}) copy-start(s32[4]{0:T(128)} %constant.34) | copy-start | bytes 52
  6.5 127.1 %all-gather.2.cloned.1.call-start = ((), (), s32[]{:S(2)}) async-start(), calls=%async_computation.2 | async-start | bytes 4456448 | tf_op jit(solution)/shard_map/all_gather | solution.py:168
  6.5 15.7 %collective-permute-start = (bf16[64,512]{1,0:T(8,128)(2,1)}, bf16[64,512]{1,0:T(8,128)(2,1)S(1)}, u32[]{:S(2)}, u32[]{:S(2)}) collective-permute-start(bf16[64,512]{1,0:T(8,128)(2,1)} %bitcast.15), channel_id=1, source_target_pairs={{0,0},{1,64},{2,128},{3,192},{4,256},{5,320},{6,384},{7,448},{32,3... | collective-permute-start | bytes 196616 | tf_op jit(solution)/shard_map/ppermute | solution.py:159
  36.4 14.7 %all-to-all-start = ((f32[16,32,128]{2,1,0:T(8,128)}), f32[16,32,128]{2,1,0:T(8,128)S(1)}, u32[]{:S(2)}, u32[]{:S(2)}) async-start(f32[16,32,128]{2,1,0:T(8,128)} %bitcast.12), calls=%async_computation | async-start | bytes 524288 | tf_op jit(solution)/shard_map/all_to_all | solution.py:171
  98.0 18.0 %collective-permute-start.3 = (bf16[512,512]{1,0:T(8,128)(2,1)}, bf16[512,512]{1,0:T(8,128)(2,1)S(1)}, u32[]{:S(2)}, u32[]{:S(2)}) collective-permute-start(bf16[512,512]{1,0:T(8,128)(2,1)} %shard_map.67.refs_0_), channel_id=1, source_target_pairs={{0,4},{2,6},{4,0},{6,2},{1,5},{3,7},{5,1},{7,3},{8,12},{10,14},{12... | collective-permute-start | bytes 1572872 | tf_op jit(solution)/shard_map/ppermute | solution.py:151
  99.9 24.2 %collective-permute-start.2 = (bf16[512,512]{1,0:T(8,128)(2,1)}, bf16[512,512]{1,0:T(8,128)(2,1)S(1)}, u32[]{:S(2)}, u32[]{:S(2)}) collective-permute-start(bf16[512,512]{1,0:T(8,128)(2,1)} %shard_map.67.refs_0_), channel_id=1, source_target_pairs={{0,6},{2,0},{4,2},{6,4},{1,7},{3,1},{5,3},{7,5},{8,14},{10,8},{12,... | collective-permute-start | bytes 1572872 | tf_op jit(solution)/shard_map/ppermute | solution.py:151
  101.8 27.2 %collective-permute-start.1 = (bf16[512,512]{1,0:T(8,128)(2,1)}, bf16[512,512]{1,0:T(8,128)(2,1)S(1)}, u32[]{:S(2)}, u32[]{:S(2)}) collective-permute-start(bf16[512,512]{1,0:T(8,128)(2,1)} %shard_map.67.refs_0_), channel_id=1, source_target_pairs={{0,2},{2,4},{4,6},{6,0},{1,3},{3,5},{5,7},{7,1},{8,10},{10,12},{12... | collective-permute-start | bytes 1572872 | tf_op jit(solution)/shard_map/ppermute | solution.py:151
  105.2 25.9 %collective-permute-start.4 = (bf16[512,512]{1,0:T(8,128)(2,1)}, bf16[512,512]{1,0:T(8,128)(2,1)S(1)}, u32[]{:S(2)}, u32[]{:S(2)}) collective-permute-start(bf16[512,512]{1,0:T(8,128)(2,1)} %shard_map.67.refs_0_), channel_id=1, source_target_pairs={{0,1},{1,0},{2,3},{3,2},{4,5},{5,4},{6,7},{7,6},{8,9},{9,8},{10,11... | collective-permute-start | bytes 1572872 | tf_op jit(solution)/shard_map/ppermute | solution.py:151
  116.0 15.1 %collective-permute-start.7 = (bf16[512,512]{1,0:T(8,128)(2,1)S(1)}, bf16[512,512]{1,0:T(8,128)(2,1)S(1)}, u32[]{:S(2)}, u32[]{:S(2)}) collective-permute-start(bf16[512,512]{1,0:T(8,128)(2,1)S(1)} %collective-permute-done.3.refs_3_), channel_id=1, source_target_pairs={{0,1},{1,0},{2,3},{3,2},{4,5},{5,4},{6,7},{7,6},{8,9},{9,8},{10,11... | collective-permute-start | bytes 1572872 | tf_op jit(solution)/shard_map/ppermute | solution.py:151
  124.1 7.1 %collective-permute-start.6 = (bf16[512,512]{1,0:T(8,128)(2,1)S(1)}, bf16[512,512]{1,0:T(8,128)(2,1)S(1)}, u32[]{:S(2)}, u32[]{:S(2)}) collective-permute-start(bf16[512,512]{1,0:T(8,128)(2,1)S(1)} %collective-permute-done.2.refs_2_), channel_id=1, source_target_pairs={{0,1},{1,0},{2,3},{3,2},{4,5},{5,4},{6,7},{7,6},{8,9},{9,8},{10,11... | collective-permute-start | bytes 1572872 | tf_op jit(solution)/shard_map/ppermute | solution.py:151
  129.1 3.8 %collective-permute-start.5 = (bf16[512,512]{1,0:T(8,128)(2,1)S(1)}, bf16[512,512]{1,0:T(8,128)(2,1)S(1)}, u32[]{:S(2)}, u32[]{:S(2)}) collective-permute-start(bf16[512,512]{1,0:T(8,128)(2,1)S(1)} %collective-permute-done.1.refs_1_), channel_id=1, source_target_pairs={{0,1},{1,0},{2,3},{3,2},{4,5},{5,4},{6,7},{7,6},{8,9},{9,8},{10,11... | collective-permute-start | bytes 1572872 | tf_op jit(solution)/shard_map/ppermute | solution.py:151
  132.9 0.8 copy-start.1
  133.7 1.0 copy-start
  134.7 1.0 copy-start.2
Sparse Core Ops, SparseCore 0:
  32.8 84.0 all-gather.1

commit v3 on v2

v3 whole, which is shorter than its diff:
```python
import functools

import jax
import jax.numpy as jnp
from jax import lax
from jax.experimental import pallas as pl
from jax.experimental.pallas import tpu as pltpu
from jax.sharding import Mesh, PartitionSpec as P

HEAD = 128
TILE = 256
PARTS = 2
AHEAD = 8
GROUP = ("zl", "x")
NT = (((1,), (1,)), ((), ()))
TN = (((0,), (0,)), ((), ()))


def params(mib):
    return pltpu.CompilerParams(vmem_limit_bytes=mib * 1024 * 1024)


def in_vmem():
    return pl.BlockSpec(memory_space=pltpu.VMEM)


def in_hbm():
    return pl.BlockSpec(memory_space=pltpu.HBM)


def fetch(sources, buffers, sems):
    parts = sems.shape[1]
    copies = []
    for part in range(parts):
        for at, (source, buffer) in enumerate(zip(sources, buffers)):
            rows = source.shape[0] // parts
            own = pl.ds(part * rows, rows)
            copies.append(pltpu.make_async_copy(source.at[own], buffer.at[own], sems.at[at, part]))
    for copy in copies:
        copy.start()
    for copy in copies:
        copy.wait()


def block_state_kernel(k_hbm, v_hbm, s_ref, k_ref, v_ref, sems):
    fetch((k_hbm, v_hbm), (k_ref, v_ref), sems)
    for h in range(k_ref.shape[1] // HEAD):
        cols = slice(h * HEAD, (h + 1) * HEAD)
        s_ref[cols, :] = lax.dot_general(k_ref[:, cols], v_ref[:, cols], TN, preferred_element_type=jnp.float32)


def block_state(keys, values):
    return pl.pallas_call(
        block_state_kernel,
        out_shape=jax.ShapeDtypeStruct((keys.shape[1], HEAD), jnp.float32),
        in_specs=[in_hbm()] * 2,
        out_specs=in_vmem(),
        scratch_shapes=[pltpu.VMEM(keys.shape, keys.dtype)] * 2 + [pltpu.SemaphoreType.DMA((2, PARTS))],
        compiler_params=params(32),
    )(keys, values)


def total_kernel(s_ref, t_ref):
    rows = t_ref.shape[0]
    total = s_ref[:rows, :]
    for b in range(1, s_ref.shape[0] // rows):
        total = total + s_ref[b * rows:(b + 1) * rows, :]
    t_ref[...] = total


def group_total(pieces, blocks):
    return pl.pallas_call(
        total_kernel,
        out_shape=jax.ShapeDtypeStruct((pieces.shape[0] // blocks, HEAD), jnp.float32),
        in_specs=[in_vmem()],
        out_specs=in_vmem(),
        compiler_params=params(32),
    )(pieces)


def prefix_kernel(s_ref, *refs):
    *earlier_refs, p_ref = refs
    rows = earlier_refs[0].shape[0]
    total = earlier_refs[0][...]
    for ref in earlier_refs[1:]:
        total = total + ref[...]
    for b in range(s_ref.shape[0] // rows):
        at = slice(b * rows, (b + 1) * rows)
        p_ref[at, :] = total
        total = total + s_ref[at, :]


def prefix(pieces, earlier):
    return pl.pallas_call(
        prefix_kernel,
        out_shape=jax.ShapeDtypeStruct(pieces.shape, jnp.float32),
        in_specs=[in_vmem()] * (1 + len(earlier)),
        out_specs=in_vmem(),
        compiler_params=params(32),
    )(pieces, *earlier)


def attend_kernel(q_hbm, k_hbm, v_hbm, s_ref, g_ref, o_ref, q_ref, k_ref, v_ref, sems):
    fetch((q_hbm, k_hbm, v_hbm), (q_ref, k_ref, v_ref), sems)
    rows, width = o_ref.shape
    row = lax.broadcasted_iota(jnp.int32, (TILE, TILE), 0)
    col = lax.broadcasted_iota(jnp.int32, (TILE, TILE), 1)
    causal = row >= col
    for h in range(width // HEAD):
        cols = slice(h * HEAD, (h + 1) * HEAD)
        state = s_ref[cols, :]
        high = state.astype(jnp.bfloat16)
        low = (state - high.astype(jnp.float32)).astype(jnp.bfloat16)
        for first in range(0, rows, TILE):
            own = slice(first, first + TILE)
            query = q_ref[own, cols]
            scores = lax.dot_general(query, k_ref[:first + TILE, cols], NT, preferred_element_type=jnp.float32)
            left = [query, query, jnp.where(causal, scores[:, first:], 0.0).astype(jnp.bfloat16)]
            right = [high, low, v_ref[own, cols]]
            if first:
                left.append(scores[:, :first].astype(jnp.bfloat16))
                right.append(v_ref[:first, cols])
            left, right = jnp.concatenate(left, axis=1), jnp.concatenate(right, axis=0)
            attended = jnp.dot(left, right, preferred_element_type=jnp.float32)
            meansq = jnp.mean(attended * attended, axis=-1, keepdims=True)
            o_ref[own, cols] = (attended * lax.rsqrt(meansq + 1e-06) * g_ref[:, cols]).astype(jnp.bfloat16)


def attend(queries, keys, values, states, gain):
    return pl.pallas_call(
        attend_kernel,
        out_shape=jax.ShapeDtypeStruct(queries.shape, jnp.bfloat16),
        in_specs=[in_hbm()] * 3 + [in_vmem()] * 2,
        out_specs=in_vmem(),
        scratch_shapes=[pltpu.VMEM(queries.shape, queries.dtype)] * 3 + [pltpu.SemaphoreType.DMA((3, PARTS))],
        compiler_params=params(32),
    )(queries, keys, values, states, gain)


def project_kernel(order_ref, *refs):
    *hidden_hbm, w_hbm, o_ref, h_ref, w_ref, sems = refs
    groups = len(hidden_hbm)

    def copies(at):
        return (
            pltpu.make_async_copy(w_hbm.at[order_ref[at]], w_ref.at[at], sems.at[0, at]),
            pltpu.make_async_copy(hidden_hbm[at], h_ref.at[at], sems.at[1, at]),
        )

    def start(at):
        for copy in copies(at):
            copy.start()

    for at in range(AHEAD):
        start(at)
    total = None
    for at in range(groups):
        for copy in copies(at):
            copy.wait()
        if at + AHEAD < groups:
            start(at + AHEAD)
        product = lax.dot_general(h_ref[at], w_ref[at], NT, preferred_element_type=jnp.float32)
        total = product if total is None else total + product
    o_ref[...] = total.astype(o_ref.dtype)


def project(order, hidden, weight):
    groups = weight.shape[0]
    rows = hidden[0].shape[0]
    return pl.pallas_call(
        project_kernel,
        out_shape=jax.ShapeDtypeStruct((rows, weight.shape[1]), jnp.bfloat16),
        in_specs=[pl.BlockSpec(memory_space=pltpu.SMEM)] + [in_hbm()] * (groups + 1),
        out_specs=in_vmem(),
        scratch_shapes=[
            pltpu.VMEM((groups, *hidden[0].shape), hidden[0].dtype),
            pltpu.VMEM(weight.shape, weight.dtype),
            pltpu.SemaphoreType.DMA((2, groups)),
        ],
        compiler_params=params(62),
    )(order, *hidden, weight)


def shift(array, axis, by):
    size = lax.axis_size(axis)
    return lax.ppermute(array, axis, [(i, (i + by) % size) for i in range(size)])


def from_earlier(array, axis, by):
    size = lax.axis_size(axis)
    return lax.ppermute(array, axis, [(i, i + by) for i in range(size - by)])


def spread(array, axis):
    return lax.all_to_all(jnp.concatenate([array] * lax.axis_size(axis), axis=0), axis, 0, 0, tiled=True)


def turn(place):
    row, core = place // 2, place % 2
    return row * (1 - 2 * core) + 4 * core * (row == 0)


def to_columns(shard):
    pairs = []
    for z in range(16):
        for t in range(8):
            pairs.append((z * 8 + t, (z + 2 * turn(t)) % 16 * 8 + z // 2))
    return lax.ppermute(shard, ("zh", "zl", "y", "c"), pairs)


def shards(queries, keys, values, norm_gain, out_weight):
    blocks = lax.axis_size("zl") * lax.axis_size("x")
    tp = lax.axis_size("y") * lax.axis_size("c")
    shard, state = lax.optimization_barrier((to_columns(out_weight.T), block_state(keys, values)))
    near = spread(shard, "x")
    pieces = lax.all_to_all(state, GROUP, 0, 0, tiled=True)
    weight = lax.all_gather(near, ("zh", "zl"), axis=0, tiled=True)
    weight = weight.reshape(tp, -1, out_weight.shape[0])

    total = group_total(pieces, blocks)
    earlier = [from_earlier(total, "zh", by) for by in range(1, lax.axis_size("zh"))]
    states = lax.all_to_all(prefix(pieces, earlier), GROUP, 0, 0, tiled=True)
    hidden = attend(queries, keys, values, states, norm_gain[None, :])

    steps = (0, 1, -1, 2)
    held = [hidden] + [shift(hidden, "y", by) for by in steps[1:]]
    held = held + [shift(h, "c", 1) for h in held]
    row, core = lax.axis_index("y"), lax.axis_index("c")
    place = (row - jnp.array(steps, jnp.int32)) % lax.axis_size("y") * 2
    place = jnp.concatenate([place + core, place + 1 - core])
    order = (row * 2 + core + turn(place)) % tp
    return project(order.astype(jnp.int32), held, weight)


def solution(mesh):
    axes = ("zh", "zl", "x", "y", "c")
    grid = Mesh(mesh.devices.reshape(4, 4, 4, 4, 2), axes)
    seq, tp = axes[:3], axes[3:]
    return jax.shard_map(
        shards,
        mesh=grid,
        in_specs=(P(seq, tp), P(seq, tp), P(seq, tp), P(tp), P(tp, seq)),
        out_specs=P(seq, tp),
        check_vma=False,
    )
```

time: 152 us -> 133 us (0.88)
  the two profiles are of different devices: /device:TPU:9 before, /device:TPU:24 now
where the time goes in v3:
time: 133 us; the launch traced here: 132 us
  starting transfers between devices  47.6 us (36%)
  blocking collectives  43.6 us (33%)
  waiting for transfers between devices  14.2 us (11%)
  between operations  13.6 us (10%)
  Pallas kernels  8.43 us (6%)
  local copies, waits for them, and re-layouts  3.79 us (3%)
    ppermute x7, starting transfers between devices, shift(): lax.ppermute(array, axis, [(i, (i + by) % size) for i in range(size)])  22.5 us
    all_to_all x1, blocking collectives, shards(): states = lax.all_to_all(prefix(pieces, earlier), GROUP, 0, 0, tiled=True)  17.6 us
    all_to_all x1, blocking collectives, shards(): pieces = lax.all_to_all(state, GROUP, 0, 0, tiled=True)  14 us
    ppermute x3, starting transfers between devices, from_earlier(): return lax.ppermute(array, axis, [(i, i + by) for i in range(size - by)])  13.6 us
    all_to_all x1, blocking collectives, spread(): lax.all_to_all(jnp.concatenate([array] * lax.axis_size(axis), axis=0), ax...  12 us
    ppermute x1, starting transfers between devices, to_columns(): return lax.ppermute(shard, ('zh', 'zl', 'y', 'c'), pairs)  11.6 us
    ppermute x7, waiting for transfers between devices, shift(): lax.ppermute(array, axis, [(i, (i + by) % size) for i in range(size)])  6.25 us
    pallas_call x1, Pallas kernels, project(): pl.pallas_call(project_kernel, out_shape=jax.ShapeDtypeStruct((rows, weig...  5.98 us
  transfers between devices with their start and end apart: 12, of which 5 were waited for; matrix products, arithmetic and copies ran while one was open for 0% of the time, Pallas kernels for 2%

profile of v3, /device:TPU:24, one launch (start us, length us, event | category | flops | bytes accessed | tf_op | source)
XLA Modules:
  0.0 132.0 jit_solution(10839567144509470047)
XLA Ops:
  6.5 11.6 %collective-permute-start = (bf16[64,512]{1,0:T(8,128)(2,1)}, bf16[64,512]{1,0:T(8,128)(2,1)S(1)}, u32[]{:S(2)}, u32[]{:S(2)}) collective-permute-start(bf16[64,512]{1,0:T(8,128)(2,1)} %bitcast.18), channel_id=1, source_target_pairs={{0,0},{1,256},{2,64},{3,448},{4,128},{5,384},{6,192},{7,320},{32,3... | collective-permute-start | bytes 196616 | tf_op jit(solution)/shard_map/ppermute | solution.py:208
  18.1 1.0 copy-done.1
  19.2 1.0 copy-done.3
  20.2 0.5 shard_map.64
  20.7 2.4 %collective-permute-done = bf16[64,512]{1,0:T(8,128)(2,1)S(1)} collective-permute-done((bf16[64,512]{1,0:T(8,128)(2,1)}, bf16[64,512]{1,0:T(8,128)(2,1)S(1)}, u32[]{:S(2)}, u32[]{:S(2)}) %collective-permute-start) | collective-permute-done | bytes 65568 | tf_op jit(solution)/shard_map/ppermute | solution.py:208
  23.1 12.0 %all_to_all.34 = bf16[4,64,512]{2,1,0:T(8,128)(2,1)} all-to-all(bf16[4,64,512]{2,1,0:T(8,128)(2,1)S(1)} %bitcast.16), channel_id=1, replica_groups=mesh['zh'=4,'zl'=4,'x'=4,'y'=4,'c'=2] {'x'}, dimensions={0} | all-to-all | bytes 524288 | tf_op jit(solution)/shard_map/all_to_all | solution.py:195
  35.1 0.0 all-gather.2.cloned.1.call-update
  35.1 14.0 %all_to_all.35 = f32[16,32,128]{2,1,0:T(8,128)S(1)} all-to-all(f32[16,32,128]{2,1,0:T(8,128)S(1)} %bitcast.11), channel_id=1, replica_groups=mesh['zh'=4,'zl'=4,'x'=4,'y'=4,'c'=2] {'zl','x'}, dimensions={0} | all-to-all | bytes 524288 | tf_op jit(solution)/shard_map/all_to_all | solution.py:216
  49.2 5.0 %collective-permute-start.3 = (f32[32,128]{1,0:T(8,128)S(1)}, f32[32,128]{1,0:T(8,128)S(1)}, u32[]{:S(2)}, u32[]{:S(2)}) collective-permute-start(f32[32,128]{1,0:T(8,128)S(1)} %shard_map.65), channel_id=1, source_target_pairs={{0,384},{1,385},{2,386},{3,387},{4,388},{5,389},{6,390},{7,391},{8... | collective-permute-start | bytes 49160 | tf_op jit(solution)/shard_map/ppermute | solution.py:191
  54.2 4.9 %collective-permute-start.2 = (f32[32,128]{1,0:T(8,128)S(1)}, f32[32,128]{1,0:T(8,128)S(1)}, u32[]{:S(2)}, u32[]{:S(2)}) collective-permute-start(f32[32,128]{1,0:T(8,128)S(1)} %shard_map.65), channel_id=1, source_target_pairs={{0,256},{128,384},{1,257},{129,385},{2,258},{130,386},{3,259},{131... | collective-permute-start | bytes 49160 | tf_op jit(solution)/shard_map/ppermute | solution.py:191
  59.1 3.6 %collective-permute-start.1 = (f32[32,128]{1,0:T(8,128)S(1)}, f32[32,128]{1,0:T(8,128)S(1)}, u32[]{:S(2)}, u32[]{:S(2)}) collective-permute-start(f32[32,128]{1,0:T(8,128)S(1)} %shard_map.65), channel_id=1, source_target_pairs={{0,128},{128,256},{256,384},{1,129},{129,257},{257,385},{2,130},{1... | collective-permute-start | bytes 49160 | tf_op jit(solution)/shard_map/ppermute | solution.py:191
  62.8 0.0 collective-permute-done.3.refs_2_
  62.8 0.0 collective-permute-done.2.refs_1_
  62.8 1.5 %collective-permute-done.1.refs_0_ = f32[32,128]{1,0:T(8,128)S(1)} collective-permute-done((f32[32,128]{1,0:T(8,128)S(1)}, f32[32,128]{1,0:T(8,128)S(1)}, u32[]{:S(2)}, u32[]{:S(2)}) %collective-permute-start.1) | collective-permute-done | bytes 16416 | tf_op jit(solution)/shard_map/ppermute | solution.py:191
  64.3 17.6 %all_to_all.36 = f32[16,32,128]{2,1,0:T(8,128)S(1)} all-to-all(f32[16,32,128]{2,1,0:T(8,128)S(1)} %bitcast.12), channel_id=1, replica_groups=mesh['zh'=4,'zl'=4,'x'=4,'y'=4,'c'=2] {'zl','x'}, dimensions={0} | all-to-all | bytes 524288 | tf_op jit(solution)/shard_map/all_to_all | solution.py:222
  81.8 1.9 %shard_map.67.refs_0_ = bf16[512,512]{1,0:T(8,128)(2,1)S(1)} custom-call(bf16[512,512]{1,0:T(8,128)(2,1)S(1)} %copy-done.5, bf16[512,512]{1,0:T(8,128)(2,1)S(1)} %copy-done.2, bf16[512,512]{1,0:T(8,128)(2,1)S(1)} %copy-done.4, f32[512,128]{1,0:T(8,128)S(1)} %bitcast.13, f32[1,512]{1,0:T(1,128)S(1)} %bitcast.14), custom_call_target="tpu_custom_call" | custom-call | tf_op jit(solution)/shard_map/pallas_call | solution.py:130
  83.8 7.3 %collective-permute-start.6 = (bf16[512,512]{1,0:T(8,128)(2,1)S(1)}, bf16[512,512]{1,0:T(8,128)(2,1)S(1)}, u32[]{:S(2)}, u32[]{:S(2)}) collective-permute-start(bf16[512,512]{1,0:T(8,128)(2,1)S(1)} %shard_map.67.refs_0_), channel_id=1, source_target_pairs={{0,4},{2,6},{4,0},{6,2},{1,5},{3,7},{5,1},{7,3},{8,12},{10,14},{12... | collective-permute-start | bytes 1572872 | tf_op jit(solution)/shard_map/ppermute | solution.py:186
  91.1 1.9 %collective-permute-start.5 = (bf16[512,512]{1,0:T(8,128)(2,1)S(1)}, bf16[512,512]{1,0:T(8,128)(2,1)S(1)}, u32[]{:S(2)}, u32[]{:S(2)}) collective-permute-start(bf16[512,512]{1,0:T(8,128)(2,1)S(1)} %shard_map.67.refs_0_), channel_id=1, source_target_pairs={{0,6},{2,0},{4,2},{6,4},{1,7},{3,1},{5,3},{7,5},{8,14},{10,8},{12,... | collective-permute-start | bytes 1572872 | tf_op jit(solution)/shard_map/ppermute | solution.py:186
  93.0 5.1 %collective-permute-start.4 = (bf16[512,512]{1,0:T(8,128)(2,1)S(1)}, bf16[512,512]{1,0:T(8,128)(2,1)S(1)}, u32[]{:S(2)}, u32[]{:S(2)}) collective-permute-start(bf16[512,512]{1,0:T(8,128)(2,1)S(1)} %shard_map.67.refs_0_), channel_id=1, source_target_pairs={{0,2},{2,4},{4,6},{6,0},{1,3},{3,5},{5,7},{7,1},{8,10},{10,12},{12... | collective-permute-start | bytes 1572872 | tf_op jit(solution)/shard_map/ppermute | solution.py:186
  98.1 1.9 %collective-permute-start.7 = (bf16[512,512]{1,0:T(8,128)(2,1)S(1)}, bf16[512,512]{1,0:T(8,128)(2,1)S(1)}, u32[]{:S(2)}, u32[]{:S(2)}) collective-permute-start(bf16[512,512]{1,0:T(8,128)(2,1)S(1)} %shard_map.67.refs_0_), channel_id=1, source_target_pairs={{0,1},{1,0},{2,3},{3,2},{4,5},{5,4},{6,7},{7,6},{8,9},{9,8},{10,11... | collective-permute-start | bytes 1572872 | tf_op jit(solution)/shard_map/ppermute | solution.py:186
  100.1 2.6 %collective-permute-done.6.refs_3_ = bf16[512,512]{1,0:T(8,128)(2,1)S(1)} collective-permute-done((bf16[512,512]{1,0:T(8,128)(2,1)S(1)}, bf16[512,512]{1,0:T(8,128)(2,1)S(1)}, u32[]{:S(2)}, u32[]{:S(2)}) %collective-permute-start.6) | collective-permute-done | bytes 524320 | tf_op jit(solution)/shard_map/ppermute | solution.py:186
  102.7 1.9 %collective-permute-start.10 = (bf16[512,512]{1,0:T(8,128)(2,1)S(1)}, bf16[512,512]{1,0:T(8,128)(2,1)S(1)}, u32[]{:S(2)}, u32[]{:S(2)}) collective-permute-start(bf16[512,512]{1,0:T(8,128)(2,1)S(1)} %collective-permute-done.6.refs_3_), channel_id=1, source_target_pairs={{0,1},{1,0},{2,3},{3,2},{4,5},{5,4},{6,7},{7,6},{8,9},{9,8},{10,11... | collective-permute-start | bytes 1572872 | tf_op jit(solution)/shard_map/ppermute | solution.py:186
  104.6 3.6 %collective-permute-done.5.refs_2_ = bf16[512,512]{1,0:T(8,128)(2,1)S(1)} collective-permute-done((bf16[512,512]{1,0:T(8,128)(2,1)S(1)}, bf16[512,512]{1,0:T(8,128)(2,1)S(1)}, u32[]{:S(2)}, u32[]{:S(2)}) %collective-permute-start.5) | collective-permute-done | bytes 524320 | tf_op jit(solution)/shard_map/ppermute | solution.py:186
  108.2 1.9 %collective-permute-start.9 = (bf16[512,512]{1,0:T(8,128)(2,1)S(1)}, bf16[512,512]{1,0:T(8,128)(2,1)S(1)}, u32[]{:S(2)}, u32[]{:S(2)}) collective-permute-start(bf16[512,512]{1,0:T(8,128)(2,1)S(1)} %collective-permute-done.5.refs_2_), channel_id=1, source_target_pairs={{0,1},{1,0},{2,3},{3,2},{4,5},{5,4},{6,7},{7,6},{8,9},{9,8},{10,11... | collective-permute-start | bytes 1572872 | tf_op jit(solution)/shard_map/ppermute | solution.py:186
  110.1 0.0 collective-permute-done.4.refs_1_
  110.2 2.4 %collective-permute-start.8 = (bf16[512,512]{1,0:T(8,128)(2,1)S(1)}, bf16[512,512]{1,0:T(8,128)(2,1)}, u32[]{:S(2)}, u32[]{:S(2)}) collective-permute-start(bf16[512,512]{1,0:T(8,128)(2,1)S(1)} %collective-permute-done.4.refs_1_), channel_id=1, source_target_pairs={{0,1},{1,0},{2,3},{3,2},{4,5},{5,4},{6,7},{7,6},{8,9},{9,8},{10,11... | collective-permute-start | bytes 1572872 | tf_op jit(solution)/shard_map/ppermute | solution.py:186
  112.6 0.6 and_select_fusion.order_ref
  113.3 0.0 collective-permute-done.7.refs_4_
  113.3 0.9 copy-done.11
  114.2 0.8 copy-done.12
  115.0 4.1 %all-gather.2.cloned.1.call-done = bf16[4096,512]{1,0:T(8,128)(2,1)} async-done(((bf16[256,512]{1,0:T(8,128)(2,1)}), bf16[4096,512]{1,0:T(8,128)(2,1)}) %all-gather.2.cloned.1.call-update) | async-done | bytes 4194320 | tf_op jit(solution)/shard_map/all_gather | solution.py:217
  119.1 6.0 %shard_map.68 = bf16[512,512]{1,0:T(8,128)(2,1)} custom-call(s32[8]{0:T(128)} %and_select_fusion.order_ref, bf16[512,512]{1,0:T(8,128)(2,1)} %copy-done, bf16[512,512]{1,0:T(8,128)(2,1)} %copy-done.9, bf16[512,512]{1,0:T(8,128)(2,1)} %copy-done.8, bf16[512,512]{1,0:T(8,128)(2,1)} %copy-done.7, bf16[512,512]{1,0:T(8,128)(2,1)} %copy-done.10, ...), custom_call_target="tpu_custom_call" | custom-call | tf_op jit(solution)/shard_map/pallas_call | solution.py:170
  (33 shorter events, 0.1 us)
Async XLA Ops:
  6.5 106.0 %copy-start.13 = (s32[4]{0:T(128)S(1)}, s32[4]{0:T(128)}, u32[]{:S(2)}) copy-start(s32[4]{0:T(128)} %constant.69) | copy-start | bytes 52
  6.5 112.6 %all-gather.2.cloned.1.call-start = ((), (), s32[]{:S(2)}) async-start(), calls=%async_computation.3 | async-start | bytes 4456448 | tf_op jit(solution)/shard_map/all_gather | solution.py:217
  6.5 16.5 %collective-permute-start = (bf16[64,512]{1,0:T(8,128)(2,1)}, bf16[64,512]{1,0:T(8,128)(2,1)S(1)}, u32[]{:S(2)}, u32[]{:S(2)}) collective-permute-start(bf16[64,512]{1,0:T(8,128)(2,1)} %bitcast.18), channel_id=1, source_target_pairs={{0,0},{1,256},{2,64},{3,448},{4,128},{5,384},{6,192},{7,320},{32,3... | collective-permute-start | bytes 196616 | tf_op jit(solution)/shard_map/ppermute | solution.py:208
  18.1 1.0 copy-start.1
  19.2 1.0 copy-start.3
  20.2 61.6 %copy-start.2 = (bf16[512,512]{1,0:T(8,128)(2,1)S(1)}, bf16[512,512]{1,0:T(8,128)(2,1)}, u32[]{:S(2)}) copy-start(bf16[512,512]{1,0:T(8,128)(2,1)} %k_hbm.3) | copy-start | bytes 1572868
  20.2 61.6 %copy-start.4 = (bf16[512,512]{1,0:T(8,128)(2,1)S(1)}, bf16[512,512]{1,0:T(8,128)(2,1)}, u32[]{:S(2)}) copy-start(bf16[512,512]{1,0:T(8,128)(2,1)} %v_hbm.3) | copy-start | bytes 1572868
  20.2 61.6 %copy-start.5 = (bf16[512,512]{1,0:T(8,128)(2,1)S(1)}, bf16[512,512]{1,0:T(8,128)(2,1)}, u32[]{:S(2)}) copy-start(bf16[512,512]{1,0:T(8,128)(2,1)} %q_hbm.1) | copy-start | bytes 1572868
  20.2 61.6 %copy-start.6 = (f32[512]{0:T(512)S(1)}, f32[512]{0:T(512)}, u32[]{:S(2)}) copy-start(f32[512]{0:T(512)} %param.9) | copy-start | bytes 6148
  49.2 13.6 %collective-permute-start.3 = (f32[32,128]{1,0:T(8,128)S(1)}, f32[32,128]{1,0:T(8,128)S(1)}, u32[]{:S(2)}, u32[]{:S(2)}) collective-permute-start(f32[32,128]{1,0:T(8,128)S(1)} %shard_map.65), channel_id=1, source_target_pairs={{0,384},{1,385},{2,386},{3,387},{4,388},{5,389},{6,390},{7,391},{8... | collective-permute-start | bytes 49160 | tf_op jit(solution)/shard_map/ppermute | solution.py:191
  54.2 8.6 %collective-permute-start.2 = (f32[32,128]{1,0:T(8,128)S(1)}, f32[32,128]{1,0:T(8,128)S(1)}, u32[]{:S(2)}, u32[]{:S(2)}) collective-permute-start(f32[32,128]{1,0:T(8,128)S(1)} %shard_map.65), channel_id=1, source_target_pairs={{0,256},{128,384},{1,257},{129,385},{2,258},{130,386},{3,259},{131... | collective-permute-start | bytes 49160 | tf_op jit(solution)/shard_map/ppermute | solution.py:191
  59.1 5.1 %collective-permute-start.1 = (f32[32,128]{1,0:T(8,128)S(1)}, f32[32,128]{1,0:T(8,128)S(1)}, u32[]{:S(2)}, u32[]{:S(2)}) collective-permute-start(f32[32,128]{1,0:T(8,128)S(1)} %shard_map.65), channel_id=1, source_target_pairs={{0,128},{128,256},{256,384},{1,129},{129,257},{257,385},{2,130},{1... | collective-permute-start | bytes 49160 | tf_op jit(solution)/shard_map/ppermute | solution.py:191
  83.8 35.3 %copy-start = (bf16[512,512]{1,0:T(8,128)(2,1)}, bf16[512,512]{1,0:T(8,128)(2,1)S(1)}, u32[]{:S(2)}) copy-start(bf16[512,512]{1,0:T(8,128)(2,1)S(1)} %shard_map.67.refs_0_) | copy-start | bytes 1572868
  83.8 18.9 %collective-permute-start.6 = (bf16[512,512]{1,0:T(8,128)(2,1)S(1)}, bf16[512,512]{1,0:T(8,128)(2,1)S(1)}, u32[]{:S(2)}, u32[]{:S(2)}) collective-permute-start(bf16[512,512]{1,0:T(8,128)(2,1)S(1)} %shard_map.67.refs_0_), channel_id=1, source_target_pairs={{0,4},{2,6},{4,0},{6,2},{1,5},{3,7},{5,1},{7,3},{8,12},{10,14},{12... | collective-permute-start | bytes 1572872 | tf_op jit(solution)/shard_map/ppermute | solution.py:186
  91.1 17.2 %collective-permute-start.5 = (bf16[512,512]{1,0:T(8,128)(2,1)S(1)}, bf16[512,512]{1,0:T(8,128)(2,1)S(1)}, u32[]{:S(2)}, u32[]{:S(2)}) collective-permute-start(bf16[512,512]{1,0:T(8,128)(2,1)S(1)} %shard_map.67.refs_0_), channel_id=1, source_target_pairs={{0,6},{2,0},{4,2},{6,4},{1,7},{3,1},{5,3},{7,5},{8,14},{10,8},{12,... | collective-permute-start | bytes 1572872 | tf_op jit(solution)/shard_map/ppermute | solution.py:186
  93.0 17.2 %collective-permute-start.4 = (bf16[512,512]{1,0:T(8,128)(2,1)S(1)}, bf16[512,512]{1,0:T(8,128)(2,1)S(1)}, u32[]{:S(2)}, u32[]{:S(2)}) collective-permute-start(bf16[512,512]{1,0:T(8,128)(2,1)S(1)} %shard_map.67.refs_0_), channel_id=1, source_target_pairs={{0,2},{2,4},{4,6},{6,0},{1,3},{3,5},{5,7},{7,1},{8,10},{10,12},{12... | collective-permute-start | bytes 1572872 | tf_op jit(solution)/shard_map/ppermute | solution.py:186
  98.1 15.1 %collective-permute-start.7 = (bf16[512,512]{1,0:T(8,128)(2,1)S(1)}, bf16[512,512]{1,0:T(8,128)(2,1)S(1)}, u32[]{:S(2)}, u32[]{:S(2)}) collective-permute-start(bf16[512,512]{1,0:T(8,128)(2,1)S(1)} %shard_map.67.refs_0_), channel_id=1, source_target_pairs={{0,1},{1,0},{2,3},{3,2},{4,5},{5,4},{6,7},{7,6},{8,9},{9,8},{10,11... | collective-permute-start | bytes 1572872 | tf_op jit(solution)/shard_map/ppermute | solution.py:186
  102.7 16.4 %copy-start.7 = (bf16[512,512]{1,0:T(8,128)(2,1)}, bf16[512,512]{1,0:T(8,128)(2,1)S(1)}, u32[]{:S(2)}) copy-start(bf16[512,512]{1,0:T(8,128)(2,1)S(1)} %collective-permute-done.6.refs_3_) | copy-start | bytes 1572868
  102.7 10.6 %collective-permute-start.10 = (bf16[512,512]{1,0:T(8,128)(2,1)S(1)}, bf16[512,512]{1,0:T(8,128)(2,1)S(1)}, u32[]{:S(2)}, u32[]{:S(2)}) collective-permute-start(bf16[512,512]{1,0:T(8,128)(2,1)S(1)} %collective-permute-done.6.refs_3_), channel_id=1, source_target_pairs={{0,1},{1,0},{2,3},{3,2},{4,5},{5,4},{6,7},{7,6},{8,9},{9,8},{10,11... | collective-permute-start | bytes 1572872 | tf_op jit(solution)/shard_map/ppermute | solution.py:186
  108.2 10.9 %copy-start.8 = (bf16[512,512]{1,0:T(8,128)(2,1)}, bf16[512,512]{1,0:T(8,128)(2,1)S(1)}, u32[]{:S(2)}) copy-start(bf16[512,512]{1,0:T(8,128)(2,1)S(1)} %collective-permute-done.5.refs_2_) | copy-start | bytes 1572868
  108.2 5.1 %collective-permute-start.9 = (bf16[512,512]{1,0:T(8,128)(2,1)S(1)}, bf16[512,512]{1,0:T(8,128)(2,1)S(1)}, u32[]{:S(2)}, u32[]{:S(2)}) collective-permute-start(bf16[512,512]{1,0:T(8,128)(2,1)S(1)} %collective-permute-done.5.refs_2_), channel_id=1, source_target_pairs={{0,1},{1,0},{2,3},{3,2},{4,5},{5,4},{6,7},{7,6},{8,9},{9,8},{10,11... | collective-permute-start | bytes 1572872 | tf_op jit(solution)/shard_map/ppermute | solution.py:186
  110.2 3.1 %copy-start.9 = (bf16[512,512]{1,0:T(8,128)(2,1)}, bf16[512,512]{1,0:T(8,128)(2,1)S(1)}, u32[]{:S(2)}) copy-start(bf16[512,512]{1,0:T(8,128)(2,1)S(1)} %collective-permute-done.4.refs_1_) | copy-start | bytes 1572868
  110.2 4.8 %collective-permute-start.8 = (bf16[512,512]{1,0:T(8,128)(2,1)S(1)}, bf16[512,512]{1,0:T(8,128)(2,1)}, u32[]{:S(2)}, u32[]{:S(2)}) collective-permute-start(bf16[512,512]{1,0:T(8,128)(2,1)S(1)} %collective-permute-done.4.refs_1_), channel_id=1, source_target_pairs={{0,1},{1,0},{2,3},{3,2},{4,5},{5,4},{6,7},{7,6},{8,9},{9,8},{10,11... | collective-permute-start | bytes 1572872 | tf_op jit(solution)/shard_map/ppermute | solution.py:186
  113.3 1.7 %copy-start.10 = (bf16[512,512]{1,0:T(8,128)(2,1)}, bf16[512,512]{1,0:T(8,128)(2,1)S(1)}, u32[]{:S(2)}) copy-start(bf16[512,512]{1,0:T(8,128)(2,1)S(1)} %collective-permute-done.7.refs_4_) | copy-start | bytes 1572868
  113.3 0.9 copy-start.11
  114.2 0.8 copy-start.12
Sparse Core Ops, SparseCore 0:
  35.3 83.8 all-gather.1

commit v4 on v3

--- a/solution.py
+++ b/solution.py
@@ -170,14 +170,14 @@
     return pl.pallas_call(
         project_kernel,
         out_shape=jax.ShapeDtypeStruct((rows, weight.shape[1]), jnp.bfloat16),
-        in_specs=[pl.BlockSpec(memory_space=pltpu.SMEM)] + [in_hbm()] * (groups + 1),
+        in_specs=[pl.BlockSpec(memory_space=pltpu.SMEM)] + [pl.BlockSpec(memory_space=pl.ANY)] * groups + [in_hbm()],
         out_specs=in_vmem(),
         scratch_shapes=[
             pltpu.VMEM((groups, *hidden[0].shape), hidden[0].dtype),
             pltpu.VMEM(weight.shape, weight.dtype),
             pltpu.SemaphoreType.DMA((2, groups)),
         ],
-        compiler_params=params(62),
+        compiler_params=params(51),
     )(order, *hidden, weight)
 
 
@@ -192,19 +192,20 @@
 
 
 def spread(array, axis):
-    return lax.all_to_all(jnp.concatenate([array] * lax.axis_size(axis), axis=0), axis, 0, 0, tiled=True)
-
-
-def turn(place):
-    row, core = place // 2, place % 2
-    return row * (1 - 2 * core) + 4 * core * (row == 0)
+    copies = jnp.broadcast_to(array, (lax.axis_size(axis), *array.shape))
+    return lax.all_to_all(copies, axis, 0, 0, tiled=True).reshape(-1, *array.shape[1:])
+
+
+TURN = ((4, 3), (-3, 2), (0, -1), (-2, 1))
 
 
 def to_columns(shard):
     pairs = []
     for z in range(16):
         for t in range(8):
-            pairs.append((z * 8 + t, (z + 2 * turn(t)) % 16 * 8 + z // 2))
+            goal = z // 2
+            far = TURN[(t // 2 - goal // 2) % 4][t % 2]
+            pairs.append((z * 8 + t, (z + 2 * far) % 16 * 8 + goal))
     return lax.ppermute(shard, ("zh", "zl", "y", "c"), pairs)
 
 
@@ -218,7 +219,10 @@
     weight = weight.reshape(tp, -1, out_weight.shape[0])
 
     total = group_total(pieces, blocks)
-    earlier = [from_earlier(total, "zh", by) for by in range(1, lax.axis_size("zh"))]
+    earlier = []
+    for group in range(lax.axis_size("zh") - 1):
+        passed = total + earlier[-1] if earlier else total
+        earlier.append(lax.ppermute(passed, "zh", [(group, group + 1)]))
     states = lax.all_to_all(prefix(pieces, earlier), GROUP, 0, 0, tiled=True)
     hidden = attend(queries, keys, values, states, norm_gain[None, :])
 
@@ -226,9 +230,9 @@
     held = [hidden] + [shift(hidden, "y", by) for by in steps[1:]]
     held = held + [shift(h, "c", 1) for h in held]
     row, core = lax.axis_index("y"), lax.axis_index("c")
-    place = (row - jnp.array(steps, jnp.int32)) % lax.axis_size("y") * 2
-    place = jnp.concatenate([place + core, place + 1 - core])
-    order = (row * 2 + core + turn(place)) % tp
+    far = jnp.array([TURN[-by % 4] for by in steps], jnp.int32)
+    far = jnp.where(core == 0, far, far[:, ::-1]).T.reshape(-1)
+    order = (row * 2 + core + far) % tp
     return project(order.astype(jnp.int32), held, weight)
 
 

time: 133 us -> 131 us (0.985)
  waiting for transfers between devices: 14.2 us -> 22.6 us
  starting transfers between devices: 47.6 us -> 42.2 us
  blocking collectives: 43.6 us -> 41.7 us
  local copies, waits for them, and re-layouts: 3.79 us -> 2.2 us
    ppermute x7, waiting for transfers between devices: 6.25 us -> 12 us  [shift(): lax.ppermute(array, axis, [(i, (i + by) % size) for i in range(size)])]
    ppermute x7, starting transfers between devices: 22.5 us -> 17.1 us  [shift(): lax.ppermute(array, axis, [(i, (i + by) % size) for i in range(size)])]
    all_gather x1, waiting for transfers between devices: 4.12 us -> 7.54 us  [shards(): weight = lax.all_gather(near, ('zh', 'zl'), axis=0, tiled=True)]
    unnamed x28 -> x18, local copies, waits for them, and re-layouts: 3.79 us -> 2.1 us
  transfers between devices with their start and end apart: 12 -> 12, of which waited for: 5 -> 6; matrix products, arithmetic and copies ran while one was open for 0% -> 0% of each run, Pallas kernels for 2% -> 2%
where the time goes in v4:
time: 131 us; the launch traced here: 130 us
  starting transfers between devices  42.2 us (32%)
  blocking collectives  41.7 us (32%)
  waiting for transfers between devices  22.6 us (17%)
  between operations  13.6 us (10%)
  Pallas kernels  8 us (6%)
  local copies, waits for them, and re-layouts  2.2 us (2%)
    all_to_all x1, blocking collectives, shards(): states = lax.all_to_all(prefix(pieces, earlier), GROUP, 0, 0, tiled=True)  17.5 us
    ppermute x7, starting transfers between devices, shift(): lax.ppermute(array, axis, [(i, (i + by) % size) for i in range(size)])  17.1 us
    all_to_all x1, blocking collectives, shards(): pieces = lax.all_to_all(state, GROUP, 0, 0, tiled=True)  13.3 us
    ppermute x3, starting transfers between devices, shards(): earlier.append(lax.ppermute(passed, 'zh', [(group, group + 1)]))  12.6 us
    ppermute x1, starting transfers between devices, to_columns(): return lax.ppermute(shard, ('zh', 'zl', 'y', 'c'), pairs)  12.5 us
    ppermute x7, waiting for transfers between devices, shift(): lax.ppermute(array, axis, [(i, (i + by) % size) for i in range(size)])  12 us
    all_to_all x1, blocking collectives, spread(): lax.all_to_all(copies, axis, 0, 0, tiled=True).reshape(-1, *array.shape[1:])  10.9 us
    all_gather x1, waiting for transfers between devices, shards(): weight = lax.all_gather(near, ('zh', 'zl'), axis=0, tiled=True)  7.54 us
  transfers between devices with their start and end apart: 12, of which 6 were waited for; matrix products, arithmetic and copies ran while one was open for 0% of the time, Pallas kernels for 2%

profile of v4, /device:TPU:24, one launch (start us, length us, event | category | flops | bytes accessed | tf_op | source)
XLA Modules:
  0.0 130.4 jit_solution(10062537595425586153)
XLA Ops:
  6.5 12.5 %collective-permute-start = (bf16[64,512]{1,0:T(8,128)(2,1)}, bf16[64,512]{1,0:T(8,128)(2,1)S(1)}, u32[]{:S(2)}, u32[]{:S(2)}) collective-permute-start(bf16[64,512]{1,0:T(8,128)(2,1)} %bitcast.18), channel_id=1, source_target_pairs={{0,256},{1,192},{2,320},{3,128},{4,0},{5,448},{6,384},{7,64},{32,2... | collective-permute-start | bytes 196616 | tf_op jit(solution)/shard_map/ppermute | solution.py:209
  19.1 1.0 copy-done
  20.1 1.0 copy-done.2
  21.2 0.5 shard_map.64
  21.6 1.6 %collective-permute-done = bf16[64,512]{1,0:T(8,128)(2,1)S(1)} collective-permute-done((bf16[64,512]{1,0:T(8,128)(2,1)}, bf16[64,512]{1,0:T(8,128)(2,1)S(1)}, u32[]{:S(2)}, u32[]{:S(2)}) %collective-permute-start) | collective-permute-done | bytes 65568 | tf_op jit(solution)/shard_map/ppermute | solution.py:209
  23.3 10.9 %all_to_all.27 = bf16[4,64,512]{2,1,0:T(8,128)(2,1)} all-to-all(bf16[4,64,512]{2,1,0:T(8,128)(2,1)S(1)} %broadcast_in_dim.7), channel_id=1, replica_groups=mesh['zh'=4,'zl'=4,'x'=4,'y'=4,'c'=2] {'x'}, dimensions={0} | all-to-all | bytes 524288 | tf_op jit(solution)/shard_map/all_to_all | solution.py:196
  34.2 0.0 all-gather.2.cloned.1.call-update
  34.2 13.3 %all_to_all.28 = f32[16,32,128]{2,1,0:T(8,128)S(1)} all-to-all(f32[16,32,128]{2,1,0:T(8,128)S(1)} %bitcast.12), channel_id=1, replica_groups=mesh['zh'=4,'zl'=4,'x'=4,'y'=4,'c'=2] {'zl','x'}, dimensions={0} | all-to-all | bytes 524288 | tf_op jit(solution)/shard_map/all_to_all | solution.py:217
  47.5 11.3 %collective-permute-start.1 = (f32[32,128]{1,0:T(8,128)S(1)}, f32[32,128]{1,0:T(8,128)S(1)}, u32[]{:S(2)}, u32[]{:S(2)}) collective-permute-start(f32[32,128]{1,0:T(8,128)S(1)} %shard_map.65), channel_id=1, source_target_pairs={{0,128},{1,129},{2,130},{3,131},{4,132},{5,133},{6,134},{7,135},{8... | collective-permute-start | bytes 49160 | tf_op jit(solution)/shard_map/ppermute | solution.py:225
  58.8 1.4 %collective-permute-done.1.refs_0_ = f32[32,128]{1,0:T(8,128)S(1)} collective-permute-done((f32[32,128]{1,0:T(8,128)S(1)}, f32[32,128]{1,0:T(8,128)S(1)}, u32[]{:S(2)}, u32[]{:S(2)}) %collective-permute-start.1) | collective-permute-done | bytes 16416 | tf_op jit(solution)/shard_map/ppermute | solution.py:225
  60.2 0.7 collective-permute-start.2
  60.9 0.0 collective-permute-done.2.refs_1_
  60.9 0.7 collective-permute-start.3
  61.6 0.0 collective-permute-done.3.refs_2_
  61.6 17.5 %all_to_all.29 = f32[16,32,128]{2,1,0:T(8,128)S(1)} all-to-all(f32[16,32,128]{2,1,0:T(8,128)S(1)} %bitcast.13), channel_id=1, replica_groups=mesh['zh'=4,'zl'=4,'x'=4,'y'=4,'c'=2] {'zl','x'}, dimensions={0} | all-to-all | bytes 524288 | tf_op jit(solution)/shard_map/all_to_all | solution.py:226
  79.2 1.9 %shard_map.67.refs_0_ = bf16[512,512]{1,0:T(8,128)(2,1)S(1)} custom-call(bf16[512,512]{1,0:T(8,128)(2,1)S(1)} %copy-done.4, bf16[512,512]{1,0:T(8,128)(2,1)S(1)} %copy-done.1, bf16[512,512]{1,0:T(8,128)(2,1)S(1)} %copy-done.3, f32[512,128]{1,0:T(8,128)S(1)} %bitcast.14, f32[1,512]{1,0:T(1,128)S(1)} %bitcast.15), custom_call_target="tpu_custom_call" | custom-call | tf_op jit(solution)/shard_map/pallas_call | solution.py:130
  81.1 1.9 %collective-permute-start.6 = (bf16[512,512]{1,0:T(8,128)(2,1)S(1)}, bf16[512,512]{1,0:T(8,128)(2,1)S(1)}, u32[]{:S(2)}, u32[]{:S(2)}) collective-permute-start(bf16[512,512]{1,0:T(8,128)(2,1)S(1)} %shard_map.67.refs_0_), channel_id=1, source_target_pairs={{0,4},{2,6},{4,0},{6,2},{1,5},{3,7},{5,1},{7,3},{8,12},{10,14},{12... | collective-permute-start | bytes 1572872 | tf_op jit(solution)/shard_map/ppermute | solution.py:186
  83.0 1.9 %collective-permute-start.5 = (bf16[512,512]{1,0:T(8,128)(2,1)S(1)}, bf16[512,512]{1,0:T(8,128)(2,1)S(1)}, u32[]{:S(2)}, u32[]{:S(2)}) collective-permute-start(bf16[512,512]{1,0:T(8,128)(2,1)S(1)} %shard_map.67.refs_0_), channel_id=1, source_target_pairs={{0,6},{2,0},{4,2},{6,4},{1,7},{3,1},{5,3},{7,5},{8,14},{10,8},{12,... | collective-permute-start | bytes 1572872 | tf_op jit(solution)/shard_map/ppermute | solution.py:186
  85.0 5.1 %collective-permute-start.4 = (bf16[512,512]{1,0:T(8,128)(2,1)S(1)}, bf16[512,512]{1,0:T(8,128)(2,1)S(1)}, u32[]{:S(2)}, u32[]{:S(2)}) collective-permute-start(bf16[512,512]{1,0:T(8,128)(2,1)S(1)} %shard_map.67.refs_0_), channel_id=1, source_target_pairs={{0,2},{2,4},{4,6},{6,0},{1,3},{3,5},{5,7},{7,1},{8,10},{10,12},{12... | collective-permute-start | bytes 1572872 | tf_op jit(solution)/shard_map/ppermute | solution.py:186
  90.1 1.9 %collective-permute-start.7 = (bf16[512,512]{1,0:T(8,128)(2,1)S(1)}, bf16[512,512]{1,0:T(8,128)(2,1)S(1)}, u32[]{:S(2)}, u32[]{:S(2)}) collective-permute-start(bf16[512,512]{1,0:T(8,128)(2,1)S(1)} %shard_map.67.refs_0_), channel_id=1, source_target_pairs={{0,1},{1,0},{2,3},{3,2},{4,5},{5,4},{6,7},{7,6},{8,9},{9,8},{10,11... | collective-permute-start | bytes 1572872 | tf_op jit(solution)/shard_map/ppermute | solution.py:186
  92.0 6.9 %collective-permute-done.6.refs_3_ = bf16[512,512]{1,0:T(8,128)(2,1)S(1)} collective-permute-done((bf16[512,512]{1,0:T(8,128)(2,1)S(1)}, bf16[512,512]{1,0:T(8,128)(2,1)S(1)}, u32[]{:S(2)}, u32[]{:S(2)}) %collective-permute-start.6) | collective-permute-done | bytes 524320 | tf_op jit(solution)/shard_map/ppermute | solution.py:186
  98.9 1.9 %collective-permute-start.10 = (bf16[512,512]{1,0:T(8,128)(2,1)S(1)}, bf16[512,512]{1,0:T(8,128)(2,1)S(1)}, u32[]{:S(2)}, u32[]{:S(2)}) collective-permute-start(bf16[512,512]{1,0:T(8,128)(2,1)S(1)} %collective-permute-done.6.refs_3_), channel_id=1, source_target_pairs={{0,1},{1,0},{2,3},{3,2},{4,5},{5,4},{6,7},{7,6},{8,9},{9,8},{10,11... | collective-permute-start | bytes 1572872 | tf_op jit(solution)/shard_map/ppermute | solution.py:186
  100.8 3.6 %collective-permute-done.5.refs_2_ = bf16[512,512]{1,0:T(8,128)(2,1)S(1)} collective-permute-done((bf16[512,512]{1,0:T(8,128)(2,1)S(1)}, bf16[512,512]{1,0:T(8,128)(2,1)S(1)}, u32[]{:S(2)}, u32[]{:S(2)}) %collective-permute-start.5) | collective-permute-done | bytes 524320 | tf_op jit(solution)/shard_map/ppermute | solution.py:186
  104.4 1.9 %collective-permute-start.9 = (bf16[512,512]{1,0:T(8,128)(2,1)S(1)}, bf16[512,512]{1,0:T(8,128)(2,1)}, u32[]{:S(2)}, u32[]{:S(2)}) collective-permute-start(bf16[512,512]{1,0:T(8,128)(2,1)S(1)} %collective-permute-done.5.refs_2_), channel_id=1, source_target_pairs={{0,1},{1,0},{2,3},{3,2},{4,5},{5,4},{6,7},{7,6},{8,9},{9,8},{10,11... | collective-permute-start | bytes 1572872 | tf_op jit(solution)/shard_map/ppermute | solution.py:186
  106.3 0.0 collective-permute-done.4.refs_1_
  106.3 2.4 %collective-permute-start.8 = (bf16[512,512]{1,0:T(8,128)(2,1)S(1)}, bf16[512,512]{1,0:T(8,128)(2,1)}, u32[]{:S(2)}, u32[]{:S(2)}) collective-permute-start(bf16[512,512]{1,0:T(8,128)(2,1)S(1)} %collective-permute-done.4.refs_1_), channel_id=1, source_target_pairs={{0,1},{1,0},{2,3},{3,2},{4,5},{5,4},{6,7},{7,6},{8,9},{9,8},{10,11... | collective-permute-start | bytes 1572872 | tf_op jit(solution)/shard_map/ppermute | solution.py:186
  108.8 0.1 add.31
  108.9 0.0 collective-permute-done.7.refs_4_
  108.9 0.0 collective-permute-done.10.refs_7_
  108.9 1.5 %collective-permute-done.8.refs_5_ = bf16[512,512]{1,0:T(8,128)(2,1)} collective-permute-done((bf16[512,512]{1,0:T(8,128)(2,1)S(1)}, bf16[512,512]{1,0:T(8,128)(2,1)}, u32[]{:S(2)}, u32[]{:S(2)}) %collective-permute-start.8) | collective-permute-done | bytes 524320 | tf_op jit(solution)/shard_map/ppermute | solution.py:186
  110.4 7.5 %all-gather.2.cloned.1.call-done = bf16[4096,512]{1,0:T(8,128)(2,1)} async-done(((bf16[256,512]{1,0:T(8,128)(2,1)}), bf16[4096,512]{1,0:T(8,128)(2,1)}) %all-gather.2.cloned.1.call-update) | async-done | bytes 4194320 | tf_op jit(solution)/shard_map/all_gather | solution.py:218
  117.9 5.5 %shard_map.68 = bf16[512,512]{1,0:T(8,128)(2,1)} custom-call(s32[8]{0:T(128)S(1)} %and_select_fusion.order_ref, bf16[512,512]{1,0:T(8,128)(2,1)S(1)} %shard_map.67.refs_0_, bf16[512,512]{1,0:T(8,128)(2,1)S(1)} %collective-permute-done.4.refs_1_, bf16[512,512]{1,0:T(8,128)(2,1)S(1)} %collective-permute-done.5.refs_2_, ...), custom_call_target="tpu_custom_call" | custom-call | tf_op jit(solution)/shard_map/pallas_call | solution.py:170
  (25 shorter events, 0.1 us)
Async XLA Ops:
  6.5 102.2 %copy-start.7 = (s32[4,2]{0,1:T(2,128)S(1)}, s32[4,2]{0,1:T(2,128)}, u32[]{:S(2)}) copy-start(s32[4,2]{0,1:T(2,128)} %constant.29) | copy-start | bytes 100
  6.5 102.2 %copy-start.8 = (s32[4,2]{0,1:T(2,128)S(1)}, s32[4,2]{0,1:T(2,128)}, u32[]{:S(2)}) copy-start(s32[4,2]{0,1:T(2,128)} %constant.28.clone) | copy-start | bytes 100
  6.5 111.4 %all-gather.2.cloned.1.call-start = ((), (), s32[]{:S(2)}) async-start(), calls=%async_computation.3 | async-start | bytes 4456448 | tf_op jit(solution)/shard_map/all_gather | solution.py:218
  6.5 16.7 %collective-permute-start = (bf16[64,512]{1,0:T(8,128)(2,1)}, bf16[64,512]{1,0:T(8,128)(2,1)S(1)}, u32[]{:S(2)}, u32[]{:S(2)}) collective-permute-start(bf16[64,512]{1,0:T(8,128)(2,1)} %bitcast.18), channel_id=1, source_target_pairs={{0,256},{1,192},{2,320},{3,128},{4,0},{5,448},{6,384},{7,64},{32,2... | collective-permute-start | bytes 196616 | tf_op jit(solution)/shard_map/ppermute | solution.py:209
  19.1 1.0 copy-start
  20.1 1.0 copy-start.2
  21.1 58.0 %copy-start.1 = (bf16[512,512]{1,0:T(8,128)(2,1)S(1)}, bf16[512,512]{1,0:T(8,128)(2,1)}, u32[]{:S(2)}) copy-start(bf16[512,512]{1,0:T(8,128)(2,1)} %k_hbm.3) | copy-start | bytes 1572868
  21.1 58.0 %copy-start.3 = (bf16[512,512]{1,0:T(8,128)(2,1)S(1)}, bf16[512,512]{1,0:T(8,128)(2,1)}, u32[]{:S(2)}) copy-start(bf16[512,512]{1,0:T(8,128)(2,1)} %v_hbm.3) | copy-start | bytes 1572868
  21.2 58.0 %copy-start.4 = (bf16[512,512]{1,0:T(8,128)(2,1)S(1)}, bf16[512,512]{1,0:T(8,128)(2,1)}, u32[]{:S(2)}) copy-start(bf16[512,512]{1,0:T(8,128)(2,1)} %q_hbm.1) | copy-start | bytes 1572868
  21.2 58.0 %copy-start.5 = (f32[512]{0:T(512)S(1)}, f32[512]{0:T(512)}, u32[]{:S(2)}) copy-start(f32[512]{0:T(512)} %param.9) | copy-start | bytes 6148
  47.5 12.7 %collective-permute-start.1 = (f32[32,128]{1,0:T(8,128)S(1)}, f32[32,128]{1,0:T(8,128)S(1)}, u32[]{:S(2)}, u32[]{:S(2)}) collective-permute-start(f32[32,128]{1,0:T(8,128)S(1)} %shard_map.65), channel_id=1, source_target_pairs={{0,128},{1,129},{2,130},{3,131},{4,132},{5,133},{6,134},{7,135},{8... | collective-permute-start | bytes 49160 | tf_op jit(solution)/shard_map/ppermute | solution.py:225
  60.2 0.7 collective-permute-start.2
  60.9 0.7 collective-permute-start.3
  81.1 17.8 %collective-permute-start.6 = (bf16[512,512]{1,0:T(8,128)(2,1)S(1)}, bf16[512,512]{1,0:T(8,128)(2,1)S(1)}, u32[]{:S(2)}, u32[]{:S(2)}) collective-permute-start(bf16[512,512]{1,0:T(8,128)(2,1)S(1)} %shard_map.67.refs_0_), channel_id=1, source_target_pairs={{0,4},{2,6},{4,0},{6,2},{1,5},{3,7},{5,1},{7,3},{8,12},{10,14},{12... | collective-permute-start | bytes 1572872 | tf_op jit(solution)/shard_map/ppermute | solution.py:186
  83.0 21.4 %collective-permute-start.5 = (bf16[512,512]{1,0:T(8,128)(2,1)S(1)}, bf16[512,512]{1,0:T(8,128)(2,1)S(1)}, u32[]{:S(2)}, u32[]{:S(2)}) collective-permute-start(bf16[512,512]{1,0:T(8,128)(2,1)S(1)} %shard_map.67.refs_0_), channel_id=1, source_target_pairs={{0,6},{2,0},{4,2},{6,4},{1,7},{3,1},{5,3},{7,5},{8,14},{10,8},{12,... | collective-permute-start | bytes 1572872 | tf_op jit(solution)/shard_map/ppermute | solution.py:186
  85.0 21.4 %collective-permute-start.4 = (bf16[512,512]{1,0:T(8,128)(2,1)S(1)}, bf16[512,512]{1,0:T(8,128)(2,1)S(1)}, u32[]{:S(2)}, u32[]{:S(2)}) collective-permute-start(bf16[512,512]{1,0:T(8,128)(2,1)S(1)} %shard_map.67.refs_0_), channel_id=1, source_target_pairs={{0,2},{2,4},{4,6},{6,0},{1,3},{3,5},{5,7},{7,1},{8,10},{10,12},{12... | collective-permute-start | bytes 1572872 | tf_op jit(solution)/shard_map/ppermute | solution.py:186
  90.1 18.8 %collective-permute-start.7 = (bf16[512,512]{1,0:T(8,128)(2,1)S(1)}, bf16[512,512]{1,0:T(8,128)(2,1)S(1)}, u32[]{:S(2)}, u32[]{:S(2)}) collective-permute-start(bf16[512,512]{1,0:T(8,128)(2,1)S(1)} %shard_map.67.refs_0_), channel_id=1, source_target_pairs={{0,1},{1,0},{2,3},{3,2},{4,5},{5,4},{6,7},{7,6},{8,9},{9,8},{10,11... | collective-permute-start | bytes 1572872 | tf_op jit(solution)/shard_map/ppermute | solution.py:186
  98.9 10.0 %collective-permute-start.10 = (bf16[512,512]{1,0:T(8,128)(2,1)S(1)}, bf16[512,512]{1,0:T(8,128)(2,1)S(1)}, u32[]{:S(2)}, u32[]{:S(2)}) collective-permute-start(bf16[512,512]{1,0:T(8,128)(2,1)S(1)} %collective-permute-done.6.refs_3_), channel_id=1, source_target_pairs={{0,1},{1,0},{2,3},{3,2},{4,5},{5,4},{6,7},{7,6},{8,9},{9,8},{10,11... | collective-permute-start | bytes 1572872 | tf_op jit(solution)/shard_map/ppermute | solution.py:186
  104.4 4.5 %collective-permute-start.9 = (bf16[512,512]{1,0:T(8,128)(2,1)S(1)}, bf16[512,512]{1,0:T(8,128)(2,1)}, u32[]{:S(2)}, u32[]{:S(2)}) collective-permute-start(bf16[512,512]{1,0:T(8,128)(2,1)S(1)} %collective-permute-done.5.refs_2_), channel_id=1, source_target_pairs={{0,1},{1,0},{2,3},{3,2},{4,5},{5,4},{6,7},{7,6},{8,9},{9,8},{10,11... | collective-permute-start | bytes 1572872 | tf_op jit(solution)/shard_map/ppermute | solution.py:186
  106.3 4.1 %collective-permute-start.8 = (bf16[512,512]{1,0:T(8,128)(2,1)S(1)}, bf16[512,512]{1,0:T(8,128)(2,1)}, u32[]{:S(2)}, u32[]{:S(2)}) collective-permute-start(bf16[512,512]{1,0:T(8,128)(2,1)S(1)} %collective-permute-done.4.refs_1_), channel_id=1, source_target_pairs={{0,1},{1,0},{2,3},{3,2},{4,5},{5,4},{6,7},{7,6},{8,9},{9,8},{10,11... | collective-permute-start | bytes 1572872 | tf_op jit(solution)/shard_map/ppermute | solution.py:186
  108.9 9.0 %copy-start.6 = (bf16[512,512]{1,0:T(8,128)(2,1)}, bf16[512,512]{1,0:T(8,128)(2,1)S(1)}, u32[]{:S(2)}) copy-start(bf16[512,512]{1,0:T(8,128)(2,1)S(1)} %collective-permute-done.10.refs_7_) | copy-start | bytes 1572868
Sparse Core Ops, SparseCore 0:
  34.3 83.5 all-gather.1

commit v5 on v4

--- a/solution.py
+++ b/solution.py
@@ -196,7 +196,7 @@
     return lax.all_to_all(copies, axis, 0, 0, tiled=True).reshape(-1, *array.shape[1:])
 
 
-TURN = ((4, 3), (-3, 2), (0, -1), (-2, 1))
+TURN = ((4, -3), (3, -2), (0, 1), (2, -1))
 
 
 def to_columns(shard):

time: 131 us -> 130 us (level)
  starting transfers between devices: 42.2 us -> 36.8 us
  waiting for transfers between devices: 22.6 us -> 25.2 us
  blocking collectives: 41.7 us -> 43.4 us
    ppermute x1, starting transfers between devices: 12.5 us -> 8.88 us  [to_columns(): return lax.ppermute(shard, ('zh', 'zl', 'y', 'c'), pairs)]
    ppermute x1, waiting for transfers between devices: 1.65 us -> 4.32 us  [to_columns(): return lax.ppermute(shard, ('zh', 'zl', 'y', 'c'), pairs)]
    all_to_all x1, blocking collectives: 13.3 us -> 15.5 us  [shards(): pieces = lax.all_to_all(state, GROUP, 0, 0, tiled=True)]
    ppermute x3, starting transfers between devices: 12.6 us -> 10.8 us  [shards(): earlier.append(lax.ppermute(passed, 'zh', [(group, group + 1)]))]
where the time goes in v5:
time: 130 us; the launch traced here: 129 us
  blocking collectives  43.4 us (33%)
  starting transfers between devices  36.8 us (28%)
  waiting for transfers between devices  25.2 us (19%)
  between operations  13.6 us (10%)
  Pallas kernels  8 us (6%)
  local copies, waits for them, and re-layouts  2.2 us (2%)
    ppermute x7, starting transfers between devices, shift(): lax.ppermute(array, axis, [(i, (i + by) % size) for i in range(size)])  17.1 us
    all_to_all x1, blocking collectives, shards(): states = lax.all_to_all(prefix(pieces, earlier), GROUP, 0, 0, tiled=True)  17.1 us
    all_to_all x1, blocking collectives, shards(): pieces = lax.all_to_all(state, GROUP, 0, 0, tiled=True)  15.5 us
    ppermute x7, waiting for transfers between devices, shift(): lax.ppermute(array, axis, [(i, (i + by) % size) for i in range(size)])  11.6 us
    all_to_all x1, blocking collectives, spread(): lax.all_to_all(copies, axis, 0, 0, tiled=True).reshape(-1, *array.shape[1:])  10.9 us
    ppermute x3, starting transfers between devices, shards(): earlier.append(lax.ppermute(passed, 'zh', [(group, group + 1)]))  10.8 us
    ppermute x1, starting transfers between devices, to_columns(): return lax.ppermute(shard, ('zh', 'zl', 'y', 'c'), pairs)  8.88 us
    all_gather x1, waiting for transfers between devices, shards(): weight = lax.all_gather(near, ('zh', 'zl'), axis=0, tiled=True)  7.8 us
  transfers between devices with their start and end apart: 12, of which 6 were waited for; matrix products, arithmetic and copies ran while one was open for 0% of the time, Pallas kernels for 2%

profile of v5, /device:TPU:24, one launch (start us, length us, event | category | flops | bytes accessed | tf_op | source)
XLA Modules:
  0.0 129.3 jit_solution(10550418073914221401)
XLA Ops:
  6.5 8.9 %collective-permute-start = (bf16[64,512]{1,0:T(8,128)(2,1)}, bf16[64,512]{1,0:T(8,128)(2,1)S(1)}, u32[]{:S(2)}, u32[]{:S(2)}) collective-permute-start(bf16[64,512]{1,0:T(8,128)(2,1)} %bitcast.18), channel_id=1, source_target_pairs={{0,256},{1,320},{2,192},{3,384},{4,0},{5,64},{6,128},{7,448},{32,2... | collective-permute-start | bytes 196616 | tf_op jit(solution)/shard_map/ppermute | solution.py:209
  15.4 1.0 copy-done
  16.5 1.0 copy-done.2
  17.5 0.5 shard_map.64
  18.0 4.3 %collective-permute-done = bf16[64,512]{1,0:T(8,128)(2,1)S(1)} collective-permute-done((bf16[64,512]{1,0:T(8,128)(2,1)}, bf16[64,512]{1,0:T(8,128)(2,1)S(1)}, u32[]{:S(2)}, u32[]{:S(2)}) %collective-permute-start) | collective-permute-done | bytes 65568 | tf_op jit(solution)/shard_map/ppermute | solution.py:209
  22.3 10.9 %all_to_all.27 = bf16[4,64,512]{2,1,0:T(8,128)(2,1)} all-to-all(bf16[4,64,512]{2,1,0:T(8,128)(2,1)S(1)} %broadcast_in_dim.7), channel_id=1, replica_groups=mesh['zh'=4,'zl'=4,'x'=4,'y'=4,'c'=2] {'x'}, dimensions={0} | all-to-all | bytes 524288 | tf_op jit(solution)/shard_map/all_to_all | solution.py:196
  33.2 0.0 all-gather.2.cloned.1.call-update
  33.2 15.5 %all_to_all.28 = f32[16,32,128]{2,1,0:T(8,128)S(1)} all-to-all(f32[16,32,128]{2,1,0:T(8,128)S(1)} %bitcast.12), channel_id=1, replica_groups=mesh['zh'=4,'zl'=4,'x'=4,'y'=4,'c'=2] {'zl','x'}, dimensions={0} | all-to-all | bytes 524288 | tf_op jit(solution)/shard_map/all_to_all | solution.py:217
  48.8 9.5 %collective-permute-start.1 = (f32[32,128]{1,0:T(8,128)S(1)}, f32[32,128]{1,0:T(8,128)S(1)}, u32[]{:S(2)}, u32[]{:S(2)}) collective-permute-start(f32[32,128]{1,0:T(8,128)S(1)} %shard_map.65), channel_id=1, source_target_pairs={{0,128},{1,129},{2,130},{3,131},{4,132},{5,133},{6,134},{7,135},{8... | collective-permute-start | bytes 49160 | tf_op jit(solution)/shard_map/ppermute | solution.py:225
  58.3 1.4 %collective-permute-done.1.refs_0_ = f32[32,128]{1,0:T(8,128)S(1)} collective-permute-done((f32[32,128]{1,0:T(8,128)S(1)}, f32[32,128]{1,0:T(8,128)S(1)}, u32[]{:S(2)}, u32[]{:S(2)}) %collective-permute-start.1) | collective-permute-done | bytes 16416 | tf_op jit(solution)/shard_map/ppermute | solution.py:225
  59.7 0.7 collective-permute-start.2
  60.4 0.0 collective-permute-done.2.refs_1_
  60.4 0.7 collective-permute-start.3
  61.1 0.0 collective-permute-done.3.refs_2_
  61.1 17.1 %all_to_all.29 = f32[16,32,128]{2,1,0:T(8,128)S(1)} all-to-all(f32[16,32,128]{2,1,0:T(8,128)S(1)} %bitcast.13), channel_id=1, replica_groups=mesh['zh'=4,'zl'=4,'x'=4,'y'=4,'c'=2] {'zl','x'}, dimensions={0} | all-to-all | bytes 524288 | tf_op jit(solution)/shard_map/all_to_all | solution.py:226
  78.2 1.9 %shard_map.67.refs_0_ = bf16[512,512]{1,0:T(8,128)(2,1)S(1)} custom-call(bf16[512,512]{1,0:T(8,128)(2,1)S(1)} %copy-done.4, bf16[512,512]{1,0:T(8,128)(2,1)S(1)} %copy-done.1, bf16[512,512]{1,0:T(8,128)(2,1)S(1)} %copy-done.3, f32[512,128]{1,0:T(8,128)S(1)} %bitcast.14, f32[1,512]{1,0:T(1,128)S(1)} %bitcast.15), custom_call_target="tpu_custom_call" | custom-call | tf_op jit(solution)/shard_map/pallas_call | solution.py:130
  80.2 1.9 %collective-permute-start.6 = (bf16[512,512]{1,0:T(8,128)(2,1)S(1)}, bf16[512,512]{1,0:T(8,128)(2,1)S(1)}, u32[]{:S(2)}, u32[]{:S(2)}) collective-permute-start(bf16[512,512]{1,0:T(8,128)(2,1)S(1)} %shard_map.67.refs_0_), channel_id=1, source_target_pairs={{0,4},{2,6},{4,0},{6,2},{1,5},{3,7},{5,1},{7,3},{8,12},{10,14},{12... | collective-permute-start | bytes 1572872 | tf_op jit(solution)/shard_map/ppermute | solution.py:186
  82.1 1.9 %collective-permute-start.5 = (bf16[512,512]{1,0:T(8,128)(2,1)S(1)}, bf16[512,512]{1,0:T(8,128)(2,1)S(1)}, u32[]{:S(2)}, u32[]{:S(2)}) collective-permute-start(bf16[512,512]{1,0:T(8,128)(2,1)S(1)} %shard_map.67.refs_0_), channel_id=1, source_target_pairs={{0,6},{2,0},{4,2},{6,4},{1,7},{3,1},{5,3},{7,5},{8,14},{10,8},{12,... | collective-permute-start | bytes 1572872 | tf_op jit(solution)/shard_map/ppermute | solution.py:186
  84.0 5.1 %collective-permute-start.4 = (bf16[512,512]{1,0:T(8,128)(2,1)S(1)}, bf16[512,512]{1,0:T(8,128)(2,1)S(1)}, u32[]{:S(2)}, u32[]{:S(2)}) collective-permute-start(bf16[512,512]{1,0:T(8,128)(2,1)S(1)} %shard_map.67.refs_0_), channel_id=1, source_target_pairs={{0,2},{2,4},{4,6},{6,0},{1,3},{3,5},{5,7},{7,1},{8,10},{10,12},{12... | collective-permute-start | bytes 1572872 | tf_op jit(solution)/shard_map/ppermute | solution.py:186
  89.2 1.9 %collective-permute-start.7 = (bf16[512,512]{1,0:T(8,128)(2,1)S(1)}, bf16[512,512]{1,0:T(8,128)(2,1)S(1)}, u32[]{:S(2)}, u32[]{:S(2)}) collective-permute-start(bf16[512,512]{1,0:T(8,128)(2,1)S(1)} %shard_map.67.refs_0_), channel_id=1, source_target_pairs={{0,1},{1,0},{2,3},{3,2},{4,5},{5,4},{6,7},{7,6},{8,9},{9,8},{10,11... | collective-permute-start | bytes 1572872 | tf_op jit(solution)/shard_map/ppermute | solution.py:186
  91.1 6.5 %collective-permute-done.6.refs_3_ = bf16[512,512]{1,0:T(8,128)(2,1)S(1)} collective-permute-done((bf16[512,512]{1,0:T(8,128)(2,1)S(1)}, bf16[512,512]{1,0:T(8,128)(2,1)S(1)}, u32[]{:S(2)}, u32[]{:S(2)}) %collective-permute-start.6) | collective-permute-done | bytes 524320 | tf_op jit(solution)/shard_map/ppermute | solution.py:186
  97.6 1.9 %collective-permute-start.10 = (bf16[512,512]{1,0:T(8,128)(2,1)S(1)}, bf16[512,512]{1,0:T(8,128)(2,1)S(1)}, u32[]{:S(2)}, u32[]{:S(2)}) collective-permute-start(bf16[512,512]{1,0:T(8,128)(2,1)S(1)} %collective-permute-done.6.refs_3_), channel_id=1, source_target_pairs={{0,1},{1,0},{2,3},{3,2},{4,5},{5,4},{6,7},{7,6},{8,9},{9,8},{10,11... | collective-permute-start | bytes 1572872 | tf_op jit(solution)/shard_map/ppermute | solution.py:186
  99.5 3.6 %collective-permute-done.5.refs_2_ = bf16[512,512]{1,0:T(8,128)(2,1)S(1)} collective-permute-done((bf16[512,512]{1,0:T(8,128)(2,1)S(1)}, bf16[512,512]{1,0:T(8,128)(2,1)S(1)}, u32[]{:S(2)}, u32[]{:S(2)}) %collective-permute-start.5) | collective-permute-done | bytes 524320 | tf_op jit(solution)/shard_map/ppermute | solution.py:186
  103.1 1.9 %collective-permute-start.9 = (bf16[512,512]{1,0:T(8,128)(2,1)S(1)}, bf16[512,512]{1,0:T(8,128)(2,1)}, u32[]{:S(2)}, u32[]{:S(2)}) collective-permute-start(bf16[512,512]{1,0:T(8,128)(2,1)S(1)} %collective-permute-done.5.refs_2_), channel_id=1, source_target_pairs={{0,1},{1,0},{2,3},{3,2},{4,5},{5,4},{6,7},{7,6},{8,9},{9,8},{10,11... | collective-permute-start | bytes 1572872 | tf_op jit(solution)/shard_map/ppermute | solution.py:186
  105.1 0.0 collective-permute-done.4.refs_1_
  105.1 2.4 %collective-permute-start.8 = (bf16[512,512]{1,0:T(8,128)(2,1)S(1)}, bf16[512,512]{1,0:T(8,128)(2,1)}, u32[]{:S(2)}, u32[]{:S(2)}) collective-permute-start(bf16[512,512]{1,0:T(8,128)(2,1)S(1)} %collective-permute-done.4.refs_1_), channel_id=1, source_target_pairs={{0,1},{1,0},{2,3},{3,2},{4,5},{5,4},{6,7},{7,6},{8,9},{9,8},{10,11... | collective-permute-start | bytes 1572872 | tf_op jit(solution)/shard_map/ppermute | solution.py:186
  107.5 0.1 add.31
  107.6 0.0 collective-permute-done.7.refs_4_
  107.6 0.0 collective-permute-done.9.refs_6_
  107.7 1.5 %collective-permute-done.8.refs_5_ = bf16[512,512]{1,0:T(8,128)(2,1)} collective-permute-done((bf16[512,512]{1,0:T(8,128)(2,1)S(1)}, bf16[512,512]{1,0:T(8,128)(2,1)}, u32[]{:S(2)}, u32[]{:S(2)}) %collective-permute-start.8) | collective-permute-done | bytes 524320 | tf_op jit(solution)/shard_map/ppermute | solution.py:186
  109.1 7.8 %all-gather.2.cloned.1.call-done = bf16[4096,512]{1,0:T(8,128)(2,1)} async-done(((bf16[256,512]{1,0:T(8,128)(2,1)}), bf16[4096,512]{1,0:T(8,128)(2,1)}) %all-gather.2.cloned.1.call-update) | async-done | bytes 4194320 | tf_op jit(solution)/shard_map/all_gather | solution.py:218
  116.9 5.5 %shard_map.68 = bf16[512,512]{1,0:T(8,128)(2,1)} custom-call(s32[8]{0:T(128)S(1)} %and_select_fusion.order_ref, bf16[512,512]{1,0:T(8,128)(2,1)S(1)} %shard_map.67.refs_0_, bf16[512,512]{1,0:T(8,128)(2,1)S(1)} %collective-permute-done.4.refs_1_, bf16[512,512]{1,0:T(8,128)(2,1)S(1)} %collective-permute-done.5.refs_2_, ...), custom_call_target="tpu_custom_call" | custom-call | tf_op jit(solution)/shard_map/pallas_call | solution.py:170
  (25 shorter events, 0.1 us)
Async XLA Ops:
  6.5 101.0 %copy-start.7 = (s32[4,2]{0,1:T(2,128)S(1)}, s32[4,2]{0,1:T(2,128)}, u32[]{:S(2)}) copy-start(s32[4,2]{0,1:T(2,128)} %constant.29) | copy-start | bytes 100
  6.5 101.0 %copy-start.8 = (s32[4,2]{0,1:T(2,128)S(1)}, s32[4,2]{0,1:T(2,128)}, u32[]{:S(2)}) copy-start(s32[4,2]{0,1:T(2,128)} %constant.28.clone) | copy-start | bytes 100
  6.5 110.4 %all-gather.2.cloned.1.call-start = ((), (), s32[]{:S(2)}) async-start(), calls=%async_computation.3 | async-start | bytes 4456448 | tf_op jit(solution)/shard_map/all_gather | solution.py:218
  6.5 15.8 %collective-permute-start = (bf16[64,512]{1,0:T(8,128)(2,1)}, bf16[64,512]{1,0:T(8,128)(2,1)S(1)}, u32[]{:S(2)}, u32[]{:S(2)}) collective-permute-start(bf16[64,512]{1,0:T(8,128)(2,1)} %bitcast.18), channel_id=1, source_target_pairs={{0,256},{1,320},{2,192},{3,384},{4,0},{5,64},{6,128},{7,448},{32,2... | collective-permute-start | bytes 196616 | tf_op jit(solution)/shard_map/ppermute | solution.py:209
  15.4 1.0 copy-start
  16.5 1.0 copy-start.2
  17.5 60.7 %copy-start.1 = (bf16[512,512]{1,0:T(8,128)(2,1)S(1)}, bf16[512,512]{1,0:T(8,128)(2,1)}, u32[]{:S(2)}) copy-start(bf16[512,512]{1,0:T(8,128)(2,1)} %k_hbm.3) | copy-start | bytes 1572868
  17.5 60.7 %copy-start.3 = (bf16[512,512]{1,0:T(8,128)(2,1)S(1)}, bf16[512,512]{1,0:T(8,128)(2,1)}, u32[]{:S(2)}) copy-start(bf16[512,512]{1,0:T(8,128)(2,1)} %v_hbm.3) | copy-start | bytes 1572868
  17.5 60.7 %copy-start.4 = (bf16[512,512]{1,0:T(8,128)(2,1)S(1)}, bf16[512,512]{1,0:T(8,128)(2,1)}, u32[]{:S(2)}) copy-start(bf16[512,512]{1,0:T(8,128)(2,1)} %q_hbm.1) | copy-start | bytes 1572868
  17.5 60.7 %copy-start.5 = (f32[512]{0:T(512)S(1)}, f32[512]{0:T(512)}, u32[]{:S(2)}) copy-start(f32[512]{0:T(512)} %param.9) | copy-start | bytes 6148
  48.8 11.0 %collective-permute-start.1 = (f32[32,128]{1,0:T(8,128)S(1)}, f32[32,128]{1,0:T(8,128)S(1)}, u32[]{:S(2)}, u32[]{:S(2)}) collective-permute-start(f32[32,128]{1,0:T(8,128)S(1)} %shard_map.65), channel_id=1, source_target_pairs={{0,128},{1,129},{2,130},{3,131},{4,132},{5,133},{6,134},{7,135},{8... | collective-permute-start | bytes 49160 | tf_op jit(solution)/shard_map/ppermute | solution.py:225
  59.7 0.7 collective-permute-start.2
  60.4 0.7 collective-permute-start.3
  80.2 17.5 %collective-permute-start.6 = (bf16[512,512]{1,0:T(8,128)(2,1)S(1)}, bf16[512,512]{1,0:T(8,128)(2,1)S(1)}, u32[]{:S(2)}, u32[]{:S(2)}) collective-permute-start(bf16[512,512]{1,0:T(8,128)(2,1)S(1)} %shard_map.67.refs_0_), channel_id=1, source_target_pairs={{0,4},{2,6},{4,0},{6,2},{1,5},{3,7},{5,1},{7,3},{8,12},{10,14},{12... | collective-permute-start | bytes 1572872 | tf_op jit(solution)/shard_map/ppermute | solution.py:186
  82.1 21.0 %collective-permute-start.5 = (bf16[512,512]{1,0:T(8,128)(2,1)S(1)}, bf16[512,512]{1,0:T(8,128)(2,1)S(1)}, u32[]{:S(2)}, u32[]{:S(2)}) collective-permute-start(bf16[512,512]{1,0:T(8,128)(2,1)S(1)} %shard_map.67.refs_0_), channel_id=1, source_target_pairs={{0,6},{2,0},{4,2},{6,4},{1,7},{3,1},{5,3},{7,5},{8,14},{10,8},{12,... | collective-permute-start | bytes 1572872 | tf_op jit(solution)/shard_map/ppermute | solution.py:186
  84.0 21.0 %collective-permute-start.4 = (bf16[512,512]{1,0:T(8,128)(2,1)S(1)}, bf16[512,512]{1,0:T(8,128)(2,1)S(1)}, u32[]{:S(2)}, u32[]{:S(2)}) collective-permute-start(bf16[512,512]{1,0:T(8,128)(2,1)S(1)} %shard_map.67.refs_0_), channel_id=1, source_target_pairs={{0,2},{2,4},{4,6},{6,0},{1,3},{3,5},{5,7},{7,1},{8,10},{10,12},{12... | collective-permute-start | bytes 1572872 | tf_op jit(solution)/shard_map/ppermute | solution.py:186
  89.2 18.5 %collective-permute-start.7 = (bf16[512,512]{1,0:T(8,128)(2,1)S(1)}, bf16[512,512]{1,0:T(8,128)(2,1)S(1)}, u32[]{:S(2)}, u32[]{:S(2)}) collective-permute-start(bf16[512,512]{1,0:T(8,128)(2,1)S(1)} %shard_map.67.refs_0_), channel_id=1, source_target_pairs={{0,1},{1,0},{2,3},{3,2},{4,5},{5,4},{6,7},{7,6},{8,9},{9,8},{10,11... | collective-permute-start | bytes 1572872 | tf_op jit(solution)/shard_map/ppermute | solution.py:186
  97.6 10.0 %collective-permute-start.10 = (bf16[512,512]{1,0:T(8,128)(2,1)S(1)}, bf16[512,512]{1,0:T(8,128)(2,1)S(1)}, u32[]{:S(2)}, u32[]{:S(2)}) collective-permute-start(bf16[512,512]{1,0:T(8,128)(2,1)S(1)} %collective-permute-done.6.refs_3_), channel_id=1, source_target_pairs={{0,1},{1,0},{2,3},{3,2},{4,5},{5,4},{6,7},{7,6},{8,9},{9,8},{10,11... | collective-permute-start | bytes 1572872 | tf_op jit(solution)/shard_map/ppermute | solution.py:186
  103.1 4.5 %collective-permute-start.9 = (bf16[512,512]{1,0:T(8,128)(2,1)S(1)}, bf16[512,512]{1,0:T(8,128)(2,1)}, u32[]{:S(2)}, u32[]{:S(2)}) collective-permute-start(bf16[512,512]{1,0:T(8,128)(2,1)S(1)} %collective-permute-done.5.refs_2_), channel_id=1, source_target_pairs={{0,1},{1,0},{2,3},{3,2},{4,5},{5,4},{6,7},{7,6},{8,9},{9,8},{10,11... | collective-permute-start | bytes 1572872 | tf_op jit(solution)/shard_map/ppermute | solution.py:186
  105.1 4.1 %collective-permute-start.8 = (bf16[512,512]{1,0:T(8,128)(2,1)S(1)}, bf16[512,512]{1,0:T(8,128)(2,1)}, u32[]{:S(2)}, u32[]{:S(2)}) collective-permute-start(bf16[512,512]{1,0:T(8,128)(2,1)S(1)} %collective-permute-done.4.refs_1_), channel_id=1, source_target_pairs={{0,1},{1,0},{2,3},{3,2},{4,5},{5,4},{6,7},{7,6},{8,9},{9,8},{10,11... | collective-permute-start | bytes 1572872 | tf_op jit(solution)/shard_map/ppermute | solution.py:186
  107.6 9.3 %copy-start.6 = (bf16[512,512]{1,0:T(8,128)(2,1)}, bf16[512,512]{1,0:T(8,128)(2,1)S(1)}, u32[]{:S(2)}) copy-start(bf16[512,512]{1,0:T(8,128)(2,1)S(1)} %collective-permute-done.10.refs_7_) | copy-start | bytes 1572868
Sparse Core Ops, SparseCore 0:
  33.4 83.5 all-gather.1

commit v6 on v5

--- a/solution.py
+++ b/solution.py
@@ -11,7 +11,7 @@
 TILE = 256
 PARTS = 2
 AHEAD = 8
-GROUP = ("zl", "x")
+GROUP = ("x", "zl")
 NT = (((1,), (1,)), ((), ()))
 TN = (((0,), (0,)), ((), ()))
 
@@ -85,7 +85,8 @@
     for ref in earlier_refs[1:]:
         total = total + ref[...]
     for b in range(s_ref.shape[0] // rows):
-        at = slice(b * rows, (b + 1) * rows)
+        place = b % 4 * 4 + b // 4
+        at = slice(place * rows, (place + 1) * rows)
         p_ref[at, :] = total
         total = total + s_ref[at, :]
 
@@ -196,7 +197,7 @@
     return lax.all_to_all(copies, axis, 0, 0, tiled=True).reshape(-1, *array.shape[1:])
 
 
-TURN = ((4, -3), (3, -2), (0, 1), (2, -1))
+TURN = ((4, -3), (3, -2), (0, -1), (2, 1))
 
 
 def to_columns(shard):

time: 130 us -> 130 us (level)
  starting transfers between devices: 36.8 us -> 35 us
  waiting for transfers between devices: 25.2 us -> 26.8 us
    all_gather x1, waiting for transfers between devices: 7.8 us -> 10.1 us  [shards(): weight = lax.all_gather(near, ('zh', 'zl'), axis=0, tiled=True)]
    ppermute x3, starting transfers between devices: 10.8 us -> 9 us  [shards(): earlier.append(lax.ppermute(passed, 'zh', [(group, group + 1)]))]
    all_to_all x1, blocking collectives: 17.1 us -> 15.6 us  [shards(): states = lax.all_to_all(prefix(pieces, earlier), GROUP, 0, 0, tiled=True)]
where the time goes in v6:
time: 130 us; the launch traced here: 129 us
  blocking collectives  43 us (33%)
  starting transfers between devices  35 us (27%)
  waiting for transfers between devices  26.8 us (21%)
  between operations  13.6 us (10%)
  Pallas kernels  8 us (6%)
  local copies, waits for them, and re-layouts  2.2 us (2%)
    ppermute x7, starting transfers between devices, shift(): lax.ppermute(array, axis, [(i, (i + by) % size) for i in range(size)])  17.1 us
    all_to_all x1, blocking collectives, shards(): pieces = lax.all_to_all(state, GROUP, 0, 0, tiled=True)  16.6 us
    all_to_all x1, blocking collectives, shards(): states = lax.all_to_all(prefix(pieces, earlier), GROUP, 0, 0, tiled=True)  15.6 us
    ppermute x7, waiting for transfers between devices, shift(): lax.ppermute(array, axis, [(i, (i + by) % size) for i in range(size)])  11.1 us
    all_to_all x1, blocking collectives, spread(): lax.all_to_all(copies, axis, 0, 0, tiled=True).reshape(-1, *array.shape[1:])  10.9 us
    all_gather x1, waiting for transfers between devices, shards(): weight = lax.all_gather(near, ('zh', 'zl'), axis=0, tiled=True)  10.1 us
    ppermute x3, starting transfers between devices, shards(): earlier.append(lax.ppermute(passed, 'zh', [(group, group + 1)]))  9 us
    ppermute x1, starting transfers between devices, to_columns(): return lax.ppermute(shard, ('zh', 'zl', 'y', 'c'), pairs)  8.88 us
  transfers between devices with their start and end apart: 12, of which 6 were waited for; matrix products, arithmetic and copies ran while one was open for 0% of the time, Pallas kernels for 2%

profile of v6, /device:TPU:24, one launch (start us, length us, event | category | flops | bytes accessed | tf_op | source)
XLA Modules:
  0.0 128.7 jit_solution(12585290875088173099)
XLA Ops:
  6.5 8.9 %collective-permute-start = (bf16[64,512]{1,0:T(8,128)(2,1)}, bf16[64,512]{1,0:T(8,128)(2,1)S(1)}, u32[]{:S(2)}, u32[]{:S(2)}) collective-permute-start(bf16[64,512]{1,0:T(8,128)(2,1)} %bitcast.18), channel_id=1, source_target_pairs={{0,256},{1,320},{2,192},{3,384},{4,0},{5,448},{6,128},{7,64},{32,2... | collective-permute-start | bytes 196616 | tf_op jit(solution)/shard_map/ppermute | solution.py:210
  15.4 1.0 copy-done
  16.5 1.0 copy-done.2
  17.5 0.5 shard_map.64
  18.0 4.2 %collective-permute-done = bf16[64,512]{1,0:T(8,128)(2,1)S(1)} collective-permute-done((bf16[64,512]{1,0:T(8,128)(2,1)}, bf16[64,512]{1,0:T(8,128)(2,1)S(1)}, u32[]{:S(2)}, u32[]{:S(2)}) %collective-permute-start) | collective-permute-done | bytes 65568 | tf_op jit(solution)/shard_map/ppermute | solution.py:210
  22.2 10.9 %all_to_all.27 = bf16[4,64,512]{2,1,0:T(8,128)(2,1)} all-to-all(bf16[4,64,512]{2,1,0:T(8,128)(2,1)S(1)} %broadcast_in_dim.7), channel_id=1, replica_groups=mesh['zh'=4,'zl'=4,'x'=4,'y'=4,'c'=2] {'x'}, dimensions={0} | all-to-all | bytes 524288 | tf_op jit(solution)/shard_map/all_to_all | solution.py:197
  33.1 0.0 all-gather.2.cloned.1.call-update
  33.1 16.6 %all_to_all.28 = f32[16,32,128]{2,1,0:T(8,128)S(1)} all-to-all(f32[16,32,128]{2,1,0:T(8,128)S(1)} %bitcast.12), channel_id=1, replica_groups=mesh['zh'=4,'zl'=4,'x'=4,'y'=4,'c'=2] {'x','zl'}, dimensions={0} | all-to-all | bytes 524288 | tf_op jit(solution)/shard_map/all_to_all | solution.py:218
  49.7 7.7 %collective-permute-start.1 = (f32[32,128]{1,0:T(8,128)S(1)}, f32[32,128]{1,0:T(8,128)S(1)}, u32[]{:S(2)}, u32[]{:S(2)}) collective-permute-start(f32[32,128]{1,0:T(8,128)S(1)} %shard_map.65), channel_id=1, source_target_pairs={{0,128},{1,129},{2,130},{3,131},{4,132},{5,133},{6,134},{7,135},{8... | collective-permute-start | bytes 49160 | tf_op jit(solution)/shard_map/ppermute | solution.py:226
  57.4 1.4 %collective-permute-done.1.refs_0_ = f32[32,128]{1,0:T(8,128)S(1)} collective-permute-done((f32[32,128]{1,0:T(8,128)S(1)}, f32[32,128]{1,0:T(8,128)S(1)}, u32[]{:S(2)}, u32[]{:S(2)}) %collective-permute-start.1) | collective-permute-done | bytes 16416 | tf_op jit(solution)/shard_map/ppermute | solution.py:226
  58.9 0.7 collective-permute-start.2
  59.5 0.0 collective-permute-done.2.refs_1_
  59.6 0.7 collective-permute-start.3
  60.2 0.0 collective-permute-done.3.refs_2_
  60.3 15.6 %all_to_all.29 = f32[16,32,128]{2,1,0:T(8,128)S(1)} all-to-all(f32[16,32,128]{2,1,0:T(8,128)S(1)} %bitcast.13), channel_id=1, replica_groups=mesh['zh'=4,'zl'=4,'x'=4,'y'=4,'c'=2] {'x','zl'}, dimensions={0} | all-to-all | bytes 524288 | tf_op jit(solution)/shard_map/all_to_all | solution.py:227
  75.8 1.9 %shard_map.67.refs_0_ = bf16[512,512]{1,0:T(8,128)(2,1)S(1)} custom-call(bf16[512,512]{1,0:T(8,128)(2,1)S(1)} %copy-done.4, bf16[512,512]{1,0:T(8,128)(2,1)S(1)} %copy-done.1, bf16[512,512]{1,0:T(8,128)(2,1)S(1)} %copy-done.3, f32[512,128]{1,0:T(8,128)S(1)} %bitcast.14, f32[1,512]{1,0:T(1,128)S(1)} %bitcast.15), custom_call_target="tpu_custom_call" | custom-call | tf_op jit(solution)/shard_map/pallas_call | solution.py:131
  77.8 1.9 %collective-permute-start.6 = (bf16[512,512]{1,0:T(8,128)(2,1)S(1)}, bf16[512,512]{1,0:T(8,128)(2,1)S(1)}, u32[]{:S(2)}, u32[]{:S(2)}) collective-permute-start(bf16[512,512]{1,0:T(8,128)(2,1)S(1)} %shard_map.67.refs_0_), channel_id=1, source_target_pairs={{0,4},{2,6},{4,0},{6,2},{1,5},{3,7},{5,1},{7,3},{8,12},{10,14},{12... | collective-permute-start | bytes 1572872 | tf_op jit(solution)/shard_map/ppermute | solution.py:187
  79.7 1.9 %collective-permute-start.5 = (bf16[512,512]{1,0:T(8,128)(2,1)S(1)}, bf16[512,512]{1,0:T(8,128)(2,1)S(1)}, u32[]{:S(2)}, u32[]{:S(2)}) collective-permute-start(bf16[512,512]{1,0:T(8,128)(2,1)S(1)} %shard_map.67.refs_0_), channel_id=1, source_target_pairs={{0,6},{2,0},{4,2},{6,4},{1,7},{3,1},{5,3},{7,5},{8,14},{10,8},{12,... | collective-permute-start | bytes 1572872 | tf_op jit(solution)/shard_map/ppermute | solution.py:187
  81.6 5.1 %collective-permute-start.4 = (bf16[512,512]{1,0:T(8,128)(2,1)S(1)}, bf16[512,512]{1,0:T(8,128)(2,1)S(1)}, u32[]{:S(2)}, u32[]{:S(2)}) collective-permute-start(bf16[512,512]{1,0:T(8,128)(2,1)S(1)} %shard_map.67.refs_0_), channel_id=1, source_target_pairs={{0,2},{2,4},{4,6},{6,0},{1,3},{3,5},{5,7},{7,1},{8,10},{10,12},{12... | collective-permute-start | bytes 1572872 | tf_op jit(solution)/shard_map/ppermute | solution.py:187
  86.8 1.9 %collective-permute-start.7 = (bf16[512,512]{1,0:T(8,128)(2,1)S(1)}, bf16[512,512]{1,0:T(8,128)(2,1)S(1)}, u32[]{:S(2)}, u32[]{:S(2)}) collective-permute-start(bf16[512,512]{1,0:T(8,128)(2,1)S(1)} %shard_map.67.refs_0_), channel_id=1, source_target_pairs={{0,1},{1,0},{2,3},{3,2},{4,5},{5,4},{6,7},{7,6},{8,9},{9,8},{10,11... | collective-permute-start | bytes 1572872 | tf_op jit(solution)/shard_map/ppermute | solution.py:187
  88.7 6.0 %collective-permute-done.6.refs_3_ = bf16[512,512]{1,0:T(8,128)(2,1)S(1)} collective-permute-done((bf16[512,512]{1,0:T(8,128)(2,1)S(1)}, bf16[512,512]{1,0:T(8,128)(2,1)S(1)}, u32[]{:S(2)}, u32[]{:S(2)}) %collective-permute-start.6) | collective-permute-done | bytes 524320 | tf_op jit(solution)/shard_map/ppermute | solution.py:187
  94.8 1.9 %collective-permute-start.10 = (bf16[512,512]{1,0:T(8,128)(2,1)S(1)}, bf16[512,512]{1,0:T(8,128)(2,1)S(1)}, u32[]{:S(2)}, u32[]{:S(2)}) collective-permute-start(bf16[512,512]{1,0:T(8,128)(2,1)S(1)} %collective-permute-done.6.refs_3_), channel_id=1, source_target_pairs={{0,1},{1,0},{2,3},{3,2},{4,5},{5,4},{6,7},{7,6},{8,9},{9,8},{10,11... | collective-permute-start | bytes 1572872 | tf_op jit(solution)/shard_map/ppermute | solution.py:187
  96.7 3.6 %collective-permute-done.5.refs_2_ = bf16[512,512]{1,0:T(8,128)(2,1)S(1)} collective-permute-done((bf16[512,512]{1,0:T(8,128)(2,1)S(1)}, bf16[512,512]{1,0:T(8,128)(2,1)S(1)}, u32[]{:S(2)}, u32[]{:S(2)}) %collective-permute-start.5) | collective-permute-done | bytes 524320 | tf_op jit(solution)/shard_map/ppermute | solution.py:187
  100.2 1.9 %collective-permute-start.9 = (bf16[512,512]{1,0:T(8,128)(2,1)S(1)}, bf16[512,512]{1,0:T(8,128)(2,1)}, u32[]{:S(2)}, u32[]{:S(2)}) collective-permute-start(bf16[512,512]{1,0:T(8,128)(2,1)S(1)} %collective-permute-done.5.refs_2_), channel_id=1, source_target_pairs={{0,1},{1,0},{2,3},{3,2},{4,5},{5,4},{6,7},{7,6},{8,9},{9,8},{10,11... | collective-permute-start | bytes 1572872 | tf_op jit(solution)/shard_map/ppermute | solution.py:187
  102.1 0.0 collective-permute-done.4.refs_1_
  102.2 2.4 %collective-permute-start.8 = (bf16[512,512]{1,0:T(8,128)(2,1)S(1)}, bf16[512,512]{1,0:T(8,128)(2,1)}, u32[]{:S(2)}, u32[]{:S(2)}) collective-permute-start(bf16[512,512]{1,0:T(8,128)(2,1)S(1)} %collective-permute-done.4.refs_1_), channel_id=1, source_target_pairs={{0,1},{1,0},{2,3},{3,2},{4,5},{5,4},{6,7},{7,6},{8,9},{9,8},{10,11... | collective-permute-start | bytes 1572872 | tf_op jit(solution)/shard_map/ppermute | solution.py:187
  104.6 0.1 add.31
  104.7 0.0 collective-permute-done.7.refs_4_
  104.7 0.0 collective-permute-done.10.refs_7_
  104.7 1.5 %collective-permute-done.8.refs_5_ = bf16[512,512]{1,0:T(8,128)(2,1)} collective-permute-done((bf16[512,512]{1,0:T(8,128)(2,1)S(1)}, bf16[512,512]{1,0:T(8,128)(2,1)}, u32[]{:S(2)}, u32[]{:S(2)}) %collective-permute-start.8) | collective-permute-done | bytes 524320 | tf_op jit(solution)/shard_map/ppermute | solution.py:187
  106.2 10.1 %all-gather.2.cloned.1.call-done = bf16[4096,512]{1,0:T(8,128)(2,1)} async-done(((bf16[256,512]{1,0:T(8,128)(2,1)}), bf16[4096,512]{1,0:T(8,128)(2,1)}) %all-gather.2.cloned.1.call-update) | async-done | bytes 4194320 | tf_op jit(solution)/shard_map/all_gather | solution.py:219
  116.3 5.6 %shard_map.68 = bf16[512,512]{1,0:T(8,128)(2,1)} custom-call(s32[8]{0:T(128)S(1)} %and_select_fusion.order_ref, bf16[512,512]{1,0:T(8,128)(2,1)S(1)} %shard_map.67.refs_0_, bf16[512,512]{1,0:T(8,128)(2,1)S(1)} %collective-permute-done.4.refs_1_, bf16[512,512]{1,0:T(8,128)(2,1)S(1)} %collective-permute-done.5.refs_2_, ...), custom_call_target="tpu_custom_call" | custom-call | tf_op jit(solution)/shard_map/pallas_call | solution.py:171
  (25 shorter events, 0.1 us)
Async XLA Ops:
  6.5 98.0 %copy-start.7 = (s32[4,2]{0,1:T(2,128)S(1)}, s32[4,2]{0,1:T(2,128)}, u32[]{:S(2)}) copy-start(s32[4,2]{0,1:T(2,128)} %constant.29) | copy-start | bytes 100
  6.5 98.0 %copy-start.8 = (s32[4,2]{0,1:T(2,128)S(1)}, s32[4,2]{0,1:T(2,128)}, u32[]{:S(2)}) copy-start(s32[4,2]{0,1:T(2,128)} %constant.28.clone) | copy-start | bytes 100
  6.5 109.7 %all-gather.2.cloned.1.call-start = ((), (), s32[]{:S(2)}) async-start(), calls=%async_computation.3 | async-start | bytes 4456448 | tf_op jit(solution)/shard_map/all_gather | solution.py:219
  6.5 15.7 %collective-permute-start = (bf16[64,512]{1,0:T(8,128)(2,1)}, bf16[64,512]{1,0:T(8,128)(2,1)S(1)}, u32[]{:S(2)}, u32[]{:S(2)}) collective-permute-start(bf16[64,512]{1,0:T(8,128)(2,1)} %bitcast.18), channel_id=1, source_target_pairs={{0,256},{1,320},{2,192},{3,384},{4,0},{5,448},{6,128},{7,64},{32,2... | collective-permute-start | bytes 196616 | tf_op jit(solution)/shard_map/ppermute | solution.py:210
  15.4 1.0 copy-start
  16.5 1.0 copy-start.2
  17.5 58.3 %copy-start.1 = (bf16[512,512]{1,0:T(8,128)(2,1)S(1)}, bf16[512,512]{1,0:T(8,128)(2,1)}, u32[]{:S(2)}) copy-start(bf16[512,512]{1,0:T(8,128)(2,1)} %k_hbm.3) | copy-start | bytes 1572868
  17.5 58.3 %copy-start.3 = (bf16[512,512]{1,0:T(8,128)(2,1)S(1)}, bf16[512,512]{1,0:T(8,128)(2,1)}, u32[]{:S(2)}) copy-start(bf16[512,512]{1,0:T(8,128)(2,1)} %v_hbm.3) | copy-start | bytes 1572868
  17.5 58.3 %copy-start.4 = (bf16[512,512]{1,0:T(8,128)(2,1)S(1)}, bf16[512,512]{1,0:T(8,128)(2,1)}, u32[]{:S(2)}) copy-start(bf16[512,512]{1,0:T(8,128)(2,1)} %q_hbm.1) | copy-start | bytes 1572868
  17.5 58.3 %copy-start.5 = (f32[512]{0:T(512)S(1)}, f32[512]{0:T(512)}, u32[]{:S(2)}) copy-start(f32[512]{0:T(512)} %param.9) | copy-start | bytes 6148
  49.7 9.1 %collective-permute-start.1 = (f32[32,128]{1,0:T(8,128)S(1)}, f32[32,128]{1,0:T(8,128)S(1)}, u32[]{:S(2)}, u32[]{:S(2)}) collective-permute-start(f32[32,128]{1,0:T(8,128)S(1)} %shard_map.65), channel_id=1, source_target_pairs={{0,128},{1,129},{2,130},{3,131},{4,132},{5,133},{6,134},{7,135},{8... | collective-permute-start | bytes 49160 | tf_op jit(solution)/shard_map/ppermute | solution.py:226
  58.9 0.7 collective-permute-start.2
  59.6 0.7 collective-permute-start.3
  77.8 17.0 %collective-permute-start.6 = (bf16[512,512]{1,0:T(8,128)(2,1)S(1)}, bf16[512,512]{1,0:T(8,128)(2,1)S(1)}, u32[]{:S(2)}, u32[]{:S(2)}) collective-permute-start(bf16[512,512]{1,0:T(8,128)(2,1)S(1)} %shard_map.67.refs_0_), channel_id=1, source_target_pairs={{0,4},{2,6},{4,0},{6,2},{1,5},{3,7},{5,1},{7,3},{8,12},{10,14},{12... | collective-permute-start | bytes 1572872 | tf_op jit(solution)/shard_map/ppermute | solution.py:187
  79.7 20.5 %collective-permute-start.5 = (bf16[512,512]{1,0:T(8,128)(2,1)S(1)}, bf16[512,512]{1,0:T(8,128)(2,1)S(1)}, u32[]{:S(2)}, u32[]{:S(2)}) collective-permute-start(bf16[512,512]{1,0:T(8,128)(2,1)S(1)} %shard_map.67.refs_0_), channel_id=1, source_target_pairs={{0,6},{2,0},{4,2},{6,4},{1,7},{3,1},{5,3},{7,5},{8,14},{10,8},{12,... | collective-permute-start | bytes 1572872 | tf_op jit(solution)/shard_map/ppermute | solution.py:187
  81.6 20.5 %collective-permute-start.4 = (bf16[512,512]{1,0:T(8,128)(2,1)S(1)}, bf16[512,512]{1,0:T(8,128)(2,1)S(1)}, u32[]{:S(2)}, u32[]{:S(2)}) collective-permute-start(bf16[512,512]{1,0:T(8,128)(2,1)S(1)} %shard_map.67.refs_0_), channel_id=1, source_target_pairs={{0,2},{2,4},{4,6},{6,0},{1,3},{3,5},{5,7},{7,1},{8,10},{10,12},{12... | collective-permute-start | bytes 1572872 | tf_op jit(solution)/shard_map/ppermute | solution.py:187
  86.8 17.9 %collective-permute-start.7 = (bf16[512,512]{1,0:T(8,128)(2,1)S(1)}, bf16[512,512]{1,0:T(8,128)(2,1)S(1)}, u32[]{:S(2)}, u32[]{:S(2)}) collective-permute-start(bf16[512,512]{1,0:T(8,128)(2,1)S(1)} %shard_map.67.refs_0_), channel_id=1, source_target_pairs={{0,1},{1,0},{2,3},{3,2},{4,5},{5,4},{6,7},{7,6},{8,9},{9,8},{10,11... | collective-permute-start | bytes 1572872 | tf_op jit(solution)/shard_map/ppermute | solution.py:187
  94.8 10.0 %collective-permute-start.10 = (bf16[512,512]{1,0:T(8,128)(2,1)S(1)}, bf16[512,512]{1,0:T(8,128)(2,1)S(1)}, u32[]{:S(2)}, u32[]{:S(2)}) collective-permute-start(bf16[512,512]{1,0:T(8,128)(2,1)S(1)} %collective-permute-done.6.refs_3_), channel_id=1, source_target_pairs={{0,1},{1,0},{2,3},{3,2},{4,5},{5,4},{6,7},{7,6},{8,9},{9,8},{10,11... | collective-permute-start | bytes 1572872 | tf_op jit(solution)/shard_map/ppermute | solution.py:187
  100.2 4.5 %collective-permute-start.9 = (bf16[512,512]{1,0:T(8,128)(2,1)S(1)}, bf16[512,512]{1,0:T(8,128)(2,1)}, u32[]{:S(2)}, u32[]{:S(2)}) collective-permute-start(bf16[512,512]{1,0:T(8,128)(2,1)S(1)} %collective-permute-done.5.refs_2_), channel_id=1, source_target_pairs={{0,1},{1,0},{2,3},{3,2},{4,5},{5,4},{6,7},{7,6},{8,9},{9,8},{10,11... | collective-permute-start | bytes 1572872 | tf_op jit(solution)/shard_map/ppermute | solution.py:187
  102.2 4.1 %collective-permute-start.8 = (bf16[512,512]{1,0:T(8,128)(2,1)S(1)}, bf16[512,512]{1,0:T(8,128)(2,1)}, u32[]{:S(2)}, u32[]{:S(2)}) collective-permute-start(bf16[512,512]{1,0:T(8,128)(2,1)S(1)} %collective-permute-done.4.refs_1_), channel_id=1, source_target_pairs={{0,1},{1,0},{2,3},{3,2},{4,5},{5,4},{6,7},{7,6},{8,9},{9,8},{10,11... | collective-permute-start | bytes 1572872 | tf_op jit(solution)/shard_map/ppermute | solution.py:187
  104.7 11.6 %copy-start.6 = (bf16[512,512]{1,0:T(8,128)(2,1)}, bf16[512,512]{1,0:T(8,128)(2,1)S(1)}, u32[]{:S(2)}) copy-start(bf16[512,512]{1,0:T(8,128)(2,1)S(1)} %collective-permute-done.10.refs_7_) | copy-start | bytes 1572868
Sparse Core Ops, SparseCore 0:
  33.3 82.9 all-gather.1

commit v7 on v6

--- a/solution.py
+++ b/solution.py
@@ -10,7 +10,7 @@
 HEAD = 128
 TILE = 256
 PARTS = 2
-AHEAD = 8
+NEAR = 5
 GROUP = ("x", "zl")
 NT = (((1,), (1,)), ((), ()))
 TN = (((0,), (0,)), ((), ()))
@@ -139,30 +139,34 @@
 
 
 def project_kernel(order_ref, *refs):
-    *hidden_hbm, w_hbm, o_ref, h_ref, w_ref, sems = refs
-    groups = len(hidden_hbm)
-
-    def copies(at):
-        return (
-            pltpu.make_async_copy(w_hbm.at[order_ref[at]], w_ref.at[at], sems.at[0, at]),
-            pltpu.make_async_copy(hidden_hbm[at], h_ref.at[at], sems.at[1, at]),
-        )
-
-    def start(at):
-        for copy in copies(at):
-            copy.start()
-
-    for at in range(AHEAD):
-        start(at)
+    *hidden_refs, w_hbm, o_hbm, h_ref, w_ref, o_ref, sems, out_sems = refs
+    groups = len(hidden_refs)
+    columns = o_ref.shape[1] // 2
+    copies = [pltpu.make_async_copy(w_hbm.at[order_ref[at]], w_ref.at[at], sems.at[at]) for at in range(groups)]
+    for at in range(NEAR, groups):
+        copies.append(pltpu.make_async_copy(hidden_refs[at], h_ref.at[at - NEAR], sems.at[groups + at - NEAR]))
+    for copy in copies:
+        copy.start()
     total = None
     for at in range(groups):
-        for copy in copies(at):
+        copies[at].wait()
+        if at >= NEAR:
+            copies[groups + at - NEAR].wait()
+        part = hidden_refs[at][...] if at < NEAR else h_ref[at - NEAR]
+        if at < groups - 1:
+            product = lax.dot_general(part, w_ref[at], NT, preferred_element_type=jnp.float32)
+            total = product if total is None else total + product
+            continue
+        outs = []
+        for half in range(2):
+            own = slice(half * columns, (half + 1) * columns)
+            product = lax.dot_general(part, w_ref[at, own], NT, preferred_element_type=jnp.float32)
+            o_ref[:, own] = (total[:, own] + product).astype(o_ref.dtype)
+            place = pl.ds(half * columns, columns)
+            outs.append(pltpu.make_async_copy(o_ref.at[:, place], o_hbm.at[:, place], out_sems.at[half]))
+            outs[-1].start()
+        for copy in outs:
             copy.wait()
-        if at + AHEAD < groups:
-            start(at + AHEAD)
-        product = lax.dot_general(h_ref[at], w_ref[at], NT, preferred_element_type=jnp.float32)
-        total = product if total is None else total + product
-    o_ref[...] = total.astype(o_ref.dtype)
 
 
 def project(order, hidden, weight):
@@ -171,12 +175,17 @@
     return pl.pallas_call(
         project_kernel,
         out_shape=jax.ShapeDtypeStruct((rows, weight.shape[1]), jnp.bfloat16),
-        in_specs=[pl.BlockSpec(memory_space=pltpu.SMEM)] + [pl.BlockSpec(memory_space=pl.ANY)] * groups + [in_hbm()],
-        out_specs=in_vmem(),
+        in_specs=[pl.BlockSpec(memory_space=pltpu.SMEM)]
+        + [in_vmem()] * NEAR
+        + [pl.BlockSpec(memory_space=pl.ANY)] * (groups - NEAR)
+        + [in_hbm()],
+        out_specs=in_hbm(),
         scratch_shapes=[
-            pltpu.VMEM((groups, *hidden[0].shape), hidden[0].dtype),
+            pltpu.VMEM((groups - NEAR, *hidden[0].shape), hidden[0].dtype),
             pltpu.VMEM(weight.shape, weight.dtype),
-            pltpu.SemaphoreType.DMA((2, groups)),
+            pltpu.VMEM((rows, weight.shape[1]), jnp.bfloat16),
+            pltpu.SemaphoreType.DMA((2 * groups - NEAR,)),
+            pltpu.SemaphoreType.DMA((2,)),
         ],
         compiler_params=params(51),
     )(order, *hidden, weight)
@@ -214,7 +223,7 @@
     blocks = lax.axis_size("zl") * lax.axis_size("x")
     tp = lax.axis_size("y") * lax.axis_size("c")
     shard, state = lax.optimization_barrier((to_columns(out_weight.T), block_state(keys, values)))
-    near = spread(shard, "x")
+    near, state = lax.optimization_barrier((spread(shard, "x"), state))
     pieces = lax.all_to_all(state, GROUP, 0, 0, tiled=True)
     weight = lax.all_gather(near, ("zh", "zl"), axis=0, tiled=True)
     weight = weight.reshape(tp, -1, out_weight.shape[0])

time: 130 us -> 130 us (level)
  no operation moved by 1% of the time
where the time goes in v7:
time: 130 us; the launch traced here: 129 us
  blocking collectives  43 us (33%)
  starting transfers between devices  35 us (27%)
  waiting for transfers between devices  26.8 us (21%)
  between operations  13.6 us (10%)
  Pallas kernels  7.95 us (6%)
  local copies, waits for them, and re-layouts  2.2 us (2%)
    ppermute x7, starting transfers between devices, shift(): lax.ppermute(array, axis, [(i, (i + by) % size) for i in range(size)])  17.1 us
    all_to_all x1, blocking collectives, shards(): pieces = lax.all_to_all(state, GROUP, 0, 0, tiled=True)  16.6 us
    all_to_all x1, blocking collectives, shards(): states = lax.all_to_all(prefix(pieces, earlier), GROUP, 0, 0, tiled=True)  15.6 us
    ppermute x7, waiting for transfers between devices, shift(): lax.ppermute(array, axis, [(i, (i + by) % size) for i in range(size)])  11.1 us
    all_to_all x1, blocking collectives, spread(): lax.all_to_all(copies, axis, 0, 0, tiled=True).reshape(-1, *array.shape[1:])  10.9 us
    all_gather x1, waiting for transfers between devices, shards(): weight = lax.all_gather(near, ('zh', 'zl'), axis=0, tiled=True)  10.1 us
    ppermute x3, starting transfers between devices, shards(): earlier.append(lax.ppermute(passed, 'zh', [(group, group + 1)]))  9 us
    ppermute x1, starting transfers between devices, to_columns(): return lax.ppermute(shard, ('zh', 'zl', 'y', 'c'), pairs)  8.88 us
  transfers between devices with their start and end apart: 12, of which 6 were waited for; matrix products, arithmetic and copies ran while one was open for 0% of the time, Pallas kernels for 2%

profile of v7, /device:TPU:24, one launch (start us, length us, event | category | flops | bytes accessed | tf_op | source)
XLA Modules:
  0.0 128.6 jit_solution(6879770411851581815)
XLA Ops:
  6.5 8.9 %collective-permute-start = (bf16[64,512]{1,0:T(8,128)(2,1)}, bf16[64,512]{1,0:T(8,128)(2,1)S(1)}, u32[]{:S(2)}, u32[]{:S(2)}) collective-permute-start(bf16[64,512]{1,0:T(8,128)(2,1)} %bitcast.18), channel_id=1, source_target_pairs={{0,256},{1,320},{2,192},{3,384},{4,0},{5,448},{6,128},{7,64},{32,2... | collective-permute-start | bytes 196616 | tf_op jit(solution)/shard_map/ppermute | solution.py:219
  15.4 1.0 copy-done
  16.5 1.0 copy-done.2
  17.5 0.5 shard_map.64
  18.0 4.2 %collective-permute-done = bf16[64,512]{1,0:T(8,128)(2,1)S(1)} collective-permute-done((bf16[64,512]{1,0:T(8,128)(2,1)}, bf16[64,512]{1,0:T(8,128)(2,1)S(1)}, u32[]{:S(2)}, u32[]{:S(2)}) %collective-permute-start) | collective-permute-done | bytes 65568 | tf_op jit(solution)/shard_map/ppermute | solution.py:219
  22.2 10.9 %all_to_all.27 = bf16[4,64,512]{2,1,0:T(8,128)(2,1)} all-to-all(bf16[4,64,512]{2,1,0:T(8,128)(2,1)S(1)} %broadcast_in_dim.6), channel_id=1, replica_groups=mesh['zh'=4,'zl'=4,'x'=4,'y'=4,'c'=2] {'x'}, dimensions={0} | all-to-all | bytes 524288 | tf_op jit(solution)/shard_map/all_to_all | solution.py:206
  33.1 0.0 all-gather.2.cloned.1.call-update
  33.1 16.6 %all_to_all.28 = f32[16,32,128]{2,1,0:T(8,128)S(1)} all-to-all(f32[16,32,128]{2,1,0:T(8,128)S(1)} %bitcast.12), channel_id=1, replica_groups=mesh['zh'=4,'zl'=4,'x'=4,'y'=4,'c'=2] {'x','zl'}, dimensions={0} | all-to-all | bytes 524288 | tf_op jit(solution)/shard_map/all_to_all | solution.py:227
  49.7 7.7 %collective-permute-start.1 = (f32[32,128]{1,0:T(8,128)S(1)}, f32[32,128]{1,0:T(8,128)S(1)}, u32[]{:S(2)}, u32[]{:S(2)}) collective-permute-start(f32[32,128]{1,0:T(8,128)S(1)} %shard_map.65), channel_id=1, source_target_pairs={{0,128},{1,129},{2,130},{3,131},{4,132},{5,133},{6,134},{7,135},{8... | collective-permute-start | bytes 49160 | tf_op jit(solution)/shard_map/ppermute | solution.py:235
  57.4 1.4 %collective-permute-done.1.refs_0_ = f32[32,128]{1,0:T(8,128)S(1)} collective-permute-done((f32[32,128]{1,0:T(8,128)S(1)}, f32[32,128]{1,0:T(8,128)S(1)}, u32[]{:S(2)}, u32[]{:S(2)}) %collective-permute-start.1) | collective-permute-done | bytes 16416 | tf_op jit(solution)/shard_map/ppermute | solution.py:235
  58.9 0.7 collective-permute-start.2
  59.5 0.0 collective-permute-done.2.refs_1_
  59.6 0.7 collective-permute-start.3
  60.2 0.0 collective-permute-done.3.refs_2_
  60.3 15.6 %all_to_all.29 = f32[16,32,128]{2,1,0:T(8,128)S(1)} all-to-all(f32[16,32,128]{2,1,0:T(8,128)S(1)} %bitcast.13), channel_id=1, replica_groups=mesh['zh'=4,'zl'=4,'x'=4,'y'=4,'c'=2] {'x','zl'}, dimensions={0} | all-to-all | bytes 524288 | tf_op jit(solution)/shard_map/all_to_all | solution.py:236
  75.8 1.9 %shard_map.67.refs_0_ = bf16[512,512]{1,0:T(8,128)(2,1)S(1)} custom-call(bf16[512,512]{1,0:T(8,128)(2,1)S(1)} %copy-done.4, bf16[512,512]{1,0:T(8,128)(2,1)S(1)} %copy-done.1, bf16[512,512]{1,0:T(8,128)(2,1)S(1)} %copy-done.3, f32[512,128]{1,0:T(8,128)S(1)} %bitcast.14, f32[1,512]{1,0:T(1,128)S(1)} %bitcast.15), custom_call_target="tpu_custom_call" | custom-call | tf_op jit(solution)/shard_map/pallas_call | solution.py:131
  77.8 1.9 %collective-permute-start.6 = (bf16[512,512]{1,0:T(8,128)(2,1)S(1)}, bf16[512,512]{1,0:T(8,128)(2,1)S(1)}, u32[]{:S(2)}, u32[]{:S(2)}) collective-permute-start(bf16[512,512]{1,0:T(8,128)(2,1)S(1)} %shard_map.67.refs_0_), channel_id=1, source_target_pairs={{0,4},{2,6},{4,0},{6,2},{1,5},{3,7},{5,1},{7,3},{8,12},{10,14},{12... | collective-permute-start | bytes 1572872 | tf_op jit(solution)/shard_map/ppermute | solution.py:196
  79.7 1.9 %collective-permute-start.5 = (bf16[512,512]{1,0:T(8,128)(2,1)S(1)}, bf16[512,512]{1,0:T(8,128)(2,1)S(1)}, u32[]{:S(2)}, u32[]{:S(2)}) collective-permute-start(bf16[512,512]{1,0:T(8,128)(2,1)S(1)} %shard_map.67.refs_0_), channel_id=1, source_target_pairs={{0,6},{2,0},{4,2},{6,4},{1,7},{3,1},{5,3},{7,5},{8,14},{10,8},{12,... | collective-permute-start | bytes 1572872 | tf_op jit(solution)/shard_map/ppermute | solution.py:196
  81.6 5.1 %collective-permute-start.4 = (bf16[512,512]{1,0:T(8,128)(2,1)S(1)}, bf16[512,512]{1,0:T(8,128)(2,1)S(1)}, u32[]{:S(2)}, u32[]{:S(2)}) collective-permute-start(bf16[512,512]{1,0:T(8,128)(2,1)S(1)} %shard_map.67.refs_0_), channel_id=1, source_target_pairs={{0,2},{2,4},{4,6},{6,0},{1,3},{3,5},{5,7},{7,1},{8,10},{10,12},{12... | collective-permute-start | bytes 1572872 | tf_op jit(solution)/shard_map/ppermute | solution.py:196
  86.8 1.9 %collective-permute-start.7 = (bf16[512,512]{1,0:T(8,128)(2,1)S(1)}, bf16[512,512]{1,0:T(8,128)(2,1)S(1)}, u32[]{:S(2)}, u32[]{:S(2)}) collective-permute-start(bf16[512,512]{1,0:T(8,128)(2,1)S(1)} %shard_map.67.refs_0_), channel_id=1, source_target_pairs={{0,1},{1,0},{2,3},{3,2},{4,5},{5,4},{6,7},{7,6},{8,9},{9,8},{10,11... | collective-permute-start | bytes 1572872 | tf_op jit(solution)/shard_map/ppermute | solution.py:196
  88.7 6.0 %collective-permute-done.6.refs_3_ = bf16[512,512]{1,0:T(8,128)(2,1)S(1)} collective-permute-done((bf16[512,512]{1,0:T(8,128)(2,1)S(1)}, bf16[512,512]{1,0:T(8,128)(2,1)S(1)}, u32[]{:S(2)}, u32[]{:S(2)}) %collective-permute-start.6) | collective-permute-done | bytes 524320 | tf_op jit(solution)/shard_map/ppermute | solution.py:196
  94.8 1.9 %collective-permute-start.10 = (bf16[512,512]{1,0:T(8,128)(2,1)S(1)}, bf16[512,512]{1,0:T(8,128)(2,1)S(1)}, u32[]{:S(2)}, u32[]{:S(2)}) collective-permute-start(bf16[512,512]{1,0:T(8,128)(2,1)S(1)} %collective-permute-done.6.refs_3_), channel_id=1, source_target_pairs={{0,1},{1,0},{2,3},{3,2},{4,5},{5,4},{6,7},{7,6},{8,9},{9,8},{10,11... | collective-permute-start | bytes 1572872 | tf_op jit(solution)/shard_map/ppermute | solution.py:196
  96.7 3.6 %collective-permute-done.5.refs_2_ = bf16[512,512]{1,0:T(8,128)(2,1)S(1)} collective-permute-done((bf16[512,512]{1,0:T(8,128)(2,1)S(1)}, bf16[512,512]{1,0:T(8,128)(2,1)S(1)}, u32[]{:S(2)}, u32[]{:S(2)}) %collective-permute-start.5) | collective-permute-done | bytes 524320 | tf_op jit(solution)/shard_map/ppermute | solution.py:196
  100.2 1.9 %collective-permute-start.9 = (bf16[512,512]{1,0:T(8,128)(2,1)S(1)}, bf16[512,512]{1,0:T(8,128)(2,1)}, u32[]{:S(2)}, u32[]{:S(2)}) collective-permute-start(bf16[512,512]{1,0:T(8,128)(2,1)S(1)} %collective-permute-done.5.refs_2_), channel_id=1, source_target_pairs={{0,1},{1,0},{2,3},{3,2},{4,5},{5,4},{6,7},{7,6},{8,9},{9,8},{10,11... | collective-permute-start | bytes 1572872 | tf_op jit(solution)/shard_map/ppermute | solution.py:196
  102.1 0.0 collective-permute-done.4.refs_1_
  102.2 2.4 %collective-permute-start.8 = (bf16[512,512]{1,0:T(8,128)(2,1)S(1)}, bf16[512,512]{1,0:T(8,128)(2,1)}, u32[]{:S(2)}, u32[]{:S(2)}) collective-permute-start(bf16[512,512]{1,0:T(8,128)(2,1)S(1)} %collective-permute-done.4.refs_1_), channel_id=1, source_target_pairs={{0,1},{1,0},{2,3},{3,2},{4,5},{5,4},{6,7},{7,6},{8,9},{9,8},{10,11... | collective-permute-start | bytes 1572872 | tf_op jit(solution)/shard_map/ppermute | solution.py:196
  104.6 0.1 add.31
  104.7 0.0 collective-permute-done.7.refs_4_
  104.7 0.0 collective-permute-done.10.refs_7_
  104.7 1.5 %collective-permute-done.8.refs_5_ = bf16[512,512]{1,0:T(8,128)(2,1)} collective-permute-done((bf16[512,512]{1,0:T(8,128)(2,1)S(1)}, bf16[512,512]{1,0:T(8,128)(2,1)}, u32[]{:S(2)}, u32[]{:S(2)}) %collective-permute-start.8) | collective-permute-done | bytes 524320 | tf_op jit(solution)/shard_map/ppermute | solution.py:196
  106.2 10.1 %all-gather.2.cloned.1.call-done = bf16[4096,512]{1,0:T(8,128)(2,1)} async-done(((bf16[256,512]{1,0:T(8,128)(2,1)}), bf16[4096,512]{1,0:T(8,128)(2,1)}) %all-gather.2.cloned.1.call-update) | async-done | bytes 4194320 | tf_op jit(solution)/shard_map/all_gather | solution.py:228
  116.3 5.5 %shard_map.68 = bf16[512,512]{1,0:T(8,128)(2,1)} custom-call(s32[8]{0:T(128)S(1)} %and_select_fusion.order_ref, bf16[512,512]{1,0:T(8,128)(2,1)S(1)} %shard_map.67.refs_0_, bf16[512,512]{1,0:T(8,128)(2,1)S(1)} %collective-permute-done.4.refs_1_, bf16[512,512]{1,0:T(8,128)(2,1)S(1)} %collective-permute-done.5.refs_2_, ...), custom_call_target="tpu_custom_call" | custom-call | tf_op jit(solution)/shard_map/pallas_call | solution.py:175
  (25 shorter events, 0.1 us)
Async XLA Ops:
  6.5 98.0 %copy-start.7 = (s32[4,2]{0,1:T(2,128)S(1)}, s32[4,2]{0,1:T(2,128)}, u32[]{:S(2)}) copy-start(s32[4,2]{0,1:T(2,128)} %constant.29) | copy-start | bytes 100
  6.5 98.0 %copy-start.8 = (s32[4,2]{0,1:T(2,128)S(1)}, s32[4,2]{0,1:T(2,128)}, u32[]{:S(2)}) copy-start(s32[4,2]{0,1:T(2,128)} %constant.28.clone) | copy-start | bytes 100
  6.5 109.7 %all-gather.2.cloned.1.call-start = ((), (), s32[]{:S(2)}) async-start(), calls=%async_computation.3 | async-start | bytes 4456448 | tf_op jit(solution)/shard_map/all_gather | solution.py:228
  6.5 15.7 %collective-permute-start = (bf16[64,512]{1,0:T(8,128)(2,1)}, bf16[64,512]{1,0:T(8,128)(2,1)S(1)}, u32[]{:S(2)}, u32[]{:S(2)}) collective-permute-start(bf16[64,512]{1,0:T(8,128)(2,1)} %bitcast.18), channel_id=1, source_target_pairs={{0,256},{1,320},{2,192},{3,384},{4,0},{5,448},{6,128},{7,64},{32,2... | collective-permute-start | bytes 196616 | tf_op jit(solution)/shard_map/ppermute | solution.py:219
  15.4 1.0 copy-start
  16.5 1.0 copy-start.2
  17.5 58.3 %copy-start.1 = (bf16[512,512]{1,0:T(8,128)(2,1)S(1)}, bf16[512,512]{1,0:T(8,128)(2,1)}, u32[]{:S(2)}) copy-start(bf16[512,512]{1,0:T(8,128)(2,1)} %k_hbm.3) | copy-start | bytes 1572868
  17.5 58.3 %copy-start.3 = (bf16[512,512]{1,0:T(8,128)(2,1)S(1)}, bf16[512,512]{1,0:T(8,128)(2,1)}, u32[]{:S(2)}) copy-start(bf16[512,512]{1,0:T(8,128)(2,1)} %v_hbm.3) | copy-start | bytes 1572868
  17.5 58.3 %copy-start.4 = (bf16[512,512]{1,0:T(8,128)(2,1)S(1)}, bf16[512,512]{1,0:T(8,128)(2,1)}, u32[]{:S(2)}) copy-start(bf16[512,512]{1,0:T(8,128)(2,1)} %q_hbm.1) | copy-start | bytes 1572868
  17.5 58.3 %copy-start.5 = (f32[512]{0:T(512)S(1)}, f32[512]{0:T(512)}, u32[]{:S(2)}) copy-start(f32[512]{0:T(512)} %param.9) | copy-start | bytes 6148
  49.7 9.1 %collective-permute-start.1 = (f32[32,128]{1,0:T(8,128)S(1)}, f32[32,128]{1,0:T(8,128)S(1)}, u32[]{:S(2)}, u32[]{:S(2)}) collective-permute-start(f32[32,128]{1,0:T(8,128)S(1)} %shard_map.65), channel_id=1, source_target_pairs={{0,128},{1,129},{2,130},{3,131},{4,132},{5,133},{6,134},{7,135},{8... | collective-permute-start | bytes 49160 | tf_op jit(solution)/shard_map/ppermute | solution.py:235
  58.9 0.7 collective-permute-start.2
  59.6 0.7 collective-permute-start.3
  77.8 17.0 %collective-permute-start.6 = (bf16[512,512]{1,0:T(8,128)(2,1)S(1)}, bf16[512,512]{1,0:T(8,128)(2,1)S(1)}, u32[]{:S(2)}, u32[]{:S(2)}) collective-permute-start(bf16[512,512]{1,0:T(8,128)(2,1)S(1)} %shard_map.67.refs_0_), channel_id=1, source_target_pairs={{0,4},{2,6},{4,0},{6,2},{1,5},{3,7},{5,1},{7,3},{8,12},{10,14},{12... | collective-permute-start | bytes 1572872 | tf_op jit(solution)/shard_map/ppermute | solution.py:196
  79.7 20.5 %collective-permute-start.5 = (bf16[512,512]{1,0:T(8,128)(2,1)S(1)}, bf16[512,512]{1,0:T(8,128)(2,1)S(1)}, u32[]{:S(2)}, u32[]{:S(2)}) collective-permute-start(bf16[512,512]{1,0:T(8,128)(2,1)S(1)} %shard_map.67.refs_0_), channel_id=1, source_target_pairs={{0,6},{2,0},{4,2},{6,4},{1,7},{3,1},{5,3},{7,5},{8,14},{10,8},{12,... | collective-permute-start | bytes 1572872 | tf_op jit(solution)/shard_map/ppermute | solution.py:196
  81.6 20.5 %collective-permute-start.4 = (bf16[512,512]{1,0:T(8,128)(2,1)S(1)}, bf16[512,512]{1,0:T(8,128)(2,1)S(1)}, u32[]{:S(2)}, u32[]{:S(2)}) collective-permute-start(bf16[512,512]{1,0:T(8,128)(2,1)S(1)} %shard_map.67.refs_0_), channel_id=1, source_target_pairs={{0,2},{2,4},{4,6},{6,0},{1,3},{3,5},{5,7},{7,1},{8,10},{10,12},{12... | collective-permute-start | bytes 1572872 | tf_op jit(solution)/shard_map/ppermute | solution.py:196
  86.8 17.9 %collective-permute-start.7 = (bf16[512,512]{1,0:T(8,128)(2,1)S(1)}, bf16[512,512]{1,0:T(8,128)(2,1)S(1)}, u32[]{:S(2)}, u32[]{:S(2)}) collective-permute-start(bf16[512,512]{1,0:T(8,128)(2,1)S(1)} %shard_map.67.refs_0_), channel_id=1, source_target_pairs={{0,1},{1,0},{2,3},{3,2},{4,5},{5,4},{6,7},{7,6},{8,9},{9,8},{10,11... | collective-permute-start | bytes 1572872 | tf_op jit(solution)/shard_map/ppermute | solution.py:196
  94.8 10.0 %collective-permute-start.10 = (bf16[512,512]{1,0:T(8,128)(2,1)S(1)}, bf16[512,512]{1,0:T(8,128)(2,1)S(1)}, u32[]{:S(2)}, u32[]{:S(2)}) collective-permute-start(bf16[512,512]{1,0:T(8,128)(2,1)S(1)} %collective-permute-done.6.refs_3_), channel_id=1, source_target_pairs={{0,1},{1,0},{2,3},{3,2},{4,5},{5,4},{6,7},{7,6},{8,9},{9,8},{10,11... | collective-permute-start | bytes 1572872 | tf_op jit(solution)/shard_map/ppermute | solution.py:196
  100.2 4.5 %collective-permute-start.9 = (bf16[512,512]{1,0:T(8,128)(2,1)S(1)}, bf16[512,512]{1,0:T(8,128)(2,1)}, u32[]{:S(2)}, u32[]{:S(2)}) collective-permute-start(bf16[512,512]{1,0:T(8,128)(2,1)S(1)} %collective-permute-done.5.refs_2_), channel_id=1, source_target_pairs={{0,1},{1,0},{2,3},{3,2},{4,5},{5,4},{6,7},{7,6},{8,9},{9,8},{10,11... | collective-permute-start | bytes 1572872 | tf_op jit(solution)/shard_map/ppermute | solution.py:196
  102.2 4.1 %collective-permute-start.8 = (bf16[512,512]{1,0:T(8,128)(2,1)S(1)}, bf16[512,512]{1,0:T(8,128)(2,1)}, u32[]{:S(2)}, u32[]{:S(2)}) collective-permute-start(bf16[512,512]{1,0:T(8,128)(2,1)S(1)} %collective-permute-done.4.refs_1_), channel_id=1, source_target_pairs={{0,1},{1,0},{2,3},{3,2},{4,5},{5,4},{6,7},{7,6},{8,9},{9,8},{10,11... | collective-permute-start | bytes 1572872 | tf_op jit(solution)/shard_map/ppermute | solution.py:196
  104.7 11.6 %copy-start.6 = (bf16[512,512]{1,0:T(8,128)(2,1)}, bf16[512,512]{1,0:T(8,128)(2,1)S(1)}, u32[]{:S(2)}) copy-start(bf16[512,512]{1,0:T(8,128)(2,1)S(1)} %collective-permute-done.10.refs_7_) | copy-start | bytes 1572868
Sparse Core Ops, SparseCore 0:
  33.3 82.9 all-gather.1

commit v8 on v7

--- a/solution.py
+++ b/solution.py
@@ -141,32 +141,30 @@
 def project_kernel(order_ref, *refs):
     *hidden_refs, w_hbm, o_hbm, h_ref, w_ref, o_ref, sems, out_sems = refs
     groups = len(hidden_refs)
-    columns = o_ref.shape[1] // 2
     copies = [pltpu.make_async_copy(w_hbm.at[order_ref[at]], w_ref.at[at], sems.at[at]) for at in range(groups)]
     for at in range(NEAR, groups):
         copies.append(pltpu.make_async_copy(hidden_refs[at], h_ref.at[at - NEAR], sems.at[groups + at - NEAR]))
     for copy in copies:
         copy.start()
-    total = None
-    for at in range(groups):
-        copies[at].wait()
-        if at >= NEAR:
-            copies[groups + at - NEAR].wait()
-        part = hidden_refs[at][...] if at < NEAR else h_ref[at - NEAR]
-        if at < groups - 1:
+    rows = o_ref.shape[0] // 2
+    outs = []
+    for half in range(2):
+        own = slice(half * rows, (half + 1) * rows)
+        total = None
+        for at in range(groups):
+            if half == 0:
+                copies[at].wait()
+                if at >= NEAR:
+                    copies[groups + at - NEAR].wait()
+            part = hidden_refs[at][own, :] if at < NEAR else h_ref[at - NEAR, own]
             product = lax.dot_general(part, w_ref[at], NT, preferred_element_type=jnp.float32)
             total = product if total is None else total + product
-            continue
-        outs = []
-        for half in range(2):
-            own = slice(half * columns, (half + 1) * columns)
-            product = lax.dot_general(part, w_ref[at, own], NT, preferred_element_type=jnp.float32)
-            o_ref[:, own] = (total[:, own] + product).astype(o_ref.dtype)
-            place = pl.ds(half * columns, columns)
-            outs.append(pltpu.make_async_copy(o_ref.at[:, place], o_hbm.at[:, place], out_sems.at[half]))
-            outs[-1].start()
-        for copy in outs:
-            copy.wait()
+        o_ref[own, :] = total.astype(o_ref.dtype)
+        place = pl.ds(half * rows, rows)
+        outs.append(pltpu.make_async_copy(o_ref.at[place], o_hbm.at[place], out_sems.at[half]))
+        outs[-1].start()
+    for copy in outs:
+        copy.wait()
 
 
 def project(order, hidden, weight):

time: 130 us -> 130 us (level)
  no operation moved by 1% of the time
where the time goes in v8:
time: 130 us; the launch traced here: 129 us
  blocking collectives  43 us (33%)
  starting transfers between devices  35 us (27%)
  waiting for transfers between devices  26.8 us (21%)
  between operations  13.6 us (10%)
  Pallas kernels  7.97 us (6%)
  local copies, waits for them, and re-layouts  2.2 us (2%)
    ppermute x7, starting transfers between devices, shift(): lax.ppermute(array, axis, [(i, (i + by) % size) for i in range(size)])  17.1 us
    all_to_all x1, blocking collectives, shards(): pieces = lax.all_to_all(state, GROUP, 0, 0, tiled=True)  16.6 us
    all_to_all x1, blocking collectives, shards(): states = lax.all_to_all(prefix(pieces, earlier), GROUP, 0, 0, tiled=True)  15.6 us
    ppermute x7, waiting for transfers between devices, shift(): lax.ppermute(array, axis, [(i, (i + by) % size) for i in range(size)])  11.1 us
    all_to_all x1, blocking collectives, spread(): lax.all_to_all(copies, axis, 0, 0, tiled=True).reshape(-1, *array.shape[1:])  10.9 us
    all_gather x1, waiting for transfers between devices, shards(): weight = lax.all_gather(near, ('zh', 'zl'), axis=0, tiled=True)  10.1 us
    ppermute x3, starting transfers between devices, shards(): earlier.append(lax.ppermute(passed, 'zh', [(group, group + 1)]))  9 us
    ppermute x1, starting transfers between devices, to_columns(): return lax.ppermute(shard, ('zh', 'zl', 'y', 'c'), pairs)  8.88 us
  transfers between devices with their start and end apart: 12, of which 6 were waited for; matrix products, arithmetic and copies ran while one was open for 0% of the time, Pallas kernels for 2%

profile of v8, /device:TPU:24, one launch (start us, length us, event | category | flops | bytes accessed | tf_op | source)
XLA Modules:
  0.0 128.7 jit_solution(15951133782986233650)
XLA Ops:
  6.5 8.9 %collective-permute-start = (bf16[64,512]{1,0:T(8,128)(2,1)}, bf16[64,512]{1,0:T(8,128)(2,1)S(1)}, u32[]{:S(2)}, u32[]{:S(2)}) collective-permute-start(bf16[64,512]{1,0:T(8,128)(2,1)} %bitcast.18), channel_id=1, source_target_pairs={{0,256},{1,320},{2,192},{3,384},{4,0},{5,448},{6,128},{7,64},{32,2... | collective-permute-start | bytes 196616 | tf_op jit(solution)/shard_map/ppermute | solution.py:217
  15.4 1.0 copy-done
  16.5 1.0 copy-done.2
  17.5 0.5 shard_map.64
  18.0 4.2 %collective-permute-done = bf16[64,512]{1,0:T(8,128)(2,1)S(1)} collective-permute-done((bf16[64,512]{1,0:T(8,128)(2,1)}, bf16[64,512]{1,0:T(8,128)(2,1)S(1)}, u32[]{:S(2)}, u32[]{:S(2)}) %collective-permute-start) | collective-permute-done | bytes 65568 | tf_op jit(solution)/shard_map/ppermute | solution.py:217
  22.2 10.9 %all_to_all.27 = bf16[4,64,512]{2,1,0:T(8,128)(2,1)} all-to-all(bf16[4,64,512]{2,1,0:T(8,128)(2,1)S(1)} %broadcast_in_dim.6), channel_id=1, replica_groups=mesh['zh'=4,'zl'=4,'x'=4,'y'=4,'c'=2] {'x'}, dimensions={0} | all-to-all | bytes 524288 | tf_op jit(solution)/shard_map/all_to_all | solution.py:204
  33.1 0.0 all-gather.2.cloned.1.call-update
  33.1 16.6 %all_to_all.28 = f32[16,32,128]{2,1,0:T(8,128)S(1)} all-to-all(f32[16,32,128]{2,1,0:T(8,128)S(1)} %bitcast.12), channel_id=1, replica_groups=mesh['zh'=4,'zl'=4,'x'=4,'y'=4,'c'=2] {'x','zl'}, dimensions={0} | all-to-all | bytes 524288 | tf_op jit(solution)/shard_map/all_to_all | solution.py:225
  49.7 7.7 %collective-permute-start.1 = (f32[32,128]{1,0:T(8,128)S(1)}, f32[32,128]{1,0:T(8,128)S(1)}, u32[]{:S(2)}, u32[]{:S(2)}) collective-permute-start(f32[32,128]{1,0:T(8,128)S(1)} %shard_map.65), channel_id=1, source_target_pairs={{0,128},{1,129},{2,130},{3,131},{4,132},{5,133},{6,134},{7,135},{8... | collective-permute-start | bytes 49160 | tf_op jit(solution)/shard_map/ppermute | solution.py:233
  57.4 1.4 %collective-permute-done.1.refs_0_ = f32[32,128]{1,0:T(8,128)S(1)} collective-permute-done((f32[32,128]{1,0:T(8,128)S(1)}, f32[32,128]{1,0:T(8,128)S(1)}, u32[]{:S(2)}, u32[]{:S(2)}) %collective-permute-start.1) | collective-permute-done | bytes 16416 | tf_op jit(solution)/shard_map/ppermute | solution.py:233
  58.9 0.7 collective-permute-start.2
  59.5 0.0 collective-permute-done.2.refs_1_
  59.6 0.7 collective-permute-start.3
  60.2 0.0 collective-permute-done.3.refs_2_
  60.3 15.6 %all_to_all.29 = f32[16,32,128]{2,1,0:T(8,128)S(1)} all-to-all(f32[16,32,128]{2,1,0:T(8,128)S(1)} %bitcast.13), channel_id=1, replica_groups=mesh['zh'=4,'zl'=4,'x'=4,'y'=4,'c'=2] {'x','zl'}, dimensions={0} | all-to-all | bytes 524288 | tf_op jit(solution)/shard_map/all_to_all | solution.py:234
  75.8 1.9 %shard_map.67.refs_0_ = bf16[512,512]{1,0:T(8,128)(2,1)S(1)} custom-call(bf16[512,512]{1,0:T(8,128)(2,1)S(1)} %copy-done.4, bf16[512,512]{1,0:T(8,128)(2,1)S(1)} %copy-done.1, bf16[512,512]{1,0:T(8,128)(2,1)S(1)} %copy-done.3, f32[512,128]{1,0:T(8,128)S(1)} %bitcast.14, f32[1,512]{1,0:T(1,128)S(1)} %bitcast.15), custom_call_target="tpu_custom_call" | custom-call | tf_op jit(solution)/shard_map/pallas_call | solution.py:131
  77.8 1.9 %collective-permute-start.6 = (bf16[512,512]{1,0:T(8,128)(2,1)S(1)}, bf16[512,512]{1,0:T(8,128)(2,1)S(1)}, u32[]{:S(2)}, u32[]{:S(2)}) collective-permute-start(bf16[512,512]{1,0:T(8,128)(2,1)S(1)} %shard_map.67.refs_0_), channel_id=1, source_target_pairs={{0,4},{2,6},{4,0},{6,2},{1,5},{3,7},{5,1},{7,3},{8,12},{10,14},{12... | collective-permute-start | bytes 1572872 | tf_op jit(solution)/shard_map/ppermute | solution.py:194
  79.7 1.9 %collective-permute-start.5 = (bf16[512,512]{1,0:T(8,128)(2,1)S(1)}, bf16[512,512]{1,0:T(8,128)(2,1)S(1)}, u32[]{:S(2)}, u32[]{:S(2)}) collective-permute-start(bf16[512,512]{1,0:T(8,128)(2,1)S(1)} %shard_map.67.refs_0_), channel_id=1, source_target_pairs={{0,6},{2,0},{4,2},{6,4},{1,7},{3,1},{5,3},{7,5},{8,14},{10,8},{12,... | collective-permute-start | bytes 1572872 | tf_op jit(solution)/shard_map/ppermute | solution.py:194
  81.6 5.1 %collective-permute-start.4 = (bf16[512,512]{1,0:T(8,128)(2,1)S(1)}, bf16[512,512]{1,0:T(8,128)(2,1)S(1)}, u32[]{:S(2)}, u32[]{:S(2)}) collective-permute-start(bf16[512,512]{1,0:T(8,128)(2,1)S(1)} %shard_map.67.refs_0_), channel_id=1, source_target_pairs={{0,2},{2,4},{4,6},{6,0},{1,3},{3,5},{5,7},{7,1},{8,10},{10,12},{12... | collective-permute-start | bytes 1572872 | tf_op jit(solution)/shard_map/ppermute | solution.py:194
  86.8 1.9 %collective-permute-start.7 = (bf16[512,512]{1,0:T(8,128)(2,1)S(1)}, bf16[512,512]{1,0:T(8,128)(2,1)S(1)}, u32[]{:S(2)}, u32[]{:S(2)}) collective-permute-start(bf16[512,512]{1,0:T(8,128)(2,1)S(1)} %shard_map.67.refs_0_), channel_id=1, source_target_pairs={{0,1},{1,0},{2,3},{3,2},{4,5},{5,4},{6,7},{7,6},{8,9},{9,8},{10,11... | collective-permute-start | bytes 1572872 | tf_op jit(solution)/shard_map/ppermute | solution.py:194
  88.7 6.0 %collective-permute-done.6.refs_3_ = bf16[512,512]{1,0:T(8,128)(2,1)S(1)} collective-permute-done((bf16[512,512]{1,0:T(8,128)(2,1)S(1)}, bf16[512,512]{1,0:T(8,128)(2,1)S(1)}, u32[]{:S(2)}, u32[]{:S(2)}) %collective-permute-start.6) | collective-permute-done | bytes 524320 | tf_op jit(solution)/shard_map/ppermute | solution.py:194
  94.8 1.9 %collective-permute-start.10 = (bf16[512,512]{1,0:T(8,128)(2,1)S(1)}, bf16[512,512]{1,0:T(8,128)(2,1)S(1)}, u32[]{:S(2)}, u32[]{:S(2)}) collective-permute-start(bf16[512,512]{1,0:T(8,128)(2,1)S(1)} %collective-permute-done.6.refs_3_), channel_id=1, source_target_pairs={{0,1},{1,0},{2,3},{3,2},{4,5},{5,4},{6,7},{7,6},{8,9},{9,8},{10,11... | collective-permute-start | bytes 1572872 | tf_op jit(solution)/shard_map/ppermute | solution.py:194
  96.7 3.6 %collective-permute-done.5.refs_2_ = bf16[512,512]{1,0:T(8,128)(2,1)S(1)} collective-permute-done((bf16[512,512]{1,0:T(8,128)(2,1)S(1)}, bf16[512,512]{1,0:T(8,128)(2,1)S(1)}, u32[]{:S(2)}, u32[]{:S(2)}) %collective-permute-start.5) | collective-permute-done | bytes 524320 | tf_op jit(solution)/shard_map/ppermute | solution.py:194
  100.2 1.9 %collective-permute-start.9 = (bf16[512,512]{1,0:T(8,128)(2,1)S(1)}, bf16[512,512]{1,0:T(8,128)(2,1)}, u32[]{:S(2)}, u32[]{:S(2)}) collective-permute-start(bf16[512,512]{1,0:T(8,128)(2,1)S(1)} %collective-permute-done.5.refs_2_), channel_id=1, source_target_pairs={{0,1},{1,0},{2,3},{3,2},{4,5},{5,4},{6,7},{7,6},{8,9},{9,8},{10,11... | collective-permute-start | bytes 1572872 | tf_op jit(solution)/shard_map/ppermute | solution.py:194
  102.1 0.0 collective-permute-done.4.refs_1_
  102.2 2.4 %collective-permute-start.8 = (bf16[512,512]{1,0:T(8,128)(2,1)S(1)}, bf16[512,512]{1,0:T(8,128)(2,1)}, u32[]{:S(2)}, u32[]{:S(2)}) collective-permute-start(bf16[512,512]{1,0:T(8,128)(2,1)S(1)} %collective-permute-done.4.refs_1_), channel_id=1, source_target_pairs={{0,1},{1,0},{2,3},{3,2},{4,5},{5,4},{6,7},{7,6},{8,9},{9,8},{10,11... | collective-permute-start | bytes 1572872 | tf_op jit(solution)/shard_map/ppermute | solution.py:194
  104.6 0.1 add.31
  104.7 0.0 collective-permute-done.7.refs_4_
  104.7 0.0 collective-permute-done.10.refs_7_
  104.7 1.5 %collective-permute-done.8.refs_5_ = bf16[512,512]{1,0:T(8,128)(2,1)} collective-permute-done((bf16[512,512]{1,0:T(8,128)(2,1)S(1)}, bf16[512,512]{1,0:T(8,128)(2,1)}, u32[]{:S(2)}, u32[]{:S(2)}) %collective-permute-start.8) | collective-permute-done | bytes 524320 | tf_op jit(solution)/shard_map/ppermute | solution.py:194
  106.2 10.1 %all-gather.2.cloned.1.call-done = bf16[4096,512]{1,0:T(8,128)(2,1)} async-done(((bf16[256,512]{1,0:T(8,128)(2,1)}), bf16[4096,512]{1,0:T(8,128)(2,1)}) %all-gather.2.cloned.1.call-update) | async-done | bytes 4194320 | tf_op jit(solution)/shard_map/all_gather | solution.py:226
  116.3 5.5 %shard_map.68 = bf16[512,512]{1,0:T(8,128)(2,1)} custom-call(s32[8]{0:T(128)S(1)} %and_select_fusion.order_ref, bf16[512,512]{1,0:T(8,128)(2,1)S(1)} %shard_map.67.refs_0_, bf16[512,512]{1,0:T(8,128)(2,1)S(1)} %collective-permute-done.4.refs_1_, bf16[512,512]{1,0:T(8,128)(2,1)S(1)} %collective-permute-done.5.refs_2_, ...), custom_call_target="tpu_custom_call" | custom-call | tf_op jit(solution)/shard_map/pallas_call | solution.py:173
  (25 shorter events, 0.1 us)
Async XLA Ops:
  6.5 98.0 %copy-start.7 = (s32[4,2]{0,1:T(2,128)S(1)}, s32[4,2]{0,1:T(2,128)}, u32[]{:S(2)}) copy-start(s32[4,2]{0,1:T(2,128)} %constant.29) | copy-start | bytes 100
  6.5 98.0 %copy-start.8 = (s32[4,2]{0,1:T(2,128)S(1)}, s32[4,2]{0,1:T(2,128)}, u32[]{:S(2)}) copy-start(s32[4,2]{0,1:T(2,128)} %constant.28.clone) | copy-start | bytes 100
  6.5 109.7 %all-gather.2.cloned.1.call-start = ((), (), s32[]{:S(2)}) async-start(), calls=%async_computation.3 | async-start | bytes 4456448 | tf_op jit(solution)/shard_map/all_gather | solution.py:226
  6.5 15.7 %collective-permute-start = (bf16[64,512]{1,0:T(8,128)(2,1)}, bf16[64,512]{1,0:T(8,128)(2,1)S(1)}, u32[]{:S(2)}, u32[]{:S(2)}) collective-permute-start(bf16[64,512]{1,0:T(8,128)(2,1)} %bitcast.18), channel_id=1, source_target_pairs={{0,256},{1,320},{2,192},{3,384},{4,0},{5,448},{6,128},{7,64},{32,2... | collective-permute-start | bytes 196616 | tf_op jit(solution)/shard_map/ppermute | solution.py:217
  15.4 1.0 copy-start
  16.5 1.0 copy-start.2
  17.5 58.3 %copy-start.1 = (bf16[512,512]{1,0:T(8,128)(2,1)S(1)}, bf16[512,512]{1,0:T(8,128)(2,1)}, u32[]{:S(2)}) copy-start(bf16[512,512]{1,0:T(8,128)(2,1)} %k_hbm.3) | copy-start | bytes 1572868
  17.5 58.3 %copy-start.3 = (bf16[512,512]{1,0:T(8,128)(2,1)S(1)}, bf16[512,512]{1,0:T(8,128)(2,1)}, u32[]{:S(2)}) copy-start(bf16[512,512]{1,0:T(8,128)(2,1)} %v_hbm.3) | copy-start | bytes 1572868
  17.5 58.3 %copy-start.4 = (bf16[512,512]{1,0:T(8,128)(2,1)S(1)}, bf16[512,512]{1,0:T(8,128)(2,1)}, u32[]{:S(2)}) copy-start(bf16[512,512]{1,0:T(8,128)(2,1)} %q_hbm.1) | copy-start | bytes 1572868
  17.5 58.3 %copy-start.5 = (f32[512]{0:T(512)S(1)}, f32[512]{0:T(512)}, u32[]{:S(2)}) copy-start(f32[512]{0:T(512)} %param.9) | copy-start | bytes 6148
  49.7 9.1 %collective-permute-start.1 = (f32[32,128]{1,0:T(8,128)S(1)}, f32[32,128]{1,0:T(8,128)S(1)}, u32[]{:S(2)}, u32[]{:S(2)}) collective-permute-start(f32[32,128]{1,0:T(8,128)S(1)} %shard_map.65), channel_id=1, source_target_pairs={{0,128},{1,129},{2,130},{3,131},{4,132},{5,133},{6,134},{7,135},{8... | collective-permute-start | bytes 49160 | tf_op jit(solution)/shard_map/ppermute | solution.py:233
  58.9 0.7 collective-permute-start.2
  59.6 0.7 collective-permute-start.3
  77.8 17.0 %collective-permute-start.6 = (bf16[512,512]{1,0:T(8,128)(2,1)S(1)}, bf16[512,512]{1,0:T(8,128)(2,1)S(1)}, u32[]{:S(2)}, u32[]{:S(2)}) collective-permute-start(bf16[512,512]{1,0:T(8,128)(2,1)S(1)} %shard_map.67.refs_0_), channel_id=1, source_target_pairs={{0,4},{2,6},{4,0},{6,2},{1,5},{3,7},{5,1},{7,3},{8,12},{10,14},{12... | collective-permute-start | bytes 1572872 | tf_op jit(solution)/shard_map/ppermute | solution.py:194
  79.7 20.5 %collective-permute-start.5 = (bf16[512,512]{1,0:T(8,128)(2,1)S(1)}, bf16[512,512]{1,0:T(8,128)(2,1)S(1)}, u32[]{:S(2)}, u32[]{:S(2)}) collective-permute-start(bf16[512,512]{1,0:T(8,128)(2,1)S(1)} %shard_map.67.refs_0_), channel_id=1, source_target_pairs={{0,6},{2,0},{4,2},{6,4},{1,7},{3,1},{5,3},{7,5},{8,14},{10,8},{12,... | collective-permute-start | bytes 1572872 | tf_op jit(solution)/shard_map/ppermute | solution.py:194
  81.6 20.5 %collective-permute-start.4 = (bf16[512,512]{1,0:T(8,128)(2,1)S(1)}, bf16[512,512]{1,0:T(8,128)(2,1)S(1)}, u32[]{:S(2)}, u32[]{:S(2)}) collective-permute-start(bf16[512,512]{1,0:T(8,128)(2,1)S(1)} %shard_map.67.refs_0_), channel_id=1, source_target_pairs={{0,2},{2,4},{4,6},{6,0},{1,3},{3,5},{5,7},{7,1},{8,10},{10,12},{12... | collective-permute-start | bytes 1572872 | tf_op jit(solution)/shard_map/ppermute | solution.py:194
  86.8 17.9 %collective-permute-start.7 = (bf16[512,512]{1,0:T(8,128)(2,1)S(1)}, bf16[512,512]{1,0:T(8,128)(2,1)S(1)}, u32[]{:S(2)}, u32[]{:S(2)}) collective-permute-start(bf16[512,512]{1,0:T(8,128)(2,1)S(1)} %shard_map.67.refs_0_), channel_id=1, source_target_pairs={{0,1},{1,0},{2,3},{3,2},{4,5},{5,4},{6,7},{7,6},{8,9},{9,8},{10,11... | collective-permute-start | bytes 1572872 | tf_op jit(solution)/shard_map/ppermute | solution.py:194
  94.8 10.0 %collective-permute-start.10 = (bf16[512,512]{1,0:T(8,128)(2,1)S(1)}, bf16[512,512]{1,0:T(8,128)(2,1)S(1)}, u32[]{:S(2)}, u32[]{:S(2)}) collective-permute-start(bf16[512,512]{1,0:T(8,128)(2,1)S(1)} %collective-permute-done.6.refs_3_), channel_id=1, source_target_pairs={{0,1},{1,0},{2,3},{3,2},{4,5},{5,4},{6,7},{7,6},{8,9},{9,8},{10,11... | collective-permute-start | bytes 1572872 | tf_op jit(solution)/shard_map/ppermute | solution.py:194
  100.2 4.5 %collective-permute-start.9 = (bf16[512,512]{1,0:T(8,128)(2,1)S(1)}, bf16[512,512]{1,0:T(8,128)(2,1)}, u32[]{:S(2)}, u32[]{:S(2)}) collective-permute-start(bf16[512,512]{1,0:T(8,128)(2,1)S(1)} %collective-permute-done.5.refs_2_), channel_id=1, source_target_pairs={{0,1},{1,0},{2,3},{3,2},{4,5},{5,4},{6,7},{7,6},{8,9},{9,8},{10,11... | collective-permute-start | bytes 1572872 | tf_op jit(solution)/shard_map/ppermute | solution.py:194
  102.2 4.1 %collective-permute-start.8 = (bf16[512,512]{1,0:T(8,128)(2,1)S(1)}, bf16[512,512]{1,0:T(8,128)(2,1)}, u32[]{:S(2)}, u32[]{:S(2)}) collective-permute-start(bf16[512,512]{1,0:T(8,128)(2,1)S(1)} %collective-permute-done.4.refs_1_), channel_id=1, source_target_pairs={{0,1},{1,0},{2,3},{3,2},{4,5},{5,4},{6,7},{7,6},{8,9},{9,8},{10,11... | collective-permute-start | bytes 1572872 | tf_op jit(solution)/shard_map/ppermute | solution.py:194
  104.7 11.6 %copy-start.6 = (bf16[512,512]{1,0:T(8,128)(2,1)}, bf16[512,512]{1,0:T(8,128)(2,1)S(1)}, u32[]{:S(2)}) copy-start(bf16[512,512]{1,0:T(8,128)(2,1)S(1)} %collective-permute-done.10.refs_7_) | copy-start | bytes 1572868
Sparse Core Ops, SparseCore 0:
  33.3 82.9 all-gather.1
